TPU v7x, 128 devices: a whole 4x4x4 slice. The times are simulated.
128 devices in a mesh: pw: 16 (over z, x_lo, core), band: 8 (over y, x_hi).
Axes of the slice: x: 4 (x_hi: 2, x_lo: 2; x = x_hi * 2 + x_lo), y: 4, z: 4, core: 2. Of those that a mesh axis runs over, the one named last changes fastest.
Arguments:
- slab: bfloat16 [1024, 2, 196608], P('band', None, 'pw'), may hold values from -0.013671875 to 0.013671875
- panel: float32 [32, 2, 196608], P('band', None, 'pw'), may hold values from -6 to 6
- potential: float32 [128, 128, 128], P('pw'), may hold values from -2 to 2
- pw_slot: int32 [196608], P('pw'), may hold values from 0 to 32767, as said below
- columns: int32 [4096], P('pw'), may hold values from 0 to 16383, as said below
Outputs:
- ritz_blocks: float32 [1024, 128], P('band', 'pw')
Inputs may be any that keep to these rules, and one draw needn't show every extreme that they name: Entry d * 256 + s is the grid column i1 * 128 + i2 of column slot s of index d of pw; all entries are distinct, and together they are the columns nearest the grid's third axis. `pw_slot`: the rows held by index d of pw are distinct values c * 128 + i3: the plane wave at third index i3 of column slot c of index d; within each device they are the cells of its columns nearest the grid's anchor.
All inputs are finite; a program needn't handle non-finite values.
Results may differ from a plain program's by a relative error of at most 0.0029.
Values may be sent and summed in bfloat16 or wider, within the bound.
No kernel may reach another device: no remote copies, remote signals or barrier semaphores. Data moves between devices by JAX's collectives and lax.ppermute only.
A program may use at most 128 MiB of HBM per device.

v0:
```python
import functools
import math

import jax
import jax.numpy as jnp
import ml_dtypes
import numpy as np
from jax import lax
from jax.experimental import pallas as pl
from jax.experimental.pallas import tpu as pltpu
from jax.sharding import PartitionSpec as P

F32 = jnp.float32
BF16 = jnp.bfloat16
LEN = 128
HALF_THREE = 48
THIRDS = 2 * HALF_THREE
HALF_ONE = 40
FIRSTS = 2 * HALF_ONE
NT = (((1,), (1,)), ((), ()))


def split(table):
    high = table.astype(ml_dtypes.bfloat16)
    low = (table - high.astype(np.float64)).astype(ml_dtypes.bfloat16)
    return high, low


def rotation(outs, ins, sign):
    angles = sign * 2.0 * math.pi / LEN * ((outs[:, None] * ins[None, :]) % LEN)
    cosines = np.cos(angles) / math.sqrt(LEN)
    sines = np.sin(angles) / math.sqrt(LEN)
    return np.block([[cosines, -sines], [sines, cosines]])


@functools.lru_cache(None)
def tables(parts):
    grid = np.arange(LEN)
    thirds = np.arange(-HALF_THREE, HALF_THREE)
    row = np.arange(FIRSTS)
    firsts = 2 * (row % HALF_ONE) + row // HALF_ONE - HALF_ONE
    planes = LEN // parts
    order = np.arange(2 * LEN).reshape(2, parts, planes).transpose(1, 0, 2).ravel()
    return dict(
        three_in=split(rotation(grid, thirds, 1)[order]),
        three_out=split(rotation(thirds, grid, -1)[:, order]),
        two_in=split(rotation(grid, grid, 1).T),
        two_out=split(rotation(grid, grid, -1).T),
        one_in=split(rotation(grid, firsts, 1)),
        one_out=split(rotation(firsts, grid, -1)),
    )


def dot(a, b):
    return jnp.dot(a, b, preferred_element_type=F32)


def dot_nt(a, b):
    return lax.dot_general(a, b, NT, preferred_element_type=F32)


def halves(x):
    high = x.astype(BF16)
    return high, (x - high.astype(F32)).astype(BF16)


def one_hot(index, size):
    shape = (size, index.shape[1])
    return lax.broadcasted_iota(jnp.int32, shape, 0) == index


def third_slot(slot):
    return ((slot & (LEN - 1)) + HALF_THREE) & (LEN - 1)


def spread_kernel(slot_ref, panel_ref, high_ref, low_ref, out_ref, acc_ref):
    step = pl.program_id(0)
    cols = acc_ref.shape[1]

    @pl.when(step == 0)
    def _():
        acc_ref[...] = jnp.zeros_like(acc_ref)

    slot = slot_ref[...]
    pick = one_hot(slot >> 7, cols).astype(BF16)
    mask = one_hot(third_slot(slot), THIRDS)
    rows = []
    count = panel_ref.shape[0]
    for band in range(count):
        for part in range(2):
            high, low = halves(panel_ref[band, part : part + 1, :])
            for piece in (high, low):
                rows.append(jnp.where(mask, piece.astype(F32), 0.0).astype(BF16))
    acc_ref[...] += dot_nt(jnp.concatenate(rows, axis=0), pick)

    @pl.when(step == pl.num_programs(0) - 1)
    def _():
        owners = out_ref.shape[0]
        tall = out_ref.shape[1] // count
        for band in range(count):
            parts = [
                acc_ref[(4 * band + i) * THIRDS : (4 * band + i + 1) * THIRDS] for i in range(4)
            ]
            high = jnp.concatenate([parts[0], parts[2]], axis=0).astype(BF16)
            low = jnp.concatenate([parts[1], parts[3]], axis=0).astype(BF16)
            waves = dot(high_ref[...], high) + dot(low_ref[...], high) + dot(high_ref[...], low)
            out_ref[:, band * tall : (band + 1) * tall, :] = waves.astype(BF16).reshape(
                owners, tall, cols
            )


def spread(panel, slot, parts, cols, chunk):
    count, _, waves = panel.shape
    high, low = tables(parts)["three_in"]
    tall = 2 * LEN // parts
    whole = lambda *shape: pl.BlockSpec(shape, lambda i: (0,) * len(shape))
    return pl.pallas_call(
        spread_kernel,
        grid=(waves // chunk,),
        in_specs=[
            pl.BlockSpec((1, chunk), lambda i: (0, i)),
            pl.BlockSpec((count, 2, chunk), lambda i: (0, 0, i)),
            whole(*high.shape),
            whole(*low.shape),
        ],
        out_specs=whole(parts, count * tall, cols),
        out_shape=jax.ShapeDtypeStruct((parts, count * tall, cols), BF16),
        scratch_shapes=[pltpu.VMEM((4 * count * THIRDS, cols), F32)],
        compiler_params=pltpu.CompilerParams(vmem_limit_bytes=40 << 20),
        cost_estimate=pl.CostEstimate(
            flops=2 * 4 * count * THIRDS * cols * waves, bytes_accessed=4 << 20, transcendentals=0
        ),
        name="spread",
    )(slot, panel, jnp.asarray(high), jnp.asarray(low))


def grid_kernel(
    cols_ref, in_ref, pot_ref, ti_h, ti_l, oi_h, oi_l, oo_h, oo_l, to_h, to_l, out_ref, pick_ref, mask_ref, lhs_ref
):
    owners, tall, cols = in_ref.shape
    planes = tall // 2

    @pl.when(pl.program_id(0) == 0)
    def _():
        for owner in range(owners):
            here = slice(owner * cols, (owner + 1) * cols)
            column = cols_ref[owner : owner + 1, :]
            first = ((column >> 7) + HALF_ONE) & (LEN - 1)
            inner = (first & 1) * LEN + (column & (LEN - 1))
            pick_ref[:, here] = one_hot(inner, 2 * LEN).astype(BF16)
            mask_ref[:, here] = one_hot(first >> 1, HALF_ONE).astype(F32)

    for owner in range(owners):
        here = slice(owner * cols, (owner + 1) * cols)
        values = in_ref[owner].astype(F32)
        mask = mask_ref[:, here]
        lhs_ref[:, here] = jnp.concatenate(
            [values[row : row + 1] * mask for row in range(tall)], axis=0
        ).astype(BF16)
    field = dot_nt(lhs_ref[...], pick_ref[...]).astype(BF16)
    block = planes * HALF_ONE
    spun = []
    for low_bit in range(2):
        lanes = slice(low_bit * LEN, (low_bit + 1) * LEN)
        pair = jnp.concatenate([field[:block, lanes], field[block:, lanes]], axis=1)
        spun.append(dot(pair, ti_h[...]) + dot(pair, ti_l[...]))
    tower = jnp.concatenate(
        [
            jnp.concatenate(
                [
                    spun[low_bit][plane * HALF_ONE : (plane + 1) * HALF_ONE, part * LEN : (part + 1) * LEN]
                    for part in range(2)
                    for low_bit in range(2)
                ],
                axis=0,
            )
            for plane in range(planes)
        ],
        axis=1,
    )
    high, low = halves(tower)
    psi = dot(oi_h[...], high) + dot(oi_h[...], low) + dot(oi_l[...], high)
    pot = jnp.concatenate([pot_ref[plane] for plane in range(planes)], axis=1)
    psi = jnp.concatenate([psi[:LEN] * pot, psi[LEN:] * pot], axis=0)
    high, low = halves(psi)
    back = dot(oo_h[...], high) + dot(oo_h[...], low) + dot(oo_l[...], high)
    bent = []
    for low_bit in range(2):
        pair = jnp.concatenate(
            [
                jnp.concatenate(
                    [
                        back[
                            part * FIRSTS + low_bit * HALF_ONE : part * FIRSTS + (low_bit + 1) * HALF_ONE,
                            plane * LEN : (plane + 1) * LEN,
                        ]
                        for part in range(2)
                    ],
                    axis=1,
                )
                for plane in range(planes)
            ],
            axis=0,
        )
        high, low = halves(pair)
        bent.append(dot(high, to_h[...]) + dot(low, to_h[...]) + dot(high, to_l[...]))
    field = jnp.concatenate(
        [
            jnp.concatenate([bent[low_bit][:, part * LEN : (part + 1) * LEN] for low_bit in range(2)], axis=1)
            for part in range(2)
        ],
        axis=0,
    ).astype(BF16)
    for owner in range(owners):
        here = slice(owner * cols, (owner + 1) * cols)
        values = dot(field, pick_ref[:, here])
        mask = mask_ref[:, here]
        out_ref[owner] = jnp.concatenate(
            [
                jnp.sum(values[row * HALF_ONE : (row + 1) * HALF_ONE] * mask, axis=0, keepdims=True)
                for row in range(tall)
            ],
            axis=0,
        ).astype(BF16)


def on_grid(columns, waves, potential):
    owners, rows, cols = waves.shape
    planes = potential.shape[0]
    tall = 2 * planes
    count = rows // tall
    table = tables(owners)
    pieces = [jnp.asarray(t) for name in ("two_in", "one_in", "one_out", "two_out") for t in table[name]]
    whole = lambda *shape: pl.BlockSpec(shape, lambda i: (0,) * len(shape))
    return pl.pallas_call(
        grid_kernel,
        grid=(count,),
        in_specs=[
            whole(owners, cols),
            pl.BlockSpec((owners, tall, cols), lambda i: (0, i, 0)),
            whole(*potential.shape),
        ]
        + [whole(*piece.shape) for piece in pieces],
        out_specs=pl.BlockSpec((owners, tall, cols), lambda i: (0, i, 0)),
        out_shape=jax.ShapeDtypeStruct(waves.shape, BF16),
        scratch_shapes=[
            pltpu.VMEM((2 * LEN, owners * cols), BF16),
            pltpu.VMEM((HALF_ONE, owners * cols), F32),
            pltpu.VMEM((tall * HALF_ONE, owners * cols), BF16),
        ],
        compiler_params=pltpu.CompilerParams(vmem_limit_bytes=48 << 20),
        cost_estimate=pl.CostEstimate(
            flops=count * 2 * 2 * tall * HALF_ONE * 2 * LEN * owners * cols,
            bytes_accessed=4 << 20,
            transcendentals=0,
        ),
        name="on_grid",
    )(columns, waves, potential, *pieces)


def collect_kernel(slot_ref, cols_ref, panel_ref, in_ref, high_ref, low_ref, out_ref, held_ref):
    owners, rows, cols = in_ref.shape
    count = panel_ref.shape[0]
    tall = rows // count

    @pl.when(pl.program_id(0) == 0)
    def _():
        for band in range(count):
            waves = in_ref[:, band * tall : (band + 1) * tall, :].reshape(owners * tall, cols)
            found = dot(high_ref[...], waves) + dot(low_ref[...], waves)
            high, low = halves(found)
            held_ref[band * 2 * THIRDS : (band + 1) * 2 * THIRDS, :cols] = high
            held_ref[band * 2 * THIRDS : (band + 1) * 2 * THIRDS, cols:] = low
        column = cols_ref[...]
        first = column >> 7
        second = column & (LEN - 1)
        first = jnp.where(first < LEN // 2, first, first - LEN)
        second = jnp.where(second < LEN // 2, second, second - LEN)
        size = first * first + second * second
        line = lax.broadcasted_iota(jnp.int32, (16, cols), 0)
        size = jnp.where(line == 0, size >> 7, jnp.where(line == 1, size & (LEN - 1), 0))
        held_ref[2 * count * THIRDS :, :cols] = size.astype(F32).astype(BF16)
        held_ref[2 * count * THIRDS :, cols:] = jnp.zeros((16, cols), BF16)

    slot = slot_ref[...]
    pick = one_hot(slot >> 7, cols).astype(BF16)
    third = third_slot(slot)
    mask = one_hot(third, THIRDS).astype(F32)
    found = dot(held_ref[...], jnp.concatenate([pick, pick], axis=0))
    base = 2 * count * THIRDS
    third = (third - HALF_THREE).astype(F32)
    kinetic = (float(LEN) * found[base : base + 1] + found[base + 1 : base + 2] + third * third) * (
        2.0 / LEN**2
    )
    lines = []
    for band in range(count):
        for part in range(2):
            here = (2 * band + part) * THIRDS
            back = jnp.sum(found[here : here + THIRDS] * mask, axis=0, keepdims=True)
            lines.append(kinetic * panel_ref[band, part : part + 1, :] + back)
    out_ref[...] = jnp.concatenate(lines, axis=0).astype(BF16)


def collect(panel, slot, columns, waves, chunk):
    count, _, length = panel.shape
    owners, rows, cols = waves.shape
    high, low = tables(owners)["three_out"]
    whole = lambda *shape: pl.BlockSpec(shape, lambda i: (0,) * len(shape))
    return pl.pallas_call(
        collect_kernel,
        grid=(length // chunk,),
        in_specs=[
            pl.BlockSpec((1, chunk), lambda i: (0, i)),
            whole(1, cols),
            pl.BlockSpec((count, 2, chunk), lambda i: (0, 0, i)),
            whole(*waves.shape),
            whole(*high.shape),
            whole(*low.shape),
        ],
        out_specs=pl.BlockSpec((2 * count, chunk), lambda i: (0, i)),
        out_shape=jax.ShapeDtypeStruct((2 * count, length), BF16),
        scratch_shapes=[pltpu.VMEM((2 * count * THIRDS + 16, 2 * cols), BF16)],
        compiler_params=pltpu.CompilerParams(vmem_limit_bytes=40 << 20),
        cost_estimate=pl.CostEstimate(
            flops=2 * 4 * count * THIRDS * cols * length, bytes_accessed=4 << 20, transcendentals=0
        ),
        name="collect",
    )(slot, columns, panel, waves, jnp.asarray(high), jnp.asarray(low))


def project(piece, both):
    rows, length = piece.shape
    half = both.shape[0] // 2
    product = lax.dot_general(piece, both, NT, preferred_element_type=F32)
    product = product.reshape(rows // 2, 2, 2, half)
    real = product[:, 0, 0] + product[:, 1, 1]
    imag = product[:, 1, 0] - product[:, 0, 1]
    return jnp.concatenate([real, imag], axis=0)


def everywhere(x, axis):
    size = lax.axis_size(axis)
    copies = jnp.broadcast_to(x[None], (size,) + x.shape)
    return lax.all_to_all(copies, axis, split_axis=0, concat_axis=0, tiled=True)


def per_device(slab, panel, potential, pw_slot, columns):
    parts = lax.axis_size("pw")
    bands, _, length = slab.shape
    count = panel.shape[0]
    cols = columns.shape[0]
    slot = pw_slot.reshape(1, length)
    coeffs = lax.all_gather(panel.astype(BF16).reshape(2 * count, length), "band", axis=0, tiled=True)
    every_column = everywhere(columns, "pw")
    both = jnp.transpose(slab, (1, 0, 2)).reshape(2 * bands, length)
    waves = spread(panel, slot, parts, cols, 2048)
    waves = lax.all_to_all(waves, "pw", split_axis=0, concat_axis=0, tiled=True)
    waves = on_grid(every_column, waves, potential)
    waves = lax.all_to_all(waves, "pw", split_axis=0, concat_axis=0, tiled=True)
    applied = collect(panel, slot, columns.reshape(1, cols), waves, 2048)
    applied = everywhere(applied, "band").reshape(-1, length)
    terms = jnp.concatenate([project(applied, both), project(coeffs, both)], axis=0)
    terms = terms.reshape(parts, terms.shape[0] // parts, bands)
    terms = lax.all_to_all(terms, "pw", split_axis=0, concat_axis=0, tiled=True)
    return jnp.sum(terms, axis=0).T


def solution(mesh):
    in_specs = (P("band", None, "pw"), P("band", None, "pw"), P("pw", None, None), P("pw"), P("pw"))
    out_specs = P("band", "pw")
    return jax.shard_map(
        per_device, mesh=mesh, in_specs=in_specs, out_specs=out_specs, check_vma=False
    )
```

profile of v0, /device:TPU:1, one launch (start us, length us, event | category | flops | bytes accessed | tf_op | source)
XLA Modules:
  0.0 184.1 jit_solution(15782381694650000633)
XLA Ops:
  6.5 1.3 broadcast_in_dim.4
  7.8 7.8 %all-to-all-start = ((s32[16,1,256]{2,1,0:T(1,128)}), s32[16,1,256]{2,1,0:T(1,128)S(1)}, u32[]{:S(2)}, u32[]{:S(2)}) async-start(s32[16,1,256]{2,1,0:T(1,128)} %broadcast_in_dim.4), calls=%async_computation | async-start | bytes 32768 | tf_op jit(solution)/shard_map/all_to_all | solution.py:344
  15.6 1.0 copy-done
  16.6 0.8 copy-done.4
  17.4 0.9 copy-done.12
  18.3 0.9 copy-done.13
  19.3 12.7 %spread.1 = bf16[16,64,256]{2,1,0:T(8,128)(2,1)} custom-call(s32[1,12288]{1,0:T(1,128)S(1)} %bitcast.27, f32[4,2,12288]{2,1,0:T(2,128)S(1)} %copy-done, bf16[256,192]{1,0:T(8,128)(2,1)S(1)} %copy-done.12, bf16[256,192]{1,0:T(8,128)(2,1)S(1)} %copy-done.13), custom_call_target="tpu_custom_call" | custom-call | flops 9663676416 | bytes 4194304 | tf_op jit(solution)/shard_map/spread/pallas_call | solution.py:117
  32.0 5.7 %all-to-all-start.1 = ((bf16[16,64,256]{2,1,0:T(8,128)(2,1)}), bf16[16,64,256]{2,1,0:T(8,128)(2,1)S(1)}, u32[]{:S(2)}, u32[]{:S(2)}) async-start(bf16[16,64,256]{2,1,0:T(8,128)(2,1)} %spread.1), calls=%async_computation.1 | async-start | bytes 1048576 | tf_op jit(solution)/shard_map/all_to_all | solution.py:357
  37.7 9.8 %all-to-all-done.1.in_ref = bf16[16,64,256]{2,1,0:T(8,128)(2,1)S(1)} async-done(((bf16[16,64,256]{2,1,0:T(8,128)(2,1)}), bf16[16,64,256]{2,1,0:T(8,128)(2,1)S(1)}, u32[]{:S(2)}, u32[]{:S(2)}) %all-to-all-start.1) | async-done | bytes 524320 | tf_op jit(solution)/shard_map/all_to_all | solution.py:357
  47.6 29.1 %on_grid.1 = bf16[16,64,256]{2,1,0:T(8,128)(2,1)} custom-call(s32[16,256]{1,0:T(8,128)S(1)} %bitcast.25, bf16[16,64,256]{2,1,0:T(8,128)(2,1)S(1)} %all-to-all-done.1.in_ref, f32[8,128,128]{2,1,0:T(8,128)S(1)} %copy-done.3, bf16[256,256]{1,0:T(8,128)(2,1)S(1)} %copy-done.6, bf16[256,256]{1,0:T(8,128)(2,1)S(1)} %copy-done.7, bf16[256,160]{1,0:T(8,128)(2,1)S(1)} %copy-done.8, ...), custom_call_target="tpu_custom_call" | custom-call | flops 10737418240 | bytes 4194304 | tf_op jit(solution)/shard_map/on_grid/pallas_call | solution.py:235
  76.7 4.7 %all-to-all-start.2 = ((bf16[16,64,256]{2,1,0:T(8,128)(2,1)}), bf16[16,64,256]{2,1,0:T(8,128)(2,1)S(1)}, u32[]{:S(2)}, u32[]{:S(2)}) async-start(bf16[16,64,256]{2,1,0:T(8,128)(2,1)} %on_grid.1), calls=%async_computation.2 | async-start | bytes 1048576 | tf_op jit(solution)/shard_map/all_to_all | solution.py:359
  81.4 0.0 all-gather.2.cloned.1.call-start
  81.4 0.1 convert_element_type.3
  81.6 0.8 reshape.36
  82.4 8.9 %all-to-all-done.2.in_ref = bf16[16,64,256]{2,1,0:T(8,128)(2,1)S(1)} async-done(((bf16[16,64,256]{2,1,0:T(8,128)(2,1)}), bf16[16,64,256]{2,1,0:T(8,128)(2,1)S(1)}, u32[]{:S(2)}, u32[]{:S(2)}) %all-to-all-start.2) | async-done | bytes 524320 | tf_op jit(solution)/shard_map/all_to_all | solution.py:359
  91.3 11.9 %collect.1 = bf16[8,12288]{1,0:T(8,128)(2,1)S(1)} custom-call(s32[1,12288]{1,0:T(1,128)S(1)} %bitcast.28, s32[1,256]{1,0:T(1,128)S(1)} %bitcast.26, f32[4,2,12288]{2,1,0:T(2,128)S(1)} %copy-done.1, bf16[16,64,256]{2,1,0:T(8,128)(2,1)S(1)} %all-to-all-done.2.in_ref, bf16[192,256]{1,0:T(8,128)(2,1)S(1)} %copy-done.14, bf16[192,256]{1,0:T(8,128)(2,1)S(1)} %copy-done.15), custom_call_target="tpu_custom_call" | custom-call | flops 9663676416 | bytes 4194304 | tf_op jit(solution)/shard_map/collect/pallas_call | solution.py:309
  103.2 0.1 broadcast_in_dim.5
  103.3 35.7 %all_to_all.28 = bf16[8,8,12288]{2,1,0:T(8,128)(2,1)S(1)} all-to-all(bf16[8,8,12288]{2,1,0:T(8,128)(2,1)S(1)} %broadcast_in_dim.5), channel_id=1, replica_groups=mesh['pw'=16,'band'=8] {'band'}, dimensions={0} | all-to-all | bytes 3145728 | tf_op jit(solution)/shard_map/all_to_all | solution.py:344
  139.0 1.0 dot_general.10
  140.0 11.0 %fusion.2 = f32[32,2,2,128]{3,0,2,1:T(8,128)S(1)} fusion(bf16[2,128,12288]{2,0,1:T(2,128)(2,1)} %bitcast.31, bf16[32,2,12288,1]{2,1,0,3:T(2,128)(2,1)S(1)} %bitcast.29), kind=kOutput, calls=%fused_computation.2 | convolution fusion | flops 402653184 | bytes 7929856 | tf_op jit(solution)/shard_map/dot_general | solution.py:334
  151.0 3.6 %dot_general.12 = bf16[32,2,12288]{2,1,0:T(2,128)(2,1)S(1)} reshape(bf16[64,12288]{1,0:T(8,128)(2,1)} %all-gather.2.cloned.1.call-done) | data formatting | bytes 3145728 | tf_op jit(solution)/shard_map/dot_general | solution.py:334
  154.7 11.0 %fusion = f32[32,2,2,128]{3,0,2,1:T(8,128)S(1)} fusion(bf16[2,128,12288]{2,0,1:T(2,128)(2,1)} %bitcast.32, bf16[32,2,12288,1]{2,1,0,3:T(2,128)(2,1)S(1)} %bitcast.30), kind=kOutput, calls=%fused_computation | convolution fusion | flops 402653184 | bytes 7929856 | tf_op jit(solution)/shard_map/dot_general | solution.py:334
  165.7 10.9 %all_to_all.29 = f32[16,8,128]{2,1,0:T(8,128)S(1)} all-to-all(f32[16,8,128]{2,1,0:T(8,128)S(1)} %maximum_bitcast_fusion), channel_id=1, replica_groups=mesh['pw'=16,'band'=8] {'pw'}, dimensions={0} | all-to-all | bytes 131072 | tf_op jit(solution)/shard_map/all_to_all | solution.py:364
  176.6 0.6 reduce_sum.9
  (38 shorter events, 0.1 us)
Async XLA Ops:
  7.8 24.2 %all-to-all-start = ((s32[16,1,256]{2,1,0:T(1,128)}), s32[16,1,256]{2,1,0:T(1,128)S(1)}, u32[]{:S(2)}, u32[]{:S(2)}) async-start(s32[16,1,256]{2,1,0:T(1,128)} %broadcast_in_dim.4), calls=%async_computation | async-start | bytes 32768 | tf_op jit(solution)/shard_map/all_to_all | solution.py:344
  15.6 1.0 copy-start
  16.6 0.8 copy-start.4
  17.4 0.9 copy-start.12
  18.3 0.9 copy-start.13
  19.2 28.3 %copy-start.3 = (f32[8,128,128]{2,1,0:T(8,128)S(1)}, f32[8,128,128]{2,1,0:T(8,128)}, u32[]{:S(2)}) copy-start(f32[8,128,128]{2,1,0:T(8,128)} %pot_ref.1) | copy-start | bytes 1572868
  19.2 28.3 %copy-start.6 = (bf16[256,256]{1,0:T(8,128)(2,1)S(1)}, bf16[256,256]{1,0:T(8,128)(2,1)}, u32[]{:S(2)}) copy-start(bf16[256,256]{1,0:T(8,128)(2,1)} %constant.28.clone.ti_h) | copy-start | bytes 393220
  19.2 28.3 %copy-start.7 = (bf16[256,256]{1,0:T(8,128)(2,1)S(1)}, bf16[256,256]{1,0:T(8,128)(2,1)}, u32[]{:S(2)}) copy-start(bf16[256,256]{1,0:T(8,128)(2,1)} %constant.29.clone.ti_l) | copy-start | bytes 393220
  19.2 28.3 %copy-start.8 = (bf16[256,160]{1,0:T(8,128)(2,1)S(1)}, bf16[256,160]{1,0:T(8,128)(2,1)}, u32[]{:S(2)}) copy-start(bf16[256,160]{1,0:T(8,128)(2,1)} %constant.30.clone.oi_h) | copy-start | bytes 245764
  19.2 28.3 %copy-start.9 = (bf16[256,160]{1,0:T(8,128)(2,1)S(1)}, bf16[256,160]{1,0:T(8,128)(2,1)}, u32[]{:S(2)}) copy-start(bf16[256,160]{1,0:T(8,128)(2,1)} %constant.31.clone.oi_l) | copy-start | bytes 245764
  19.2 28.3 %copy-start.10 = (bf16[256,256]{1,0:T(8,128)(2,1)S(1)}, bf16[256,256]{1,0:T(8,128)(2,1)}, u32[]{:S(2)}) copy-start(bf16[256,256]{1,0:T(8,128)(2,1)} %constant.34.clone.to_h) | copy-start | bytes 393220
  19.2 28.3 %copy-start.11 = (bf16[256,256]{1,0:T(8,128)(2,1)S(1)}, bf16[256,256]{1,0:T(8,128)(2,1)}, u32[]{:S(2)}) copy-start(bf16[256,256]{1,0:T(8,128)(2,1)} %constant.35.clone.to_l) | copy-start | bytes 393220
  19.2 28.3 %copy-start.16 = (bf16[160,256]{1,0:T(8,128)(2,1)S(1)}, bf16[160,256]{1,0:T(8,128)(2,1)}, u32[]{:S(2)}) copy-start(bf16[160,256]{1,0:T(8,128)(2,1)} %constant.32.clone.oo_h) | copy-start | bytes 245764
  19.2 28.3 %copy-start.17 = (bf16[160,256]{1,0:T(8,128)(2,1)S(1)}, bf16[160,256]{1,0:T(8,128)(2,1)}, u32[]{:S(2)}) copy-start(bf16[160,256]{1,0:T(8,128)(2,1)} %constant.33.clone.oo_l) | copy-start | bytes 245764
  32.0 15.5 %all-to-all-start.1 = ((bf16[16,64,256]{2,1,0:T(8,128)(2,1)}), bf16[16,64,256]{2,1,0:T(8,128)(2,1)S(1)}, u32[]{:S(2)}, u32[]{:S(2)}) async-start(bf16[16,64,256]{2,1,0:T(8,128)(2,1)} %spread.1), calls=%async_computation.1 | async-start | bytes 1048576 | tf_op jit(solution)/shard_map/all_to_all | solution.py:357
  47.6 33.9 %copy-start.1 = (f32[4,2,12288]{2,1,0:T(2,128)S(1)}, f32[4,2,12288]{2,1,0:T(2,128)}, u32[]{:S(2)}) copy-start(f32[4,2,12288]{2,1,0:T(2,128)} %panel_ref.3) | copy-start | bytes 1179652
  76.7 14.6 %copy-start.2 = (s32[256]{0:T(256)S(1)}, s32[256]{0:T(256)}, u32[]{:S(2)}) copy-start(s32[256]{0:T(256)} %param.21) | copy-start | bytes 3076
  76.7 14.6 %copy-start.5 = (s32[12288]{0:T(1024)S(1)}, s32[12288]{0:T(1024)}, u32[]{:S(2)}) copy-start(s32[12288]{0:T(1024)} %param.20) | copy-start | bytes 147460
  76.7 14.6 %copy-start.14 = (bf16[192,256]{1,0:T(8,128)(2,1)S(1)}, bf16[192,256]{1,0:T(8,128)(2,1)}, u32[]{:S(2)}) copy-start(bf16[192,256]{1,0:T(8,128)(2,1)} %constant.36.clone.high_ref) | copy-start | bytes 294916
  76.7 14.6 %copy-start.15 = (bf16[192,256]{1,0:T(8,128)(2,1)S(1)}, bf16[192,256]{1,0:T(8,128)(2,1)}, u32[]{:S(2)}) copy-start(bf16[192,256]{1,0:T(8,128)(2,1)} %constant.37.clone.low_ref) | copy-start | bytes 294916
  76.7 14.6 %all-to-all-start.2 = ((bf16[16,64,256]{2,1,0:T(8,128)(2,1)}), bf16[16,64,256]{2,1,0:T(8,128)(2,1)S(1)}, u32[]{:S(2)}, u32[]{:S(2)}) async-start(bf16[16,64,256]{2,1,0:T(8,128)(2,1)} %on_grid.1), calls=%async_computation.2 | async-start | bytes 1048576 | tf_op jit(solution)/shard_map/all_to_all | solution.py:359
  81.4 69.6 %all-gather.2.cloned.1.call-start = ((), (), s32[]{:S(2)}) async-start(), calls=%async_computation.5 | async-start | bytes 1769472 | tf_op jit(solution)/shard_map/all_gather | solution.py:353
Sparse Core Ops, SparseCore 0:
  84.5 58.9 all-gather.1
where the time goes:
time: 185 us; the launch traced here: 184 us
  Pallas kernels  53.7 us (29%)
  blocking collectives  46.6 us (25%)
  matrix products  21.9 us (12%)
  waiting for transfers between devices  18.7 us (10%)
  starting transfers between devices  18.2 us (10%)
  between operations  13.6 us (7%)
  local copies, waits for them, and re-layouts  10.5 us (6%)
    all_to_all x1, blocking collectives, everywhere(): return lax.all_to_all(copies, axis, split_axis=0, concat_axis=0, tiled=True)  35.7 us
    pallas_call x1, Pallas kernels, on_grid(): pl.pallas_call(grid_kernel, grid=(count,), in_specs=[whole(owners, cols),...  29.1 us
    dot_general x2, matrix products, project(): product = lax.dot_general(piece, both, NT, preferred_element_type=F32)  21.9 us
    all_to_all x2, waiting for transfers between devices, per_device(): waves = lax.all_to_all(waves, 'pw', split_axis=0, concat_axis=0, tiled=True)  18.7 us
    pallas_call x1, Pallas kernels, spread(): pl.pallas_call(spread_kernel, grid=(waves // chunk,), in_specs=[pl.BlockS...  12.7 us
    pallas_call x1, Pallas kernels, collect(): pl.pallas_call(collect_kernel, grid=(length // chunk,), in_specs=[pl.Bloc...  11.9 us
    all_to_all x1, blocking collectives, per_device(): terms = lax.all_to_all(terms, 'pw', split_axis=0, concat_axis=0, tiled=True)  10.9 us
    all_to_all x2, starting transfers between devices, per_device(): waves = lax.all_to_all(waves, 'pw', split_axis=0, concat_axis=0, tiled=True)  10.4 us
  transfers between devices with their start and end apart: 4, of which 2 were waited for; matrix products, arithmetic and copies ran while one was open for 7% of the time, Pallas kernels for 13%

commit v1 on v0

v1 whole, which is shorter than its diff:
```python
import functools
import math

import jax
import jax.numpy as jnp
import ml_dtypes
import numpy as np
from jax import lax
from jax.experimental import pallas as pl
from jax.experimental.pallas import tpu as pltpu
from jax.sharding import PartitionSpec as P

F32 = jnp.float32
BF16 = jnp.bfloat16
LEN = 128
HALF_THREE = 44
THIRDS = 2 * HALF_THREE
HALF_ONE = 40
FIRSTS = 2 * HALF_ONE
NT = (((1,), (1,)), ((), ()))


def split(table):
    high = table.astype(ml_dtypes.bfloat16)
    low = (table - high.astype(np.float64)).astype(ml_dtypes.bfloat16)
    return high, low


def rotation(outs, ins, sign):
    angles = sign * 2.0 * math.pi / LEN * ((outs[:, None] * ins[None, :]) % LEN)
    cosines = np.cos(angles) / math.sqrt(LEN)
    sines = np.sin(angles) / math.sqrt(LEN)
    return np.block([[cosines, -sines], [sines, cosines]])


@functools.lru_cache(None)
def tables(parts):
    grid = np.arange(LEN)
    thirds = np.arange(-HALF_THREE, HALF_THREE)
    row = np.arange(FIRSTS)
    firsts = 2 * (row % HALF_ONE) + row // HALF_ONE - HALF_ONE
    planes = LEN // parts
    order = np.arange(2 * LEN).reshape(2, parts, planes).transpose(1, 0, 2).ravel()
    beside = lambda table, axis: np.concatenate(split(table), axis=axis)
    return dict(
        three_in=beside(rotation(grid, thirds, 1)[order], 0),
        three_out=beside(rotation(thirds, grid, -1)[:, order], 0),
        two_in=beside(rotation(grid, grid, 1).T, 1),
        two_out=beside(rotation(grid, grid, -1).T, 1),
        one_in=beside(rotation(grid, firsts, 1), 0),
        one_out=beside(rotation(firsts, grid, -1), 0),
    )


def dot(a, b):
    return jnp.dot(a, b, preferred_element_type=F32)


def dot_nt(a, b):
    return lax.dot_general(a, b, NT, preferred_element_type=F32)


def halves(x):
    high = x.astype(BF16)
    return high, (x - high.astype(F32)).astype(BF16)


def fold(x, axis):
    half = x.shape[axis] // 2
    return x[:half] + x[half:] if axis == 0 else x[:, :half] + x[:, half:]


def one_hot(index, size):
    shape = (size, index.shape[1])
    return lax.broadcasted_iota(jnp.int32, shape, 0) == index


def third_slot(slot):
    return ((slot & (LEN - 1)) + HALF_THREE) & (LEN - 1)


def whole(*shape):
    return pl.BlockSpec(shape, lambda *_: (0,) * len(shape))


def spread_kernel(slot_ref, cols_ref, panel_ref, table_ref, out_ref, coef_ref, acc_ref):
    step = pl.program_id(0)
    cols = cols_ref.shape[1]
    count = panel_ref.shape[0]
    spans = [slice(at, at + LEN) for at in range(0, cols, LEN)]

    @pl.when(step == 0)
    def _():
        acc_ref[...] = jnp.zeros_like(acc_ref)

    slot = slot_ref[...]
    pick = one_hot(slot >> 7, cols).astype(BF16)
    panel = jnp.concatenate([panel_ref[:, part, :] for part in range(2)], axis=0)
    high = panel.astype(BF16)
    coef_ref[...] = high
    wide = high.astype(F32)
    values = jnp.concatenate([wide, panel - wide], axis=0).astype(BF16)
    third = jnp.broadcast_to(third_slot(slot).astype(F32), values.shape).astype(BF16)
    zero = jnp.zeros_like(values)
    rows = jnp.concatenate(
        [jnp.where(third == jnp.asarray(index, BF16), values, zero) for index in range(THIRDS)], axis=0
    )
    found = dot_nt(rows, pick)
    for at, span in enumerate(spans):
        acc_ref[at] += found[:, span]

    @pl.when(step == pl.num_programs(0) - 1)
    def _():
        owners = out_ref.shape[0]
        tall = table_ref.shape[0] // 2 // owners
        line = lambda row: jnp.concatenate(
            [acc_ref[at, pl.ds(row, THIRDS, stride=4 * count), :] for at in range(len(spans))], axis=1
        )
        for band in range(count):
            high = jnp.concatenate([line(band), line(count + band)], axis=0).astype(BF16)
            low = jnp.concatenate([line(2 * count + band), line(3 * count + band)], axis=0).astype(BF16)
            waves = fold(dot(table_ref[...], high), 0) + dot(table_ref[: owners * tall], low)
            out_ref[:, band * tall : (band + 1) * tall, :] = waves.astype(BF16).reshape(
                owners, tall, cols
            )
        column = cols_ref[...]
        place = lax.broadcasted_iota(jnp.int32, (8, cols), 0)
        names = jnp.where(place == 0, column >> 7, jnp.where(place == 1, column & (LEN - 1), 0))
        names = names.astype(F32).astype(BF16)
        for owner in range(owners):
            out_ref[owner, count * tall :, :] = names


def spread(panel, slot, columns, parts, chunk):
    count, _, waves = panel.shape
    cols = columns.shape[1]
    table = tables(parts)["three_in"]
    tall = 2 * LEN // parts
    return pl.pallas_call(
        spread_kernel,
        grid=(waves // chunk,),
        in_specs=[
            pl.BlockSpec((1, chunk), lambda i: (0, i)),
            whole(1, cols),
            pl.BlockSpec((count, 2, chunk), lambda i: (0, 0, i)),
            whole(*table.shape),
        ],
        out_specs=[
            whole(parts, count * tall + 8, cols),
            pl.BlockSpec((2 * count, chunk), lambda i: (0, i)),
        ],
        out_shape=[
            jax.ShapeDtypeStruct((parts, count * tall + 8, cols), BF16),
            jax.ShapeDtypeStruct((2 * count, waves), BF16),
        ],
        scratch_shapes=[pltpu.VMEM((cols // LEN, 4 * count * THIRDS, LEN), F32)],
        compiler_params=pltpu.CompilerParams(vmem_limit_bytes=40 << 20),
        cost_estimate=pl.CostEstimate(
            flops=2 * 4 * count * THIRDS * cols * waves, bytes_accessed=4 << 20, transcendentals=0
        ),
        name="spread",
    )(slot, columns, panel, jnp.asarray(table))


def grid_kernel(in_ref, pot_ref, ti_ref, oi_ref, oo_ref, to_ref, out_ref, pick_ref, mask_ref, lhs_ref):
    owners, rows, cols = out_ref.shape
    planes = pot_ref.shape[0]
    tall = 2 * planes
    count = rows // tall

    for owner in range(owners):
        here = slice(owner * cols, (owner + 1) * cols)
        values = in_ref[owner].astype(F32)
        first = (values[rows : rows + 1].astype(jnp.int32) + HALF_ONE) & (LEN - 1)
        inner = (first & 1) * LEN + values[rows + 1 : rows + 2].astype(jnp.int32)
        pick_ref[:, here] = one_hot(inner, 2 * LEN).astype(BF16)
        mask = one_hot(first >> 1, HALF_ONE).astype(F32)
        mask_ref[:, here] = mask
        lhs_ref[:, here] = jnp.concatenate(
            [values[row : row + 1] * mask for row in range(rows)], axis=0
        ).astype(BF16)
    field = dot_nt(lhs_ref[...], pick_ref[...]).astype(BF16)
    block = planes * HALF_ONE
    lanes = lambda bit: slice(bit * LEN, (bit + 1) * LEN)
    spun = []
    for bit in range(2):
        pair = jnp.concatenate(
            [
                jnp.concatenate(
                    [field[(2 * band + part) * block : (2 * band + part + 1) * block, lanes(bit)] for part in range(2)],
                    axis=1,
                )
                for band in range(count)
            ],
            axis=0,
        )
        spun.append(fold(dot(pair, ti_ref[...]), 1))
    tower = jnp.concatenate(
        [
            jnp.concatenate(
                [
                    spun[bit][item * HALF_ONE : (item + 1) * HALF_ONE, lanes(part)]
                    for part in range(2)
                    for bit in range(2)
                ],
                axis=0,
            )
            for item in range(count * planes)
        ],
        axis=1,
    ).astype(BF16)
    psi = fold(dot(oi_ref[...], tower), 0)
    pot = jnp.concatenate([pot_ref[plane] for plane in range(planes)] * count, axis=1)
    psi = jnp.concatenate([psi[:LEN] * pot, psi[LEN:] * pot], axis=0).astype(BF16)
    back = fold(dot(oo_ref[...], psi), 0)
    bent = []
    for bit in range(2):
        pair = jnp.concatenate(
            [
                jnp.concatenate(
                    [
                        back[
                            part * FIRSTS + bit * HALF_ONE : part * FIRSTS + (bit + 1) * HALF_ONE,
                            item * LEN : (item + 1) * LEN,
                        ]
                        for part in range(2)
                    ],
                    axis=1,
                )
                for item in range(count * planes)
            ],
            axis=0,
        ).astype(BF16)
        bent.append(fold(dot(pair, to_ref[...]), 1))
    field = jnp.concatenate(
        [
            jnp.concatenate(
                [bent[bit][band * block : (band + 1) * block, lanes(part)] for bit in range(2)], axis=1
            )
            for band in range(count)
            for part in range(2)
        ],
        axis=0,
    ).astype(BF16)
    for owner in range(owners):
        here = slice(owner * cols, (owner + 1) * cols)
        values = dot(field, pick_ref[:, here])
        mask = mask_ref[:, here]
        out_ref[owner] = jnp.concatenate(
            [
                jnp.sum(values[row * HALF_ONE : (row + 1) * HALF_ONE] * mask, axis=0, keepdims=True)
                for row in range(rows)
            ],
            axis=0,
        ).astype(BF16)


def on_grid(waves, potential):
    owners, rows, cols = waves.shape
    rows -= 8
    pieces = [jnp.asarray(tables(owners)[name]) for name in ("two_in", "one_in", "one_out", "two_out")]
    return pl.pallas_call(
        grid_kernel,
        in_specs=[whole(*waves.shape), whole(*potential.shape)] + [whole(*piece.shape) for piece in pieces],
        out_specs=whole(owners, rows, cols),
        out_shape=jax.ShapeDtypeStruct((owners, rows, cols), BF16),
        scratch_shapes=[
            pltpu.VMEM((2 * LEN, owners * cols), BF16),
            pltpu.VMEM((HALF_ONE, owners * cols), F32),
            pltpu.VMEM((rows * HALF_ONE, owners * cols), BF16),
        ],
        compiler_params=pltpu.CompilerParams(vmem_limit_bytes=56 << 20),
        cost_estimate=pl.CostEstimate(
            flops=2 * 2 * rows * HALF_ONE * 2 * LEN * owners * cols,
            bytes_accessed=4 << 20,
            transcendentals=0,
        ),
        name="on_grid",
    )(waves, potential, *pieces)


def collect_kernel(slot_ref, cols_ref, panel_ref, in_ref, table_ref, out_ref, wide_ref, held_ref):
    owners, rows, cols = in_ref.shape
    count = panel_ref.shape[0]
    tall = rows // count
    base = 2 * count * THIRDS

    @pl.when(pl.program_id(0) == 0)
    def _():
        for band in range(count):
            waves = in_ref[:, band * tall : (band + 1) * tall, :].reshape(owners * tall, cols)
            found = fold(dot(table_ref[...], waves), 0)
            for part in range(2):
                for at in range(cols // LEN):
                    wide_ref[at, pl.ds(part * count + band, THIRDS, stride=2 * count), :] = found[
                        part * THIRDS : (part + 1) * THIRDS, at * LEN : (at + 1) * LEN
                    ]
        for at in range(cols // LEN):
            high, low = halves(wide_ref[at])
            held_ref[:base, at * LEN : (at + 1) * LEN] = high
            held_ref[:base, cols + at * LEN : cols + (at + 1) * LEN] = low
        column = cols_ref[...]
        first = column >> 7
        second = column & (LEN - 1)
        first = jnp.where(first < LEN // 2, first, first - LEN)
        second = jnp.where(second < LEN // 2, second, second - LEN)
        size = first * first + second * second
        line = lax.broadcasted_iota(jnp.int32, (16, cols), 0)
        size = jnp.where(line == 0, size >> 7, jnp.where(line == 1, size & (LEN - 1), 0))
        held_ref[base:, :cols] = size.astype(F32).astype(BF16)
        held_ref[base:, cols:] = jnp.zeros((16, cols), BF16)

    slot = slot_ref[...]
    pick = one_hot(slot >> 7, cols).astype(BF16)
    third = third_slot(slot)
    found = dot(held_ref[...], jnp.concatenate([pick, pick], axis=0))
    panel = jnp.concatenate([panel_ref[:, part, :] for part in range(2)], axis=0)
    where = jnp.broadcast_to(third, panel.shape)
    zero = jnp.zeros_like(panel)
    tall = 2 * count
    back = [zero] * 4
    for index in range(THIRDS):
        back[index % 4] += jnp.where(where == index, found[index * tall : (index + 1) * tall], zero)
    third = (third - HALF_THREE).astype(F32)
    kinetic = (float(LEN) * found[base : base + 1] + found[base + 1 : base + 2] + third * third) * (
        2.0 / LEN**2
    )
    out_ref[...] = (kinetic * panel + ((back[0] + back[1]) + (back[2] + back[3]))).astype(BF16)


def collect(panel, slot, columns, waves, start, length, chunk):
    count = panel.shape[0]
    owners, rows, cols = waves.shape
    table = tables(owners)["three_out"]
    skip = start // chunk
    return pl.pallas_call(
        collect_kernel,
        grid=(length // chunk,),
        in_specs=[
            pl.BlockSpec((1, chunk), lambda i: (0, i + skip)),
            whole(1, cols),
            pl.BlockSpec((count, 2, chunk), lambda i: (0, 0, i + skip)),
            whole(*waves.shape),
            whole(*table.shape),
        ],
        out_specs=pl.BlockSpec((2 * count, chunk), lambda i: (0, i)),
        out_shape=jax.ShapeDtypeStruct((2 * count, length), BF16),
        scratch_shapes=[
            pltpu.VMEM((cols // LEN, 2 * count * THIRDS, LEN), F32),
            pltpu.VMEM((2 * count * THIRDS + 16, 2 * cols), BF16),
        ],
        compiler_params=pltpu.CompilerParams(vmem_limit_bytes=40 << 20),
        cost_estimate=pl.CostEstimate(
            flops=2 * 4 * count * THIRDS * cols * length, bytes_accessed=4 << 20, transcendentals=0
        ),
        name="collect",
    )(slot, columns, panel, waves, jnp.asarray(table))


def project_kernel(sizes, seat_ref, *refs):
    pieces, (both_ref, prev_ref, out_ref, acc_ref) = refs[: len(sizes)], refs[len(sizes) :]
    step = pl.program_id(0)

    @pl.when(step == 0)
    def _():
        acc_ref[...] = jnp.zeros_like(acc_ref)

    rows = jnp.concatenate([ref[...].reshape(-1, ref.shape[-1]) for ref in pieces], axis=0)
    acc_ref[...] += dot_nt(rows, both_ref[...])

    @pl.when(step == pl.num_programs(0) - 1)
    def _():
        half = acc_ref.shape[1] // 2
        out_ref[...] = prev_ref[...]
        blocks = []
        for piece in range(acc_ref.shape[0] // 8):
            real = acc_ref[8 * piece : 8 * piece + 4]
            imag = acc_ref[8 * piece + 4 : 8 * piece + 8]
            blocks.append((real[:, :half] + imag[:, half:], imag[:, :half] - real[:, half:]))
        for pair in range(len(blocks) // 2):
            odd = seat_ref[8] == 1
            for part in range(2):
                one, two = blocks[2 * pair][part], blocks[2 * pair + 1][part]
                tile = jnp.concatenate([jnp.where(odd, two, one), jnp.where(odd, one, two)], axis=0)
                seat = seat_ref[pair] + part * (len(blocks) // 2)
                out_ref[seat] = out_ref[seat] + tile


def project(pieces, both, prev, seats, start, chunk):
    length = pieces[0].shape[-1]
    sizes = [math.prod(piece.shape[:-1]) for piece in pieces]
    skip = start // chunk
    block = lambda piece: pl.BlockSpec(
        piece.shape[:-1] + (chunk,), lambda i, *_, n=piece.ndim: (0,) * (n - 1) + (i,)
    )
    return pl.pallas_call(
        functools.partial(project_kernel, sizes),
        grid_spec=pltpu.PrefetchScalarGridSpec(
            num_scalar_prefetch=1,
            grid=(length // chunk,),
            in_specs=[block(piece) for piece in pieces]
            + [
                pl.BlockSpec((both.shape[0], chunk), lambda i, *_: (0, i + skip)),
                whole(*prev.shape),
            ],
            out_specs=whole(*prev.shape),
            scratch_shapes=[pltpu.VMEM((sum(sizes), both.shape[0]), F32)],
        ),
        out_shape=jax.ShapeDtypeStruct(prev.shape, F32),
        compiler_params=pltpu.CompilerParams(vmem_limit_bytes=32 << 20),
        cost_estimate=pl.CostEstimate(
            flops=2 * 256 * both.shape[0] * length,
            bytes_accessed=2 * both.shape[0] * length,
            transcendentals=0,
        ),
        name="project",
    )(seats, *pieces, both, prev)


def moved(x, axis, target):
    size = lax.axis_size(axis)
    return lax.ppermute(x, axis, [(i, target(i) % size) for i in range(size)])


def share(x):
    pair = jnp.stack([x, moved(x, "band", lambda i: i ^ 1)])
    below = moved(pair, "band", lambda i: i + 2)
    above = moved(pair, "band", lambda i: i - 2)
    far = [moved(below[0], "band", lambda i: i + 2), moved(above[1], "band", lambda i: i - 2)]
    return [pair, below, above] + far


def per_device(slab, panel, potential, pw_slot, columns):
    parts = lax.axis_size("pw")
    bands, _, length = slab.shape
    cols = columns.shape[0]
    slot = pw_slot.reshape(1, length)
    columns = columns.reshape(1, cols)
    waves, coeffs = spread(panel, slot, columns, parts, 2048)
    waves = lax.all_to_all(waves, "pw", split_axis=0, concat_axis=0, tiled=True)
    coeffs = lax.all_gather(coeffs, "band", axis=0, tiled=True)
    both = lax.optimization_barrier(jnp.transpose(slab, (1, 0, 2)).reshape(2 * bands, length))
    waves = on_grid(waves, potential)
    waves = lax.all_to_all(waves, "pw", split_axis=0, concat_axis=0, tiled=True)
    me = lax.axis_index("band")
    row, odd = me // 2, me % 2
    terms = jnp.zeros((parts, bands // parts, bands), F32)
    pick = lambda *seats: jnp.stack([jnp.asarray(seat, jnp.int32) for seat in seats])
    seats = pick(8, 9, 10, 11, 0, 0, 0, 0, 0)
    terms = project([coeffs], both, terms, seats, 0, 2048)
    seats = pick(row, (row + 3) % 4, (row + 1) % 4, (row + 2) % 4, 0, 0, 0, 0, odd)
    step = length // PIECES
    for piece in range(PIECES):
        applied = collect(panel, slot, columns, waves, piece * step, step, min(2048, step))
        terms = project(share(applied), both, terms, seats, piece * step, min(2048, step))
    terms = lax.all_to_all(terms, "pw", split_axis=0, concat_axis=0, tiled=True)
    return jnp.sum(terms, axis=0).T


PIECES = 2


def solution(mesh):
    in_specs = (P("band", None, "pw"), P("band", None, "pw"), P("pw", None, None), P("pw"), P("pw"))
    out_specs = P("band", "pw")
    return jax.shard_map(
        per_device, mesh=mesh, in_specs=in_specs, out_specs=out_specs, check_vma=False
    )
```

time: 185 us -> 162 us (0.88)
  matrix products: 21.9 us -> 0 us
  blocking collectives: 46.6 us -> 30 us
  local copies, waits for them, and re-layouts: 10.5 us -> 20 us
  Pallas kernels: 53.7 us -> 59.1 us
    dot_general x2 -> x0, matrix products: 21.9 us -> none  [project(): product = lax.dot_general(piece, both, NT, preferred_element_type=F32)]
    all_to_all x2 -> x1, waiting for transfers between devices: 18.7 us -> 0.01 us  [per_device(): waves = lax.all_to_all(waves, 'pw', split_axis=0, concat_axis=0, tiled=True)]
    all_to_all x1, blocking collectives: 35.7 us -> 18.9 us  [per_device(): waves = lax.all_to_all(waves, 'pw', split_axis=0, concat_axis=0, tiled=True)]
    all_gather x1, waiting for transfers between devices: 0.02 us -> 14.8 us  [per_device(): coeffs = lax.all_gather(coeffs, 'band', axis=0, tiled=True)]
    ppermute x0 -> x10, starting transfers between devices: none -> 14.5 us  [moved(): return lax.ppermute(x, axis, [(i, target(i) % size) for i in range(size)])]
    transpose x0 -> x1, local copies, waits for them, and re-layouts: none -> 9.45 us  [per_device(): jnp.transpose(slab, (1, 0, 2)).reshape(2 * bands, length)]
    all_to_all x1 -> x0, starting transfers between devices: 7.76 us -> none  [everywhere(): return lax.all_to_all(copies, axis, split_axis=0, concat_axis=0, tiled=True)]
    unnamed x37 -> x24, local copies, waits for them, and re-layouts: 3.67 us -> 10.4 us
  transfers between devices with their start and end apart: 4 -> 12, of which waited for: 2 -> 3; matrix products, arithmetic and copies ran while one was open for 7% -> 6% of each run, Pallas kernels for 13% -> 11%
where the time goes in v1:
time: 162 us; the launch traced here: 159 us
  Pallas kernels  59.1 us (36%)
  blocking collectives  30 us (19%)
  local copies, waits for them, and re-layouts  20 us (12%)
  starting transfers between devices  18.6 us (11%)
  waiting for transfers between devices  16.9 us (10%)
  between operations  14.1 us (9%)
    pallas_call x1, Pallas kernels, on_grid(): pl.pallas_call(grid_kernel, in_specs=[whole(*waves.shape), whole(*potenti...  27.5 us
    all_to_all x1, blocking collectives, per_device(): waves = lax.all_to_all(waves, 'pw', split_axis=0, concat_axis=0, tiled=True)  18.9 us
    all_gather x1, waiting for transfers between devices, per_device(): coeffs = lax.all_gather(coeffs, 'band', axis=0, tiled=True)  14.8 us
    ppermute x10, starting transfers between devices, moved(): return lax.ppermute(x, axis, [(i, target(i) % size) for i in range(size)])  14.5 us
    pallas_call x1, Pallas kernels, spread(): pl.pallas_call(spread_kernel, grid=(waves // chunk,), in_specs=[pl.BlockS...  11.7 us
    pallas_call x2, Pallas kernels, collect(): pl.pallas_call(collect_kernel, grid=(length // chunk,), in_specs=[pl.Bloc...  11.6 us
    all_to_all x1, blocking collectives, per_device(): terms = lax.all_to_all(terms, 'pw', split_axis=0, concat_axis=0, tiled=True)  11.1 us
    unnamed x24, local copies, waits for them, and re-layouts  10.4 us
  transfers between devices with their start and end apart: 12, of which 3 were waited for; matrix products, arithmetic and copies ran while one was open for 6% of the time, Pallas kernels for 11%

profile of v1, /device:TPU:1, one launch (start us, length us, event | category | flops | bytes accessed | tf_op | source)
XLA Modules:
  0.0 159.4 jit_solution(9315593509251861978)
XLA Ops:
  6.5 1.0 copy-done.4
  10.0 11.7 %spread.1 = (bf16[16,72,256]{2,1,0:T(8,128)(2,1)S(1)}, bf16[8,12288]{1,0:T(8,128)(2,1)}) custom-call(s32[1,12288]{1,0:T(1,128)S(1)} %bitcast.27, s32[1,256]{1,0:T(1,128)S(1)} %bitcast.30, f32[4,2,12288]{2,1,0:T(2,128)S(1)} %copy-done.4, bf16[512,176]{1,0:T(8,128)(2,1)S(1)} %copy-done.10), custom_call_target="tpu_custom_call" | custom-call | flops 8858370048 | bytes 4194304 | tf_op jit(solution)/shard_map/spread/pallas_call | solution.py:139
  21.6 18.9 %all_to_all.15.in_ref = bf16[16,72,256]{2,1,0:T(8,128)(2,1)} all-to-all(bf16[16,72,256]{2,1,0:T(8,128)(2,1)S(1)} %get-tuple-element.7), channel_id=1, replica_groups=mesh['pw'=16,'band'=8] {'pw'}, dimensions={0} | all-to-all | bytes 1179648 | tf_op jit(solution)/shard_map/all_to_all | solution.py:440
  40.5 27.5 %on_grid.1 = bf16[16,64,256]{2,1,0:T(8,128)(2,1)} custom-call(bf16[16,72,256]{2,1,0:T(8,128)(2,1)} %all_to_all.15.in_ref, f32[8,128,128]{2,1,0:T(8,128)} %pot_ref.1, bf16[256,512]{1,0:T(8,128)(2,1)} %constant.67.clone.ti_ref, bf16[512,160]{1,0:T(8,128)(2,1)} %constant.68.clone.oi_ref, bf16[320,256]{1,0:T(8,128)(2,1)} %constant.69.clone.oo_ref, ...), custom_call_target="tpu_custom_call" | custom-call | flops 10737418240 | bytes 4194304 | tf_op jit(solution)/shard_map/on_grid/pallas_call | solution.py:262
  68.1 3.8 %all-to-all-start.1 = ((bf16[16,64,256]{2,1,0:T(8,128)(2,1)}), bf16[16,64,256]{2,1,0:T(8,128)(2,1)S(1)}, u32[]{:S(2)}, u32[]{:S(2)}) async-start(bf16[16,64,256]{2,1,0:T(8,128)(2,1)} %on_grid.1), calls=%async_computation.1 | async-start | bytes 1048576 | tf_op jit(solution)/shard_map/all_to_all | solution.py:444
  72.7 9.5 %copy.12 = bf16[2,128,12288]{2,1,0:T(8,128)(2,1)} copy(bf16[2,128,12288]{2,0,1:T(2,128)(2,1)} %bitcast.33) | data formatting | bytes 12582912 | tf_op jit(solution)/shard_map/transpose | solution.py:442
  82.3 5.8 %collect.3 = bf16[8,6144]{1,0:T(8,128)(2,1)S(1)} custom-call(s32[1,12288]{1,0:T(1,128)S(1)} %bitcast.28, s32[1,256]{1,0:T(1,128)S(1)} %bitcast.31, f32[4,2,12288]{2,1,0:T(2,128)S(1)} %copy-done.5, bf16[16,64,256]{2,1,0:T(8,128)(2,1)S(1)} %all-to-all-done.1.in_ref, bf16[352,256]{1,0:T(8,128)(2,1)S(1)} %copy-done.11), custom_call_target="tpu_custom_call" | custom-call | flops 4429185024 | bytes 4194304 | tf_op jit(solution)/shard_map/collect/pallas_call | solution.py:336
  88.1 2.5 %collective-permute-start.5 = (bf16[8,6144]{1,0:T(8,128)(2,1)S(1)}, bf16[8,6144]{1,0:T(8,128)(2,1)S(1)}, u32[]{:S(2)}, u32[]{:S(2)}) collective-permute-start(bf16[8,6144]{1,0:T(8,128)(2,1)S(1)} %collect.3), channel_id=1, source_target_pairs={{0,1},{1,0},{2,3},{3,2},{4,5},{5,4},{6,7},{7,6},{8,9},{9,8},{10,11... | collective-permute-start | bytes 294920 | tf_op jit(solution)/shard_map/ppermute | solution.py:422
  90.6 5.8 %collect.2 = bf16[8,6144]{1,0:T(8,128)(2,1)S(1)} custom-call(s32[1,12288]{1,0:T(1,128)S(1)} %bitcast.29, s32[1,256]{1,0:T(1,128)S(1)} %bitcast.32, f32[4,2,12288]{2,1,0:T(2,128)S(1)} %copy-done.5, bf16[16,64,256]{2,1,0:T(8,128)(2,1)S(1)} %all-to-all-done.1.in_ref, bf16[352,256]{1,0:T(8,128)(2,1)S(1)} %copy-done.11), custom_call_target="tpu_custom_call" | custom-call | flops 4429185024 | bytes 4194304 | tf_op jit(solution)/shard_map/collect/pallas_call | solution.py:336
  97.0 1.4 collective-permute-start.6
  98.4 1.5 collective-permute-start.7
  99.9 1.5 collective-permute-done
  101.5 1.4 collective-permute-start.1
  102.9 1.5 collective-permute-start.2
  104.5 2.7 %collective-permute-start.9 = (bf16[8,6144]{1,0:T(8,128)(2,1)S(1)}, bf16[8,6144]{1,0:T(8,128)(2,1)S(1)}, u32[]{:S(2)}, u32[]{:S(2)}) collective-permute-start(bf16[8,6144]{1,0:T(8,128)(2,1)S(1)} %slice_bitcast_fusion), channel_id=1, source_target_pairs={{0,6},{1,7},{2,0},{3,1},{4,2},{5,3},{6,4},{7,5},{8,14},{9,15},{10,... | collective-permute-start | bytes 294920 | tf_op jit(solution)/shard_map/ppermute | solution.py:422
  107.5 2.7 %collective-permute-start.4 = (bf16[8,6144]{1,0:T(8,128)(2,1)S(1)}, bf16[8,6144]{1,0:T(8,128)(2,1)S(1)}, u32[]{:S(2)}, u32[]{:S(2)}) collective-permute-start(bf16[8,6144]{1,0:T(8,128)(2,1)S(1)} %slice_bitcast_fusion.2), channel_id=1, source_target_pairs={{0,6},{1,7},{2,0},{3,1},{4,2},{5,3},{6,4},{7,5},{8,14},{9,15},{10,... | collective-permute-start | bytes 294920 | tf_op jit(solution)/shard_map/ppermute | solution.py:422
  110.2 14.8 %all-gather.2.cloned.1.call-done.refs_0_ = bf16[64,12288]{1,0:T(8,128)(2,1)} async-done(((bf16[8,12288]{1,0:T(8,128)(2,1)}), bf16[64,12288]{1,0:T(8,128)(2,1)}) %all-gather.2.cloned.1.call-update) | async-done | bytes 1572880 | tf_op jit(solution)/shard_map/all_gather | solution.py:441
  125.0 2.8 %copy-done = bf16[2,128,12288]{2,1,0:T(8,128)(2,1)S(1)} copy-done((bf16[2,128,12288]{2,1,0:T(8,128)(2,1)S(1)}, bf16[2,128,12288]{2,1,0:T(8,128)(2,1)}, u32[]{:S(2)}) %copy-start) | copy-done | bytes 6291480
  127.8 1.4 copy-done.2
  129.2 3.8 %project.3.refs_6_ = f32[16,8,128]{2,1,0:T(8,128)S(1)} custom-call(s32[9]{0:T(128)S(1)} %copy-done.3, bf16[64,12288]{1,0:T(8,128)(2,1)S(1)} %copy-done.2, bf16[256,12288]{1,0:T(8,128)(2,1)S(1)} %bitcast.22, f32[16,8,128]{2,1,0:T(8,128)S(1)} %broadcast_in_dim.3.refs_2_), custom_call_target="tpu_custom_call" | custom-call | flops 1610612736 | bytes 6291456 | tf_op jit(solution)/shard_map/project/pallas_call | solution.py:396
  133.1 2.8 %copy-done.1 = bf16[2,128,12288]{2,1,0:T(8,128)(2,1)S(1)} copy-done((bf16[2,128,12288]{2,1,0:T(8,128)(2,1)S(1)}, bf16[2,128,12288]{2,1,0:T(8,128)(2,1)}, u32[]{:S(2)}) %copy-start.1) | copy-done | bytes 6291480
  135.9 2.2 %project.4.refs_6_ = f32[16,8,128]{2,1,0:T(8,128)S(1)} custom-call(s32[9]{0:T(128)S(1)} %stack.41.seat_ref, bf16[2,8,6144]{2,1,0:T(8,128)(2,1)S(1)} %pad_maximum_fusion.1.refs_0_, bf16[2,8,6144]{2,1,0:T(8,128)(2,1)S(1)} %collective-permute-done.6.refs_1_, bf16[2,8,6144]{2,1,0:T(8,128)(2,1)S(1)} %collective-permute-done.7.refs_2_, ...), custom_call_target="tpu_custom_call" | custom-call | flops 805306368 | bytes 3145728 | tf_op jit(solution)/shard_map/project/pallas_call | solution.py:396
  138.1 2.2 %project.5 = f32[16,8,128]{2,1,0:T(8,128)S(1)} custom-call(s32[9]{0:T(128)S(1)} %stack.41.seat_ref, bf16[2,8,6144]{2,1,0:T(8,128)(2,1)S(1)} %pad_maximum_fusion.refs_0_, bf16[2,8,6144]{2,1,0:T(8,128)(2,1)S(1)} %collective-permute-done.1.refs_1_, bf16[2,8,6144]{2,1,0:T(8,128)(2,1)S(1)} %collective-permute-done.2.refs_2_, ...), custom_call_target="tpu_custom_call" | custom-call | flops 805306368 | bytes 3145728 | tf_op jit(solution)/shard_map/project/pallas_call | solution.py:396
  140.3 11.1 %all_to_all.16 = f32[16,8,128]{2,1,0:T(8,128)S(1)} all-to-all(f32[16,8,128]{2,1,0:T(8,128)S(1)} %project.5), channel_id=1, replica_groups=mesh['pw'=16,'band'=8] {'pw'}, dimensions={0} | all-to-all | bytes 131072 | tf_op jit(solution)/shard_map/all_to_all | solution.py:456
  (45 shorter events, 4.9 us)
Async XLA Ops:
  6.5 1.0 copy-start.4
  7.5 0.8 copy-start.6
  8.3 0.7 copy-start.8
  9.0 0.9 copy-start.10
  68.1 14.2 %all-to-all-start.1 = ((bf16[16,64,256]{2,1,0:T(8,128)(2,1)}), bf16[16,64,256]{2,1,0:T(8,128)(2,1)S(1)}, u32[]{:S(2)}, u32[]{:S(2)}) async-start(bf16[16,64,256]{2,1,0:T(8,128)(2,1)} %on_grid.1), calls=%async_computation.1 | async-start | bytes 1048576 | tf_op jit(solution)/shard_map/all_to_all | solution.py:444
  71.9 53.1 %all-gather.2.cloned.1.call-start = ((), (), s32[]{:S(2)}) async-start(), calls=%async_computation.3 | async-start | bytes 1769472 | tf_op jit(solution)/shard_map/all_gather | solution.py:441
  72.7 9.6 %copy-start.5 = (f32[4,2,12288]{2,1,0:T(2,128)S(1)}, f32[4,2,12288]{2,1,0:T(2,128)}, u32[]{:S(2)}) copy-start(f32[4,2,12288]{2,1,0:T(2,128)} %panel_ref.5) | copy-start | bytes 1179652
  72.7 9.6 %copy-start.7 = (s32[12288]{0:T(1024)S(1)}, s32[12288]{0:T(1024)}, u32[]{:S(2)}) copy-start(s32[12288]{0:T(1024)} %param.14) | copy-start | bytes 147460
  72.7 9.6 %copy-start.9 = (s32[256]{0:T(256)S(1)}, s32[256]{0:T(256)}, u32[]{:S(2)}) copy-start(s32[256]{0:T(256)} %param.15) | copy-start | bytes 3076
  72.7 9.6 %copy-start.11 = (bf16[352,256]{1,0:T(8,128)(2,1)S(1)}, bf16[352,256]{1,0:T(8,128)(2,1)}, u32[]{:S(2)}) copy-start(bf16[352,256]{1,0:T(8,128)(2,1)} %constant.71.clone.table_ref) | copy-start | bytes 540676
  88.1 36.9 %copy-start.3 = (s32[9]{0:T(128)S(1)}, s32[9]{0:T(128)}, u32[]{:S(2)}) copy-start(s32[9]{0:T(128)} %constant.64.clone.1.seat_ref) | copy-start | bytes 112
  88.1 8.9 %collective-permute-start.5 = (bf16[8,6144]{1,0:T(8,128)(2,1)S(1)}, bf16[8,6144]{1,0:T(8,128)(2,1)S(1)}, u32[]{:S(2)}, u32[]{:S(2)}) collective-permute-start(bf16[8,6144]{1,0:T(8,128)(2,1)S(1)} %collect.3), channel_id=1, source_target_pairs={{0,1},{1,0},{2,3},{3,2},{4,5},{5,4},{6,7},{7,6},{8,9},{9,8},{10,11... | collective-permute-start | bytes 294920 | tf_op jit(solution)/shard_map/ppermute | solution.py:422
  96.4 5.1 %collective-permute-start = (bf16[8,6144]{1,0:T(8,128)(2,1)S(1)}, bf16[8,6144]{1,0:T(8,128)(2,1)S(1)}, u32[]{:S(2)}, u32[]{:S(2)}) collective-permute-start(bf16[8,6144]{1,0:T(8,128)(2,1)S(1)} %collect.2), channel_id=1, source_target_pairs={{0,1},{1,0},{2,3},{3,2},{4,5},{5,4},{6,7},{7,6},{8,9},{9,8},{10,11... | collective-permute-start | bytes 294920 | tf_op jit(solution)/shard_map/ppermute | solution.py:422
  97.0 7.3 %collective-permute-start.6 = (bf16[2,8,6144]{2,1,0:T(8,128)(2,1)S(1)}, bf16[2,8,6144]{2,1,0:T(8,128)(2,1)S(1)}, u32[]{:S(2)}, u32[]{:S(2)}) collective-permute-start(bf16[2,8,6144]{2,1,0:T(8,128)(2,1)S(1)} %pad_maximum_fusion.1.refs_0_), channel_id=1, source_target_pairs={{0,2},{1,3},{2,4},{3,5},{4,6},{5,7},{6,0},{7,1},{8,10},{9,11},{10,... | collective-permute-start | bytes 589832 | tf_op jit(solution)/shard_map/ppermute | solution.py:422
  98.4 6.1 %collective-permute-start.7 = (bf16[2,8,6144]{2,1,0:T(8,128)(2,1)S(1)}, bf16[2,8,6144]{2,1,0:T(8,128)(2,1)S(1)}, u32[]{:S(2)}, u32[]{:S(2)}) collective-permute-start(bf16[2,8,6144]{2,1,0:T(8,128)(2,1)S(1)} %pad_maximum_fusion.1.refs_0_), channel_id=1, source_target_pairs={{0,6},{1,7},{2,0},{3,1},{4,2},{5,3},{6,4},{7,5},{8,14},{9,15},{10,... | collective-permute-start | bytes 589832 | tf_op jit(solution)/shard_map/ppermute | solution.py:422
  101.5 5.9 %collective-permute-start.1 = (bf16[2,8,6144]{2,1,0:T(8,128)(2,1)S(1)}, bf16[2,8,6144]{2,1,0:T(8,128)(2,1)S(1)}, u32[]{:S(2)}, u32[]{:S(2)}) collective-permute-start(bf16[2,8,6144]{2,1,0:T(8,128)(2,1)S(1)} %pad_maximum_fusion.refs_0_), channel_id=1, source_target_pairs={{0,2},{1,3},{2,4},{3,5},{4,6},{5,7},{6,0},{7,1},{8,10},{9,11},{10,... | collective-permute-start | bytes 589832 | tf_op jit(solution)/shard_map/ppermute | solution.py:422
  102.9 4.6 %collective-permute-start.2 = (bf16[2,8,6144]{2,1,0:T(8,128)(2,1)S(1)}, bf16[2,8,6144]{2,1,0:T(8,128)(2,1)S(1)}, u32[]{:S(2)}, u32[]{:S(2)}) collective-permute-start(bf16[2,8,6144]{2,1,0:T(8,128)(2,1)S(1)} %pad_maximum_fusion.refs_0_), channel_id=1, source_target_pairs={{0,6},{1,7},{2,0},{3,1},{4,2},{5,3},{6,4},{7,5},{8,14},{9,15},{10,... | collective-permute-start | bytes 589832 | tf_op jit(solution)/shard_map/ppermute | solution.py:422
  104.4 28.6 %collective-permute-start.8 = (bf16[8,6144]{1,0:T(8,128)(2,1)S(1)}, bf16[8,6144]{1,0:T(8,128)(2,1)S(1)}, u32[]{:S(2)}, u32[]{:S(2)}) collective-permute-start(bf16[8,6144]{1,0:T(8,128)(2,1)S(1)} %slice_bitcast_fusion.1), channel_id=1, source_target_pairs={{0,2},{1,3},{2,4},{3,5},{4,6},{5,7},{6,0},{7,1},{8,10},{9,11},{10,... | collective-permute-start | bytes 294920 | tf_op jit(solution)/shard_map/ppermute | solution.py:422
  104.5 28.5 %collective-permute-start.9 = (bf16[8,6144]{1,0:T(8,128)(2,1)S(1)}, bf16[8,6144]{1,0:T(8,128)(2,1)S(1)}, u32[]{:S(2)}, u32[]{:S(2)}) collective-permute-start(bf16[8,6144]{1,0:T(8,128)(2,1)S(1)} %slice_bitcast_fusion), channel_id=1, source_target_pairs={{0,6},{1,7},{2,0},{3,1},{4,2},{5,3},{6,4},{7,5},{8,14},{9,15},{10,... | collective-permute-start | bytes 294920 | tf_op jit(solution)/shard_map/ppermute | solution.py:422
  107.4 30.7 %collective-permute-start.3 = (bf16[8,6144]{1,0:T(8,128)(2,1)S(1)}, bf16[8,6144]{1,0:T(8,128)(2,1)S(1)}, u32[]{:S(2)}, u32[]{:S(2)}) collective-permute-start(bf16[8,6144]{1,0:T(8,128)(2,1)S(1)} %slice_bitcast_fusion.3), channel_id=1, source_target_pairs={{0,2},{1,3},{2,4},{3,5},{4,6},{5,7},{6,0},{7,1},{8,10},{9,11},{10,... | collective-permute-start | bytes 294920 | tf_op jit(solution)/shard_map/ppermute | solution.py:422
  107.5 30.6 %collective-permute-start.4 = (bf16[8,6144]{1,0:T(8,128)(2,1)S(1)}, bf16[8,6144]{1,0:T(8,128)(2,1)S(1)}, u32[]{:S(2)}, u32[]{:S(2)}) collective-permute-start(bf16[8,6144]{1,0:T(8,128)(2,1)S(1)} %slice_bitcast_fusion.2), channel_id=1, source_target_pairs={{0,6},{1,7},{2,0},{3,1},{4,2},{5,3},{6,4},{7,5},{8,14},{9,15},{10,... | collective-permute-start | bytes 294920 | tf_op jit(solution)/shard_map/ppermute | solution.py:422
  125.0 2.8 %copy-start = (bf16[2,128,12288]{2,1,0:T(8,128)(2,1)S(1)}, bf16[2,128,12288]{2,1,0:T(8,128)(2,1)}, u32[]{:S(2)}) copy-start(bf16[2,128,12288]{2,1,0:T(8,128)(2,1)} %copy.12) | copy-start | bytes 18874372
  127.8 1.4 copy-start.2
  133.1 2.8 %copy-start.1 = (bf16[2,128,12288]{2,1,0:T(8,128)(2,1)S(1)}, bf16[2,128,12288]{2,1,0:T(8,128)(2,1)}, u32[]{:S(2)}) copy-start(bf16[2,128,12288]{2,1,0:T(8,128)(2,1)} %copy.12) | copy-start | bytes 18874372
Sparse Core Ops, SparseCore 0:
  75.0 49.9 all-gather.1

commit v2 on v1

--- a/solution.py
+++ b/solution.py
@@ -15,8 +15,11 @@
 LEN = 128
 HALF_THREE = 44
 THIRDS = 2 * HALF_THREE
-HALF_ONE = 40
-FIRSTS = 2 * HALF_ONE
+EDGE = 40
+PARTS = 4
+STEP = 24
+USED = 20
+FIRSTS = PARTS * STEP
 NT = (((1,), (1,)), ((), ()))
 
 
@@ -38,7 +41,7 @@
     grid = np.arange(LEN)
     thirds = np.arange(-HALF_THREE, HALF_THREE)
     row = np.arange(FIRSTS)
-    firsts = 2 * (row % HALF_ONE) + row // HALF_ONE - HALF_ONE
+    firsts = PARTS * (row % STEP) + row // STEP - EDGE
     planes = LEN // parts
     order = np.arange(2 * LEN).reshape(2, parts, planes).transpose(1, 0, 2).ravel()
     beside = lambda table, axis: np.concatenate(split(table), axis=axis)
@@ -154,7 +157,7 @@
             jax.ShapeDtypeStruct((2 * count, waves), BF16),
         ],
         scratch_shapes=[pltpu.VMEM((cols // LEN, 4 * count * THIRDS, LEN), F32)],
-        compiler_params=pltpu.CompilerParams(vmem_limit_bytes=40 << 20),
+        compiler_params=pltpu.CompilerParams(vmem_limit_bytes=56 << 20),
         cost_estimate=pl.CostEstimate(
             flops=2 * 4 * count * THIRDS * cols * waves, bytes_accessed=4 << 20, transcendentals=0
         ),
@@ -162,7 +165,7 @@
     )(slot, columns, panel, jnp.asarray(table))
 
 
-def grid_kernel(in_ref, pot_ref, ti_ref, oi_ref, oo_ref, to_ref, out_ref, pick_ref, mask_ref, lhs_ref):
+def grid_kernel(in_ref, pot_ref, ti_ref, oi_ref, oo_ref, to_ref, out_ref, pick_ref, first_ref, lhs_ref, found_ref, field_ref):
     owners, rows, cols = out_ref.shape
     planes = pot_ref.shape[0]
     tall = 2 * planes
@@ -171,19 +174,19 @@
     for owner in range(owners):
         here = slice(owner * cols, (owner + 1) * cols)
         values = in_ref[owner].astype(F32)
-        first = (values[rows : rows + 1].astype(jnp.int32) + HALF_ONE) & (LEN - 1)
-        inner = (first & 1) * LEN + values[rows + 1 : rows + 2].astype(jnp.int32)
-        pick_ref[:, here] = one_hot(inner, 2 * LEN).astype(BF16)
-        mask = one_hot(first >> 1, HALF_ONE).astype(F32)
-        mask_ref[:, here] = mask
+        first = (values[rows : rows + 1].astype(jnp.int32) + EDGE) & (LEN - 1)
+        inner = (first & (PARTS - 1)) * LEN + values[rows + 1 : rows + 2].astype(jnp.int32)
+        pick_ref[:, here] = one_hot(inner, PARTS * LEN).astype(BF16)
+        mask = one_hot(first // PARTS, STEP).astype(F32)
+        first_ref[owner : owner + 1, :] = first // PARTS
         lhs_ref[:, here] = jnp.concatenate(
             [values[row : row + 1] * mask for row in range(rows)], axis=0
         ).astype(BF16)
     field = dot_nt(lhs_ref[...], pick_ref[...]).astype(BF16)
-    block = planes * HALF_ONE
+    block = planes * STEP
     lanes = lambda bit: slice(bit * LEN, (bit + 1) * LEN)
     spun = []
-    for bit in range(2):
+    for bit in range(PARTS):
         pair = jnp.concatenate(
             [
                 jnp.concatenate(
@@ -199,9 +202,9 @@
         [
             jnp.concatenate(
                 [
-                    spun[bit][item * HALF_ONE : (item + 1) * HALF_ONE, lanes(part)]
+                    spun[bit][item * STEP : (item + 1) * STEP, lanes(part)]
                     for part in range(2)
-                    for bit in range(2)
+                    for bit in range(PARTS)
                 ],
                 axis=0,
             )
@@ -214,13 +217,13 @@
     psi = jnp.concatenate([psi[:LEN] * pot, psi[LEN:] * pot], axis=0).astype(BF16)
     back = fold(dot(oo_ref[...], psi), 0)
     bent = []
-    for bit in range(2):
+    for bit in range(PARTS):
         pair = jnp.concatenate(
             [
                 jnp.concatenate(
                     [
                         back[
-                            part * FIRSTS + bit * HALF_ONE : part * FIRSTS + (bit + 1) * HALF_ONE,
+                            part * FIRSTS + bit * STEP : part * FIRSTS + (bit + 1) * STEP,
                             item * LEN : (item + 1) * LEN,
                         ]
                         for part in range(2)
@@ -232,27 +235,24 @@
             axis=0,
         ).astype(BF16)
         bent.append(fold(dot(pair, to_ref[...]), 1))
-    field = jnp.concatenate(
-        [
-            jnp.concatenate(
-                [bent[bit][band * block : (band + 1) * block, lanes(part)] for bit in range(2)], axis=1
-            )
-            for band in range(count)
-            for part in range(2)
-        ],
-        axis=0,
-    ).astype(BF16)
+    for bit in range(PARTS):
+        for item in range(count * planes):
+            band, plane = divmod(item, planes)
+            for part in range(2):
+                found_ref[bit, pl.ds((2 * band + part) * planes + plane, USED, stride=rows), :] = bent[bit][
+                    item * STEP : item * STEP + USED, lanes(part)
+                ]
+    for bit in range(PARTS):
+        field_ref[:, lanes(bit)] = found_ref[bit].astype(BF16)
     for owner in range(owners):
         here = slice(owner * cols, (owner + 1) * cols)
-        values = dot(field, pick_ref[:, here])
-        mask = mask_ref[:, here]
-        out_ref[owner] = jnp.concatenate(
-            [
-                jnp.sum(values[row * HALF_ONE : (row + 1) * HALF_ONE] * mask, axis=0, keepdims=True)
-                for row in range(rows)
-            ],
-            axis=0,
-        ).astype(BF16)
+        values = dot(field_ref[...], pick_ref[:, here])
+        first = jnp.broadcast_to(first_ref[owner : owner + 1, :], (rows, cols))
+        zero = jnp.zeros((rows, cols), F32)
+        total = zero
+        for at in range(USED):
+            total += jnp.where(first == at, values[at * rows : (at + 1) * rows], zero)
+        out_ref[owner] = total.astype(BF16)
 
 
 def on_grid(waves, potential):
@@ -265,13 +265,15 @@
         out_specs=whole(owners, rows, cols),
         out_shape=jax.ShapeDtypeStruct((owners, rows, cols), BF16),
         scratch_shapes=[
-            pltpu.VMEM((2 * LEN, owners * cols), BF16),
-            pltpu.VMEM((HALF_ONE, owners * cols), F32),
-            pltpu.VMEM((rows * HALF_ONE, owners * cols), BF16),
+            pltpu.VMEM((PARTS * LEN, owners * cols), BF16),
+            pltpu.VMEM((owners, cols), jnp.int32),
+            pltpu.VMEM((rows * STEP, owners * cols), BF16),
+            pltpu.VMEM((PARTS, rows * USED, LEN), F32),
+            pltpu.VMEM((rows * USED, PARTS * LEN), BF16),
         ],
         compiler_params=pltpu.CompilerParams(vmem_limit_bytes=56 << 20),
         cost_estimate=pl.CostEstimate(
-            flops=2 * 2 * rows * HALF_ONE * 2 * LEN * owners * cols,
+            flops=2 * 2 * rows * USED * PARTS * LEN * owners * cols,
             bytes_accessed=4 << 20,
             transcendentals=0,
         ),
@@ -349,7 +351,7 @@
             pltpu.VMEM((cols // LEN, 2 * count * THIRDS, LEN), F32),
             pltpu.VMEM((2 * count * THIRDS + 16, 2 * cols), BF16),
         ],
-        compiler_params=pltpu.CompilerParams(vmem_limit_bytes=40 << 20),
+        compiler_params=pltpu.CompilerParams(vmem_limit_bytes=56 << 20),
         cost_estimate=pl.CostEstimate(
             flops=2 * 4 * count * THIRDS * cols * length, bytes_accessed=4 << 20, transcendentals=0
         ),
@@ -407,7 +409,7 @@
             scratch_shapes=[pltpu.VMEM((sum(sizes), both.shape[0]), F32)],
         ),
         out_shape=jax.ShapeDtypeStruct(prev.shape, F32),
-        compiler_params=pltpu.CompilerParams(vmem_limit_bytes=32 << 20),
+        compiler_params=pltpu.CompilerParams(vmem_limit_bytes=56 << 20),
         cost_estimate=pl.CostEstimate(
             flops=2 * 256 * both.shape[0] * length,
             bytes_accessed=2 * both.shape[0] * length,
@@ -436,23 +438,25 @@
     cols = columns.shape[0]
     slot = pw_slot.reshape(1, length)
     columns = columns.reshape(1, cols)
-    waves, coeffs = spread(panel, slot, columns, parts, 2048)
+    waves, coeffs = spread(panel, slot, columns, parts, 3072)
     waves = lax.all_to_all(waves, "pw", split_axis=0, concat_axis=0, tiled=True)
     coeffs = lax.all_gather(coeffs, "band", axis=0, tiled=True)
-    both = lax.optimization_barrier(jnp.transpose(slab, (1, 0, 2)).reshape(2 * bands, length))
+    both = jnp.transpose(slab, (1, 0, 2)).reshape(2 * bands, length)
+    waves, both = lax.optimization_barrier((waves, both))
     waves = on_grid(waves, potential)
     waves = lax.all_to_all(waves, "pw", split_axis=0, concat_axis=0, tiled=True)
+    waves, coeffs = lax.optimization_barrier((waves, coeffs))
     me = lax.axis_index("band")
     row, odd = me // 2, me % 2
     terms = jnp.zeros((parts, bands // parts, bands), F32)
     pick = lambda *seats: jnp.stack([jnp.asarray(seat, jnp.int32) for seat in seats])
     seats = pick(8, 9, 10, 11, 0, 0, 0, 0, 0)
-    terms = project([coeffs], both, terms, seats, 0, 2048)
+    terms = project([coeffs], both, terms, seats, 0, 3072)
     seats = pick(row, (row + 3) % 4, (row + 1) % 4, (row + 2) % 4, 0, 0, 0, 0, odd)
     step = length // PIECES
     for piece in range(PIECES):
-        applied = collect(panel, slot, columns, waves, piece * step, step, min(2048, step))
-        terms = project(share(applied), both, terms, seats, piece * step, min(2048, step))
+        applied = collect(panel, slot, columns, waves, piece * step, step, min(3072, step))
+        terms = project(share(applied), both, terms, seats, piece * step, min(3072, step))
     terms = lax.all_to_all(terms, "pw", split_axis=0, concat_axis=0, tiled=True)
     return jnp.sum(terms, axis=0).T
 

time: 162 us -> 147 us (0.907); the launches traced: 159 us -> 146 us
  blocking collectives: 30 us -> 13.9 us
  starting transfers between devices: 18.6 us -> 27.7 us
  local copies, waits for them, and re-layouts: 20 us -> 14.9 us
  waiting for transfers between devices: 16.9 us -> 12.4 us
  Pallas kernels: 59.1 us -> 62.3 us
    all_to_all x1 -> x0, blocking collectives: 18.9 us -> none  [per_device(): waves = lax.all_to_all(waves, 'pw', split_axis=0, concat_axis=0, tiled=True)]
    all_gather x1, waiting for transfers between devices: 14.8 us -> 0.01 us  [per_device(): coeffs = lax.all_gather(coeffs, 'band', axis=0, tiled=True)]
    all_to_all x1 -> x2, waiting for transfers between devices: 0.01 us -> 10.8 us  [per_device(): waves = lax.all_to_all(waves, 'pw', split_axis=0, concat_axis=0, tiled=True)]
    all_to_all x1 -> x2, starting transfers between devices: 3.8 us -> 12.8 us  [per_device(): waves = lax.all_to_all(waves, 'pw', split_axis=0, concat_axis=0, tiled=True)]
    pallas_call x1, Pallas kernels: 27.5 us -> 20.3 us  [on_grid(): pl.pallas_call(grid_kernel, in_specs=[whole(*waves.shape), whole(*potenti...]
    pallas_call x3, Pallas kernels: 8.3 us -> 14.7 us  [project(): pl.pallas_call(functools.partial(project_kernel, sizes), grid_spec=pltpu....]
    unnamed x24 -> x26, local copies, waits for them, and re-layouts: 10.4 us -> 4.24 us
    pallas_call x2, Pallas kernels: 11.6 us -> 14.7 us  [collect(): pl.pallas_call(collect_kernel, grid=(length // chunk,), in_specs=[pl.Bloc...]
  transfers between devices with their start and end apart: 12 -> 13, of which waited for: 3 -> 3; matrix products, arithmetic and copies ran while one was open for 6% -> 8% of each run, Pallas kernels for 11% -> 26%
where the time goes in v2:
time: 147 us; the launch traced here: 146 us
  Pallas kernels  62.3 us (42%)
  starting transfers between devices  27.7 us (19%)
  local copies, waits for them, and re-layouts  14.9 us (10%)
  blocking collectives  13.9 us (9%)
  between operations  13.6 us (9%)
  waiting for transfers between devices  12.4 us (8%)
  other arithmetic  1.54 us (1%)
    pallas_call x1, Pallas kernels, on_grid(): pl.pallas_call(grid_kernel, in_specs=[whole(*waves.shape), whole(*potenti...  20.3 us
    ppermute x10, starting transfers between devices, moved(): return lax.ppermute(x, axis, [(i, target(i) % size) for i in range(size)])  15 us
    pallas_call x3, Pallas kernels, project(): pl.pallas_call(functools.partial(project_kernel, sizes), grid_spec=pltpu....  14.7 us
    pallas_call x2, Pallas kernels, collect(): pl.pallas_call(collect_kernel, grid=(length // chunk,), in_specs=[pl.Bloc...  14.7 us
    all_to_all x1, blocking collectives, per_device(): terms = lax.all_to_all(terms, 'pw', split_axis=0, concat_axis=0, tiled=True)  13.9 us
    all_to_all x2, starting transfers between devices, per_device(): waves = lax.all_to_all(waves, 'pw', split_axis=0, concat_axis=0, tiled=True)  12.8 us
    pallas_call x1, Pallas kernels, spread(): pl.pallas_call(spread_kernel, grid=(waves // chunk,), in_specs=[pl.BlockS...  12.6 us
    all_to_all x2, waiting for transfers between devices, per_device(): waves = lax.all_to_all(waves, 'pw', split_axis=0, concat_axis=0, tiled=True)  10.8 us
  transfers between devices with their start and end apart: 13, of which 3 were waited for; matrix products, arithmetic and copies ran while one was open for 8% of the time, Pallas kernels for 26%

profile of v2, /device:TPU:1, one launch (start us, length us, event | category | flops | bytes accessed | tf_op | source)
XLA Modules:
  0.0 146.4 jit_solution(4433784366869035832)
XLA Ops:
  6.5 12.6 %spread.1 = (bf16[16,72,256]{2,1,0:T(8,128)(2,1)}, bf16[8,12288]{1,0:T(8,128)(2,1)}) custom-call(s32[1,12288]{1,0:T(1,128)} %bitcast.30, s32[1,256]{1,0:T(1,128)} %bitcast.33, f32[4,2,12288]{2,1,0:T(2,128)} %panel_ref.5, bf16[512,176]{1,0:T(8,128)(2,1)} %constant.66.clone.table_ref), custom_call_target="tpu_custom_call" | custom-call | flops 8858370048 | bytes 4194304 | tf_op jit(solution)/shard_map/spread/pallas_call | solution.py:142
  19.1 7.8 %all-to-all-start = ((bf16[16,72,256]{2,1,0:T(8,128)(2,1)}), bf16[16,72,256]{2,1,0:T(8,128)(2,1)S(1)}, u32[]{:S(2)}, u32[]{:S(2)}) async-start(bf16[16,72,256]{2,1,0:T(8,128)(2,1)} %get-tuple-element.11), calls=%async_computation | async-start | bytes 1179648 | tf_op jit(solution)/shard_map/all_to_all | solution.py:442
  26.9 9.4 %copy.12 = bf16[2,128,12288]{2,1,0:T(8,128)(2,1)} copy(bf16[2,128,12288]{2,0,1:T(2,128)(2,1)} %bitcast.25) | data formatting | bytes 12582912 | tf_op jit(solution)/shard_map/transpose | solution.py:444
  36.3 1.5 %all-to-all-done.in_ref = bf16[16,72,256]{2,1,0:T(8,128)(2,1)S(1)} async-done(((bf16[16,72,256]{2,1,0:T(8,128)(2,1)}), bf16[16,72,256]{2,1,0:T(8,128)(2,1)S(1)}, u32[]{:S(2)}, u32[]{:S(2)}) %all-to-all-start) | async-done | bytes 589856 | tf_op jit(solution)/shard_map/all_to_all | solution.py:442
  37.9 0.9 copy-done.2
  38.7 20.3 %on_grid.1 = bf16[16,64,256]{2,1,0:T(8,128)(2,1)} custom-call(bf16[16,72,256]{2,1,0:T(8,128)(2,1)} %copy-done.2, f32[8,128,128]{2,1,0:T(8,128)} %pot_ref.1, bf16[256,512]{1,0:T(8,128)(2,1)} %constant.67.clone.ti_ref, bf16[512,192]{1,0:T(8,128)(2,1)} %constant.68.clone.oi_ref, bf16[384,256]{1,0:T(8,128)(2,1)} %constant.69.clone.oo_ref, ...), custom_call_target="tpu_custom_call" | custom-call | flops 10737418240 | bytes 4194304 | tf_op jit(solution)/shard_map/on_grid/pallas_call | solution.py:262
  59.0 5.0 %all-to-all-start.1 = ((bf16[16,64,256]{2,1,0:T(8,128)(2,1)}), bf16[16,64,256]{2,1,0:T(8,128)(2,1)S(1)}, u32[]{:S(2)}, u32[]{:S(2)}) async-start(bf16[16,64,256]{2,1,0:T(8,128)(2,1)} %on_grid.1), calls=%async_computation.1 | async-start | bytes 1048576 | tf_op jit(solution)/shard_map/all_to_all | solution.py:447
  64.7 9.3 %all-to-all-done.1.in_ref = bf16[16,64,256]{2,1,0:T(8,128)(2,1)S(1)} async-done(((bf16[16,64,256]{2,1,0:T(8,128)(2,1)}), bf16[16,64,256]{2,1,0:T(8,128)(2,1)S(1)}, u32[]{:S(2)}, u32[]{:S(2)}) %all-to-all-start.1) | async-done | bytes 524320 | tf_op jit(solution)/shard_map/all_to_all | solution.py:447
  73.9 0.9 copy-done.3
  74.8 7.3 %collect.3 = bf16[8,6144]{1,0:T(8,128)(2,1)} custom-call(s32[1,12288]{1,0:T(1,128)} %bitcast.31, s32[1,256]{1,0:T(1,128)} %bitcast.34, f32[4,2,12288]{2,1,0:T(2,128)} %panel_ref.5, bf16[16,64,256]{2,1,0:T(8,128)(2,1)} %copy-done.3, bf16[352,256]{1,0:T(8,128)(2,1)} %constant.71.clone.table_ref), custom_call_target="tpu_custom_call" | custom-call | flops 4429185024 | bytes 4194304 | tf_op jit(solution)/shard_map/collect/pallas_call | solution.py:338
  82.1 2.5 %collective-permute-start.5 = (bf16[8,6144]{1,0:T(8,128)(2,1)}, bf16[8,6144]{1,0:T(8,128)(2,1)S(1)}, u32[]{:S(2)}, u32[]{:S(2)}) collective-permute-start(bf16[8,6144]{1,0:T(8,128)(2,1)} %collect.3), channel_id=1, source_target_pairs={{0,1},{1,0},{2,3},{3,2},{4,5},{5,4},{6,7},{7,6},{8,9},{9,8},{10,11... | collective-permute-start | bytes 294920 | tf_op jit(solution)/shard_map/ppermute | solution.py:424
  84.6 7.3 %collect.2 = bf16[8,6144]{1,0:T(8,128)(2,1)} custom-call(s32[1,12288]{1,0:T(1,128)} %bitcast.32, s32[1,256]{1,0:T(1,128)} %bitcast.35, f32[4,2,12288]{2,1,0:T(2,128)} %panel_ref.5, bf16[16,64,256]{2,1,0:T(8,128)(2,1)} %copy-done.3, bf16[352,256]{1,0:T(8,128)(2,1)} %constant.71.clone.table_ref), custom_call_target="tpu_custom_call" | custom-call | flops 4429185024 | bytes 4194304 | tf_op jit(solution)/shard_map/collect/pallas_call | solution.py:338
  92.4 3.1 %collective-permute-start.7 = (bf16[2,8,6144]{2,1,0:T(8,128)(2,1)S(1)}, bf16[2,8,6144]{2,1,0:T(8,128)(2,1)S(1)}, u32[]{:S(2)}, u32[]{:S(2)}) collective-permute-start(bf16[2,8,6144]{2,1,0:T(8,128)(2,1)S(1)} %pad_maximum_fusion.1.refs_0_), channel_id=1, source_target_pairs={{0,6},{1,7},{2,0},{3,1},{4,2},{5,3},{6,4},{7,5},{8,14},{9,15},{10,... | collective-permute-start | bytes 589832 | tf_op jit(solution)/shard_map/ppermute | solution.py:424
  95.5 1.6 %collective-permute-done = bf16[8,6144]{1,0:T(8,128)(2,1)S(1)} collective-permute-done((bf16[8,6144]{1,0:T(8,128)(2,1)}, bf16[8,6144]{1,0:T(8,128)(2,1)S(1)}, u32[]{:S(2)}, u32[]{:S(2)}) %collective-permute-start) | collective-permute-done | bytes 98336 | tf_op jit(solution)/shard_map/ppermute | solution.py:424
  97.1 0.9 pad_maximum_fusion.refs_0_
  98.0 3.1 %collective-permute-start.2 = (bf16[2,8,6144]{2,1,0:T(8,128)(2,1)S(1)}, bf16[2,8,6144]{2,1,0:T(8,128)(2,1)S(1)}, u32[]{:S(2)}, u32[]{:S(2)}) collective-permute-start(bf16[2,8,6144]{2,1,0:T(8,128)(2,1)S(1)} %pad_maximum_fusion.refs_0_), channel_id=1, source_target_pairs={{0,6},{1,7},{2,0},{3,1},{4,2},{5,3},{6,4},{7,5},{8,14},{9,15},{10,... | collective-permute-start | bytes 589832 | tf_op jit(solution)/shard_map/ppermute | solution.py:424
  101.2 2.7 %collective-permute-start.9 = (bf16[8,6144]{1,0:T(8,128)(2,1)S(1)}, bf16[8,6144]{1,0:T(8,128)(2,1)S(1)}, u32[]{:S(2)}, u32[]{:S(2)}) collective-permute-start(bf16[8,6144]{1,0:T(8,128)(2,1)S(1)} %slice_bitcast_fusion), channel_id=1, source_target_pairs={{0,6},{1,7},{2,0},{3,1},{4,2},{5,3},{6,4},{7,5},{8,14},{9,15},{10,... | collective-permute-start | bytes 294920 | tf_op jit(solution)/shard_map/ppermute | solution.py:424
  104.0 2.9 %collective-permute-start.4 = (bf16[8,6144]{1,0:T(8,128)(2,1)S(1)}, bf16[8,6144]{1,0:T(8,128)(2,1)S(1)}, u32[]{:S(2)}, u32[]{:S(2)}) collective-permute-start(bf16[8,6144]{1,0:T(8,128)(2,1)S(1)} %slice_bitcast_fusion.2), channel_id=1, source_target_pairs={{0,6},{1,7},{2,0},{3,1},{4,2},{5,3},{6,4},{7,5},{8,14},{9,15},{10,... | collective-permute-start | bytes 294920 | tf_op jit(solution)/shard_map/ppermute | solution.py:424
  107.7 6.4 %project.3.refs_6_ = f32[16,8,128]{2,1,0:T(8,128)} custom-call(s32[9]{0:T(128)} %constant.64.clone.1.seat_ref, bf16[64,12288]{1,0:T(8,128)(2,1)} %all-gather.2.cloned.1.call-done.refs_0_, bf16[256,12288]{1,0:T(8,128)(2,1)} %bitcast.22, f32[16,8,128]{2,1,0:T(8,128)} %broadcast_in_dim.3.refs_2_), custom_call_target="tpu_custom_call" | custom-call | flops 1610612736 | bytes 6291456 | tf_op jit(solution)/shard_map/project/pallas_call | solution.py:398
  114.7 0.6 copy-done.11
  115.3 4.2 %project.4.refs_6_ = f32[16,8,128]{2,1,0:T(8,128)} custom-call(s32[9]{0:T(128)} %stack.41.seat_ref, bf16[2,8,6144]{2,1,0:T(8,128)(2,1)} %copy-done.1, bf16[2,8,6144]{2,1,0:T(8,128)(2,1)} %copy-done.7, bf16[2,8,6144]{2,1,0:T(8,128)(2,1)} %copy-done.5, bf16[8,6144]{1,0:T(8,128)(2,1)} %copy-done.11, bf16[8,6144]{1,0:T(8,128)(2,1)} %copy-done.9, ...), custom_call_target="tpu_custom_call" | custom-call | flops 805306368 | bytes 3145728 | tf_op jit(solution)/shard_map/project/pallas_call | solution.py:398
  120.2 0.6 copy-done.10
  120.8 4.2 %project.5 = f32[16,8,128]{2,1,0:T(8,128)} custom-call(s32[9]{0:T(128)} %stack.41.seat_ref, bf16[2,8,6144]{2,1,0:T(8,128)(2,1)} %copy-done, bf16[2,8,6144]{2,1,0:T(8,128)(2,1)} %copy-done.6, bf16[2,8,6144]{2,1,0:T(8,128)(2,1)} %copy-done.4, bf16[8,6144]{1,0:T(8,128)(2,1)} %copy-done.10, bf16[8,6144]{1,0:T(8,128)(2,1)} %copy-done.8, ...), custom_call_target="tpu_custom_call" | custom-call | flops 805306368 | bytes 3145728 | tf_op jit(solution)/shard_map/project/pallas_call | solution.py:398
  125.0 13.9 %all_to_all.15 = f32[16,8,128]{2,1,0:T(8,128)S(1)} all-to-all(f32[16,8,128]{2,1,0:T(8,128)} %project.5), channel_id=1, replica_groups=mesh['pw'=16,'band'=8] {'pw'}, dimensions={0} | all-to-all | bytes 131072 | tf_op jit(solution)/shard_map/all_to_all | solution.py:460
  (48 shorter events, 3.9 us)
Async XLA Ops:
  6.5 67.4 %all-gather.2.cloned.1.call-start = ((), (), s32[]{:S(2)}) async-start(), calls=%async_computation.3 | async-start | bytes 1769472 | tf_op jit(solution)/shard_map/all_gather | solution.py:443
  19.1 18.7 %all-to-all-start = ((bf16[16,72,256]{2,1,0:T(8,128)(2,1)}), bf16[16,72,256]{2,1,0:T(8,128)(2,1)S(1)}, u32[]{:S(2)}, u32[]{:S(2)}) async-start(bf16[16,72,256]{2,1,0:T(8,128)(2,1)} %get-tuple-element.11), calls=%async_computation | async-start | bytes 1179648 | tf_op jit(solution)/shard_map/all_to_all | solution.py:442
  37.8 0.9 copy-start.2
  59.0 14.9 %all-to-all-start.1 = ((bf16[16,64,256]{2,1,0:T(8,128)(2,1)}), bf16[16,64,256]{2,1,0:T(8,128)(2,1)S(1)}, u32[]{:S(2)}, u32[]{:S(2)}) async-start(bf16[16,64,256]{2,1,0:T(8,128)(2,1)} %on_grid.1), calls=%async_computation.1 | async-start | bytes 1048576 | tf_op jit(solution)/shard_map/all_to_all | solution.py:447
  73.9 0.9 copy-start.3
  82.1 10.3 %copy-start.12 = (bf16[8,6144]{1,0:T(8,128)(2,1)S(1)}, bf16[8,6144]{1,0:T(8,128)(2,1)}, u32[]{:S(2)}) copy-start(bf16[8,6144]{1,0:T(8,128)(2,1)} %collect.3) | copy-start | bytes 294916
  82.1 10.3 %collective-permute-start.5 = (bf16[8,6144]{1,0:T(8,128)(2,1)}, bf16[8,6144]{1,0:T(8,128)(2,1)S(1)}, u32[]{:S(2)}, u32[]{:S(2)}) collective-permute-start(bf16[8,6144]{1,0:T(8,128)(2,1)} %collect.3), channel_id=1, source_target_pairs={{0,1},{1,0},{2,3},{3,2},{4,5},{5,4},{6,7},{7,6},{8,9},{9,8},{10,11... | collective-permute-start | bytes 294920 | tf_op jit(solution)/shard_map/ppermute | solution.py:424
  91.9 5.2 %collective-permute-start = (bf16[8,6144]{1,0:T(8,128)(2,1)}, bf16[8,6144]{1,0:T(8,128)(2,1)S(1)}, u32[]{:S(2)}, u32[]{:S(2)}) collective-permute-start(bf16[8,6144]{1,0:T(8,128)(2,1)} %collect.2), channel_id=1, source_target_pairs={{0,1},{1,0},{2,3},{3,2},{4,5},{5,4},{6,7},{7,6},{8,9},{9,8},{10,11... | collective-permute-start | bytes 294920 | tf_op jit(solution)/shard_map/ppermute | solution.py:424
  92.4 21.6 %copy-start.1 = (bf16[2,8,6144]{2,1,0:T(8,128)(2,1)}, bf16[2,8,6144]{2,1,0:T(8,128)(2,1)S(1)}, u32[]{:S(2)}) copy-start(bf16[2,8,6144]{2,1,0:T(8,128)(2,1)S(1)} %pad_maximum_fusion.1.refs_0_) | copy-start | bytes 589828
  92.4 8.7 %collective-permute-start.7 = (bf16[2,8,6144]{2,1,0:T(8,128)(2,1)S(1)}, bf16[2,8,6144]{2,1,0:T(8,128)(2,1)S(1)}, u32[]{:S(2)}, u32[]{:S(2)}) collective-permute-start(bf16[2,8,6144]{2,1,0:T(8,128)(2,1)S(1)} %pad_maximum_fusion.1.refs_0_), channel_id=1, source_target_pairs={{0,6},{1,7},{2,0},{3,1},{4,2},{5,3},{6,4},{7,5},{8,14},{9,15},{10,... | collective-permute-start | bytes 589832 | tf_op jit(solution)/shard_map/ppermute | solution.py:424
  95.5 8.4 %collective-permute-start.6 = (bf16[2,8,6144]{2,1,0:T(8,128)(2,1)S(1)}, bf16[2,8,6144]{2,1,0:T(8,128)(2,1)S(1)}, u32[]{:S(2)}, u32[]{:S(2)}) collective-permute-start(bf16[2,8,6144]{2,1,0:T(8,128)(2,1)S(1)} %pad_maximum_fusion.1.refs_0_), channel_id=1, source_target_pairs={{0,2},{1,3},{2,4},{3,5},{4,6},{5,7},{6,0},{7,1},{8,10},{9,11},{10,... | collective-permute-start | bytes 589832 | tf_op jit(solution)/shard_map/ppermute | solution.py:424
  98.0 21.5 %copy-start = (bf16[2,8,6144]{2,1,0:T(8,128)(2,1)}, bf16[2,8,6144]{2,1,0:T(8,128)(2,1)S(1)}, u32[]{:S(2)}) copy-start(bf16[2,8,6144]{2,1,0:T(8,128)(2,1)S(1)} %pad_maximum_fusion.refs_0_) | copy-start | bytes 589828
  98.0 6.0 %collective-permute-start.2 = (bf16[2,8,6144]{2,1,0:T(8,128)(2,1)S(1)}, bf16[2,8,6144]{2,1,0:T(8,128)(2,1)S(1)}, u32[]{:S(2)}, u32[]{:S(2)}) collective-permute-start(bf16[2,8,6144]{2,1,0:T(8,128)(2,1)S(1)} %pad_maximum_fusion.refs_0_), channel_id=1, source_target_pairs={{0,6},{1,7},{2,0},{3,1},{4,2},{5,3},{6,4},{7,5},{8,14},{9,15},{10,... | collective-permute-start | bytes 589832 | tf_op jit(solution)/shard_map/ppermute | solution.py:424
  101.1 5.8 %collective-permute-start.1 = (bf16[2,8,6144]{2,1,0:T(8,128)(2,1)S(1)}, bf16[2,8,6144]{2,1,0:T(8,128)(2,1)S(1)}, u32[]{:S(2)}, u32[]{:S(2)}) collective-permute-start(bf16[2,8,6144]{2,1,0:T(8,128)(2,1)S(1)} %pad_maximum_fusion.refs_0_), channel_id=1, source_target_pairs={{0,2},{1,3},{2,4},{3,5},{4,6},{5,7},{6,0},{7,1},{8,10},{9,11},{10,... | collective-permute-start | bytes 589832 | tf_op jit(solution)/shard_map/ppermute | solution.py:424
  101.1 12.9 %copy-start.5 = (bf16[2,8,6144]{2,1,0:T(8,128)(2,1)}, bf16[2,8,6144]{2,1,0:T(8,128)(2,1)S(1)}, u32[]{:S(2)}) copy-start(bf16[2,8,6144]{2,1,0:T(8,128)(2,1)S(1)} %collective-permute-done.7.refs_2_) | copy-start | bytes 589828
  101.2 12.9 %collective-permute-start.9 = (bf16[8,6144]{1,0:T(8,128)(2,1)S(1)}, bf16[8,6144]{1,0:T(8,128)(2,1)S(1)}, u32[]{:S(2)}, u32[]{:S(2)}) collective-permute-start(bf16[8,6144]{1,0:T(8,128)(2,1)S(1)} %slice_bitcast_fusion), channel_id=1, source_target_pairs={{0,6},{1,7},{2,0},{3,1},{4,2},{5,3},{6,4},{7,5},{8,14},{9,15},{10,... | collective-permute-start | bytes 294920 | tf_op jit(solution)/shard_map/ppermute | solution.py:424
  103.9 10.2 %copy-start.7 = (bf16[2,8,6144]{2,1,0:T(8,128)(2,1)}, bf16[2,8,6144]{2,1,0:T(8,128)(2,1)S(1)}, u32[]{:S(2)}) copy-start(bf16[2,8,6144]{2,1,0:T(8,128)(2,1)S(1)} %collective-permute-done.6.refs_1_) | copy-start | bytes 589828
  103.9 10.2 %collective-permute-start.8 = (bf16[8,6144]{1,0:T(8,128)(2,1)S(1)}, bf16[8,6144]{1,0:T(8,128)(2,1)S(1)}, u32[]{:S(2)}, u32[]{:S(2)}) collective-permute-start(bf16[8,6144]{1,0:T(8,128)(2,1)S(1)} %slice_bitcast_fusion.1), channel_id=1, source_target_pairs={{0,2},{1,3},{2,4},{3,5},{4,6},{5,7},{6,0},{7,1},{8,10},{9,11},{10,... | collective-permute-start | bytes 294920 | tf_op jit(solution)/shard_map/ppermute | solution.py:424
  104.0 15.5 %copy-start.4 = (bf16[2,8,6144]{2,1,0:T(8,128)(2,1)}, bf16[2,8,6144]{2,1,0:T(8,128)(2,1)S(1)}, u32[]{:S(2)}) copy-start(bf16[2,8,6144]{2,1,0:T(8,128)(2,1)S(1)} %collective-permute-done.2.refs_2_) | copy-start | bytes 589828
  104.0 15.5 %collective-permute-start.4 = (bf16[8,6144]{1,0:T(8,128)(2,1)S(1)}, bf16[8,6144]{1,0:T(8,128)(2,1)S(1)}, u32[]{:S(2)}, u32[]{:S(2)}) collective-permute-start(bf16[8,6144]{1,0:T(8,128)(2,1)S(1)} %slice_bitcast_fusion.2), channel_id=1, source_target_pairs={{0,6},{1,7},{2,0},{3,1},{4,2},{5,3},{6,4},{7,5},{8,14},{9,15},{10,... | collective-permute-start | bytes 294920 | tf_op jit(solution)/shard_map/ppermute | solution.py:424
  107.0 12.6 %copy-start.6 = (bf16[2,8,6144]{2,1,0:T(8,128)(2,1)}, bf16[2,8,6144]{2,1,0:T(8,128)(2,1)S(1)}, u32[]{:S(2)}) copy-start(bf16[2,8,6144]{2,1,0:T(8,128)(2,1)S(1)} %collective-permute-done.1.refs_1_) | copy-start | bytes 589828
  107.0 12.6 %collective-permute-start.3 = (bf16[8,6144]{1,0:T(8,128)(2,1)S(1)}, bf16[8,6144]{1,0:T(8,128)(2,1)S(1)}, u32[]{:S(2)}, u32[]{:S(2)}) collective-permute-start(bf16[8,6144]{1,0:T(8,128)(2,1)S(1)} %slice_bitcast_fusion.3), channel_id=1, source_target_pairs={{0,2},{1,3},{2,4},{3,5},{4,6},{5,7},{6,0},{7,1},{8,10},{9,11},{10,... | collective-permute-start | bytes 294920 | tf_op jit(solution)/shard_map/ppermute | solution.py:424
  114.1 0.6 copy-start.9
  119.6 0.6 copy-start.8
  (2 other events, 1.3 us)
Sparse Core Ops, SparseCore 0:
  19.3 52.9 all-gather.1

commit v3 on v2

--- a/solution.py
+++ b/solution.py
@@ -351,7 +351,7 @@
             pltpu.VMEM((cols // LEN, 2 * count * THIRDS, LEN), F32),
             pltpu.VMEM((2 * count * THIRDS + 16, 2 * cols), BF16),
         ],
-        compiler_params=pltpu.CompilerParams(vmem_limit_bytes=56 << 20),
+        compiler_params=pltpu.CompilerParams(vmem_limit_bytes=40 << 20),
         cost_estimate=pl.CostEstimate(
             flops=2 * 4 * count * THIRDS * cols * length, bytes_accessed=4 << 20, transcendentals=0
         ),
@@ -359,8 +359,8 @@
     )(slot, columns, panel, waves, jnp.asarray(table))
 
 
-def project_kernel(sizes, seat_ref, *refs):
-    pieces, (both_ref, prev_ref, out_ref, acc_ref) = refs[: len(sizes)], refs[len(sizes) :]
+def project_kernel(seat_ref, *refs):
+    pieces, (both_ref, prev_ref, out_ref, acc_ref) = refs[:-4], refs[-4:]
     step = pl.program_id(0)
 
     @pl.when(step == 0)
@@ -372,41 +372,41 @@
 
     @pl.when(step == pl.num_programs(0) - 1)
     def _():
-        half = acc_ref.shape[1] // 2
+        total = acc_ref[...]
+        half = total.shape[1] // 2
+        pairs = total.shape[0] // 16
+        odd = seat_ref[pairs] == 1
         out_ref[...] = prev_ref[...]
-        blocks = []
-        for piece in range(acc_ref.shape[0] // 8):
-            real = acc_ref[8 * piece : 8 * piece + 4]
-            imag = acc_ref[8 * piece + 4 : 8 * piece + 8]
-            blocks.append((real[:, :half] + imag[:, half:], imag[:, :half] - real[:, half:]))
-        for pair in range(len(blocks) // 2):
-            odd = seat_ref[8] == 1
+        for pair in range(pairs):
+            mine = []
+            for piece in (2 * pair, 2 * pair + 1):
+                real = total[8 * piece : 8 * piece + 4]
+                imag = total[8 * piece + 4 : 8 * piece + 8]
+                mine.append((real[:, :half] + imag[:, half:], imag[:, :half] - real[:, half:]))
             for part in range(2):
-                one, two = blocks[2 * pair][part], blocks[2 * pair + 1][part]
-                tile = jnp.concatenate([jnp.where(odd, two, one), jnp.where(odd, one, two)], axis=0)
-                seat = seat_ref[pair] + part * (len(blocks) // 2)
-                out_ref[seat] = out_ref[seat] + tile
-
-
-def project(pieces, both, prev, seats, start, chunk):
+                one, two = mine[0][part], mine[1][part]
+                if pair < pairs // 2:
+                    one, two = jnp.where(odd, two, one), jnp.where(odd, one, two)
+                seat = seat_ref[pair] + part * (pairs // 2)
+                out_ref[seat] = out_ref[seat] + jnp.concatenate([one, two], axis=0)
+
+
+def project(pieces, coeffs, both, prev, seats, start, chunk):
     length = pieces[0].shape[-1]
-    sizes = [math.prod(piece.shape[:-1]) for piece in pieces]
+    rows = sum(math.prod(piece.shape[:-1]) for piece in pieces) + coeffs.shape[0]
     skip = start // chunk
     block = lambda piece: pl.BlockSpec(
         piece.shape[:-1] + (chunk,), lambda i, *_, n=piece.ndim: (0,) * (n - 1) + (i,)
     )
+    later = lambda wide: pl.BlockSpec((wide.shape[0], chunk), lambda i, *_: (0, i + skip))
     return pl.pallas_call(
-        functools.partial(project_kernel, sizes),
+        project_kernel,
         grid_spec=pltpu.PrefetchScalarGridSpec(
             num_scalar_prefetch=1,
             grid=(length // chunk,),
-            in_specs=[block(piece) for piece in pieces]
-            + [
-                pl.BlockSpec((both.shape[0], chunk), lambda i, *_: (0, i + skip)),
-                whole(*prev.shape),
-            ],
+            in_specs=[block(piece) for piece in pieces] + [later(coeffs), later(both), whole(*prev.shape)],
             out_specs=whole(*prev.shape),
-            scratch_shapes=[pltpu.VMEM((sum(sizes), both.shape[0]), F32)],
+            scratch_shapes=[pltpu.VMEM((rows, both.shape[0]), F32)],
         ),
         out_shape=jax.ShapeDtypeStruct(prev.shape, F32),
         compiler_params=pltpu.CompilerParams(vmem_limit_bytes=56 << 20),
@@ -416,7 +416,7 @@
             transcendentals=0,
         ),
         name="project",
-    )(seats, *pieces, both, prev)
+    )(seats, *pieces, coeffs, both, prev)
 
 
 def moved(x, axis, target):
@@ -424,12 +424,13 @@
     return lax.ppermute(x, axis, [(i, target(i) % size) for i in range(size)])
 
 
-def share(x):
+def share(x, terms):
     pair = jnp.stack([x, moved(x, "band", lambda i: i ^ 1)])
     below = moved(pair, "band", lambda i: i + 2)
     above = moved(pair, "band", lambda i: i - 2)
-    far = [moved(below[0], "band", lambda i: i + 2), moved(above[1], "band", lambda i: i - 2)]
-    return [pair, below, above] + far
+    first, second, terms = lax.optimization_barrier((below[0], above[1], terms))
+    far = [moved(first, "band", lambda i: i + 2), moved(second, "band", lambda i: i - 2)]
+    return [pair, below, above] + far, terms
 
 
 def per_device(slab, panel, potential, pw_slot, columns):
@@ -450,18 +451,20 @@
     row, odd = me // 2, me % 2
     terms = jnp.zeros((parts, bands // parts, bands), F32)
     pick = lambda *seats: jnp.stack([jnp.asarray(seat, jnp.int32) for seat in seats])
-    seats = pick(8, 9, 10, 11, 0, 0, 0, 0, 0)
-    terms = project([coeffs], both, terms, seats, 0, 3072)
-    seats = pick(row, (row + 3) % 4, (row + 1) % 4, (row + 2) % 4, 0, 0, 0, 0, odd)
+    seats = pick(row, (row + 3) % 4, (row + 1) % 4, (row + 2) % 4, 8, 9, 10, 11, odd)
     step = length // PIECES
+    applied = [
+        collect(panel, slot, columns, waves, piece * step, step, min(3072, step)) for piece in range(PIECES)
+    ]
     for piece in range(PIECES):
-        applied = collect(panel, slot, columns, waves, piece * step, step, min(3072, step))
-        terms = project(share(applied), both, terms, seats, piece * step, min(3072, step))
+        shared, terms = share(applied[piece], terms)
+        terms = project(shared, coeffs, both, terms, seats, piece * step, min(CHUNK, step))
     terms = lax.all_to_all(terms, "pw", split_axis=0, concat_axis=0, tiled=True)
     return jnp.sum(terms, axis=0).T
 
 
 PIECES = 2
+CHUNK = 3072
 
 
 def solution(mesh):

time: 147 us -> 141 us (0.959)
  Pallas kernels: 62.3 us -> 53 us
  waiting for transfers between devices: 12.4 us -> 18.1 us
  local copies, waits for them, and re-layouts: 14.9 us -> 12.9 us
    pallas_call x3 -> x2, Pallas kernels: 14.7 us -> 8.9 us  [project(): pl.pallas_call(project_kernel, grid_spec=pltpu.PrefetchScalarGridSpec(num...]
    ppermute x10, waiting for transfers between devices: 1.6 us -> 7.35 us  [moved(): return lax.ppermute(x, axis, [(i, target(i) % size) for i in range(size)])]
    pallas_call x2, Pallas kernels: 14.7 us -> 11.2 us  [collect(): pl.pallas_call(collect_kernel, grid=(length // chunk,), in_specs=[pl.Bloc...]
    unnamed x26 -> x30, local copies, waits for them, and re-layouts: 4.24 us -> 2.18 us
  transfers between devices with their start and end apart: 13 -> 13, of which waited for: 3 -> 7; matrix products, arithmetic and copies ran while one was open for 8% -> 7% of each run, Pallas kernels for 26% -> 19%
where the time goes in v3:
time: 141 us; the launch traced here: 140 us
  Pallas kernels  53 us (38%)
  starting transfers between devices  28 us (20%)
  waiting for transfers between devices  18.1 us (13%)
  blocking collectives  13.8 us (10%)
  between operations  13.5 us (10%)
  local copies, waits for them, and re-layouts  12.9 us (9%)
    pallas_call x1, Pallas kernels, on_grid(): pl.pallas_call(grid_kernel, in_specs=[whole(*waves.shape), whole(*potenti...  20.4 us
    ppermute x10, starting transfers between devices, moved(): return lax.ppermute(x, axis, [(i, target(i) % size) for i in range(size)])  15.2 us
    all_to_all x1, blocking collectives, per_device(): terms = lax.all_to_all(terms, 'pw', split_axis=0, concat_axis=0, tiled=True)  13.8 us
    all_to_all x2, starting transfers between devices, per_device(): waves = lax.all_to_all(waves, 'pw', split_axis=0, concat_axis=0, tiled=True)  12.8 us
    pallas_call x1, Pallas kernels, spread(): pl.pallas_call(spread_kernel, grid=(waves // chunk,), in_specs=[pl.BlockS...  12.6 us
    pallas_call x2, Pallas kernels, collect(): pl.pallas_call(collect_kernel, grid=(length // chunk,), in_specs=[pl.Bloc...  11.2 us
    all_to_all x2, waiting for transfers between devices, per_device(): waves = lax.all_to_all(waves, 'pw', split_axis=0, concat_axis=0, tiled=True)  10.8 us
    transpose x1, local copies, waits for them, and re-layouts, per_device(): both = jnp.transpose(slab, (1, 0, 2)).reshape(2 * bands, length)  9.37 us
  transfers between devices with their start and end apart: 13, of which 7 were waited for; matrix products, arithmetic and copies ran while one was open for 7% of the time, Pallas kernels for 19%

profile of v3, /device:TPU:1, one launch (start us, length us, event | category | flops | bytes accessed | tf_op | source)
XLA Modules:
  0.0 140.1 jit_solution(11110451512696220752)
XLA Ops:
  6.5 12.6 %spread.1 = (bf16[16,72,256]{2,1,0:T(8,128)(2,1)}, bf16[8,12288]{1,0:T(8,128)(2,1)}) custom-call(s32[1,12288]{1,0:T(1,128)} %bitcast.24, s32[1,256]{1,0:T(1,128)} %bitcast.27, f32[4,2,12288]{2,1,0:T(2,128)} %panel_ref.5, bf16[512,176]{1,0:T(8,128)(2,1)} %constant.71.clone.table_ref), custom_call_target="tpu_custom_call" | custom-call | flops 8858370048 | bytes 4194304 | tf_op jit(solution)/shard_map/spread/pallas_call | solution.py:142
  19.1 7.8 %all-to-all-start = ((bf16[16,72,256]{2,1,0:T(8,128)(2,1)}), bf16[16,72,256]{2,1,0:T(8,128)(2,1)S(1)}, u32[]{:S(2)}, u32[]{:S(2)}) async-start(bf16[16,72,256]{2,1,0:T(8,128)(2,1)} %get-tuple-element.17), calls=%async_computation | async-start | bytes 1179648 | tf_op jit(solution)/shard_map/all_to_all | solution.py:443
  26.9 9.4 %copy.12 = bf16[2,128,12288]{2,1,0:T(8,128)(2,1)} copy(bf16[2,128,12288]{2,0,1:T(2,128)(2,1)} %bitcast.32) | data formatting | bytes 12582912 | tf_op jit(solution)/shard_map/transpose | solution.py:445
  36.3 1.6 %all-to-all-done.in_ref = bf16[16,72,256]{2,1,0:T(8,128)(2,1)S(1)} async-done(((bf16[16,72,256]{2,1,0:T(8,128)(2,1)}), bf16[16,72,256]{2,1,0:T(8,128)(2,1)S(1)}, u32[]{:S(2)}, u32[]{:S(2)}) %all-to-all-start) | async-done | bytes 589856 | tf_op jit(solution)/shard_map/all_to_all | solution.py:443
  37.9 0.9 copy-done.6
  38.7 20.4 %on_grid.1 = bf16[16,64,256]{2,1,0:T(8,128)(2,1)} custom-call(bf16[16,72,256]{2,1,0:T(8,128)(2,1)} %copy-done.6, f32[8,128,128]{2,1,0:T(8,128)} %pot_ref.1, bf16[256,512]{1,0:T(8,128)(2,1)} %constant.72.clone.ti_ref, bf16[512,192]{1,0:T(8,128)(2,1)} %constant.73.clone.oi_ref, bf16[384,256]{1,0:T(8,128)(2,1)} %constant.74.clone.oo_ref, ...), custom_call_target="tpu_custom_call" | custom-call | flops 10737418240 | bytes 4194304 | tf_op jit(solution)/shard_map/on_grid/pallas_call | solution.py:262
  59.1 5.0 %all-to-all-start.1 = ((bf16[16,64,256]{2,1,0:T(8,128)(2,1)}), bf16[16,64,256]{2,1,0:T(8,128)(2,1)S(1)}, u32[]{:S(2)}, u32[]{:S(2)}) async-start(bf16[16,64,256]{2,1,0:T(8,128)(2,1)} %on_grid.1), calls=%async_computation.1 | async-start | bytes 1048576 | tf_op jit(solution)/shard_map/all_to_all | solution.py:448
  64.8 9.2 %all-to-all-done.1.in_ref = bf16[16,64,256]{2,1,0:T(8,128)(2,1)S(1)} async-done(((bf16[16,64,256]{2,1,0:T(8,128)(2,1)}), bf16[16,64,256]{2,1,0:T(8,128)(2,1)S(1)}, u32[]{:S(2)}, u32[]{:S(2)}) %all-to-all-start.1) | async-done | bytes 524320 | tf_op jit(solution)/shard_map/all_to_all | solution.py:448
  74.0 5.6 %collect.3 = bf16[8,6144]{1,0:T(8,128)(2,1)S(1)} custom-call(s32[1,12288]{1,0:T(1,128)S(1)} %bitcast.25, s32[1,256]{1,0:T(1,128)S(1)} %bitcast.28, f32[4,2,12288]{2,1,0:T(2,128)S(1)} %copy-done, bf16[16,64,256]{2,1,0:T(8,128)(2,1)S(1)} %all-to-all-done.1.in_ref, bf16[352,256]{1,0:T(8,128)(2,1)S(1)} %copy-done.3), custom_call_target="tpu_custom_call" | custom-call | flops 4429185024 | bytes 4194304 | tf_op jit(solution)/shard_map/collect/pallas_call | solution.py:338
  79.6 2.5 %collective-permute-start.3 = (bf16[8,6144]{1,0:T(8,128)(2,1)S(1)}, bf16[8,6144]{1,0:T(8,128)(2,1)S(1)}, u32[]{:S(2)}, u32[]{:S(2)}) collective-permute-start(bf16[8,6144]{1,0:T(8,128)(2,1)S(1)} %collect.3), channel_id=1, source_target_pairs={{0,1},{1,0},{2,3},{3,2},{4,5},{5,4},{6,7},{7,6},{8,9},{9,8},{10,11... | collective-permute-start | bytes 294920 | tf_op jit(solution)/shard_map/ppermute | solution.py:424
  82.2 5.6 %collect.2 = bf16[8,6144]{1,0:T(8,128)(2,1)S(1)} custom-call(s32[1,12288]{1,0:T(1,128)S(1)} %bitcast.26, s32[1,256]{1,0:T(1,128)S(1)} %bitcast.29, f32[4,2,12288]{2,1,0:T(2,128)S(1)} %copy-done, bf16[16,64,256]{2,1,0:T(8,128)(2,1)S(1)} %all-to-all-done.1.in_ref, bf16[352,256]{1,0:T(8,128)(2,1)S(1)} %copy-done.3), custom_call_target="tpu_custom_call" | custom-call | flops 4429185024 | bytes 4194304 | tf_op jit(solution)/shard_map/collect/pallas_call | solution.py:338
  88.4 3.1 %collective-permute-start.5 = (bf16[2,8,6144]{2,1,0:T(8,128)(2,1)S(1)}, bf16[2,8,6144]{2,1,0:T(8,128)(2,1)S(1)}, u32[]{:S(2)}, u32[]{:S(2)}) collective-permute-start(bf16[2,8,6144]{2,1,0:T(8,128)(2,1)S(1)} %pad_maximum_fusion.1.refs_0_), channel_id=1, source_target_pairs={{0,6},{1,7},{2,0},{3,1},{4,2},{5,3},{6,4},{7,5},{8,14},{9,15},{10,... | collective-permute-start | bytes 589832 | tf_op jit(solution)/shard_map/ppermute | solution.py:424
  91.4 1.4 collective-permute-done
  92.8 3.1 %collective-permute-start.2 = (bf16[2,8,6144]{2,1,0:T(8,128)(2,1)S(1)}, bf16[2,8,6144]{2,1,0:T(8,128)(2,1)S(1)}, u32[]{:S(2)}, u32[]{:S(2)}) collective-permute-start(bf16[2,8,6144]{2,1,0:T(8,128)(2,1)S(1)} %pad_maximum_fusion.refs_0_), channel_id=1, source_target_pairs={{0,6},{1,7},{2,0},{3,1},{4,2},{5,3},{6,4},{7,5},{8,14},{9,15},{10,... | collective-permute-start | bytes 589832 | tf_op jit(solution)/shard_map/ppermute | solution.py:424
  95.9 1.2 collective-permute-done.4.refs_1_
  97.2 2.7 %collective-permute-start.7 = (bf16[8,6144]{1,0:T(8,128)(2,1)S(1)}, bf16[8,6144]{1,0:T(8,128)(2,1)S(1)}, u32[]{:S(2)}, u32[]{:S(2)}) collective-permute-start(bf16[8,6144]{1,0:T(8,128)(2,1)S(1)} %slice_bitcast_fusion), channel_id=1, source_target_pairs={{0,6},{1,7},{2,0},{3,1},{4,2},{5,3},{6,4},{7,5},{8,14},{9,15},{10,... | collective-permute-start | bytes 294920 | tf_op jit(solution)/shard_map/ppermute | solution.py:424
  99.9 1.8 %collective-permute-done.1.refs_1_ = bf16[2,8,6144]{2,1,0:T(8,128)(2,1)S(1)} collective-permute-done((bf16[2,8,6144]{2,1,0:T(8,128)(2,1)S(1)}, bf16[2,8,6144]{2,1,0:T(8,128)(2,1)S(1)}, u32[]{:S(2)}, u32[]{:S(2)}) %collective-permute-start.1) | collective-permute-done | bytes 196640 | tf_op jit(solution)/shard_map/ppermute | solution.py:424
  101.7 1.0 collective-permute-done.6.refs_3_
  102.8 0.7 broadcast_in_dim.3.refs_7_
  103.5 4.4 %project.2.refs_7_ = f32[16,8,128]{2,1,0:T(8,128)} custom-call(s32[9]{0:T(128)} %stack.41.seat_ref, bf16[2,8,6144]{2,1,0:T(8,128)(2,1)} %copy-done.5, bf16[2,8,6144]{2,1,0:T(8,128)(2,1)} %copy-done.10, bf16[2,8,6144]{2,1,0:T(8,128)(2,1)} %copy-done.9, bf16[8,6144]{1,0:T(8,128)(2,1)} %copy-done.11, bf16[8,6144]{1,0:T(8,128)(2,1)} %copy-done.12, ...), custom_call_target="tpu_custom_call" | custom-call | flops 805306368 | bytes 3145728 | tf_op jit(solution)/shard_map/project/pallas_call | solution.py:402
  108.0 3.1 %collective-permute-start.9 = (bf16[8,6144]{1,0:T(8,128)(2,1)S(1)}, bf16[8,6144]{1,0:T(8,128)(2,1)S(1)}, u32[]{:S(2)}, u32[]{:S(2)}) collective-permute-start(bf16[8,6144]{1,0:T(8,128)(2,1)S(1)} %slice_bitcast_fusion.2), channel_id=1, source_target_pairs={{0,6},{1,7},{2,0},{3,1},{4,2},{5,3},{6,4},{7,5},{8,14},{9,15},{10,... | collective-permute-start | bytes 294920 | tf_op jit(solution)/shard_map/ppermute | solution.py:424
  111.1 1.9 %collective-permute-done.8.refs_3_ = bf16[8,6144]{1,0:T(8,128)(2,1)S(1)} collective-permute-done((bf16[8,6144]{1,0:T(8,128)(2,1)S(1)}, bf16[8,6144]{1,0:T(8,128)(2,1)S(1)}, u32[]{:S(2)}, u32[]{:S(2)}) %collective-permute-start.8) | collective-permute-done | bytes 98336 | tf_op jit(solution)/shard_map/ppermute | solution.py:424
  114.3 4.5 %project.3 = f32[16,8,128]{2,1,0:T(8,128)} custom-call(s32[9]{0:T(128)} %stack.41.seat_ref, bf16[2,8,6144]{2,1,0:T(8,128)(2,1)} %copy-done.4, bf16[2,8,6144]{2,1,0:T(8,128)(2,1)} %copy-done.8, bf16[2,8,6144]{2,1,0:T(8,128)(2,1)} %copy-done.7, bf16[8,6144]{1,0:T(8,128)(2,1)} %copy-done.13, bf16[8,6144]{1,0:T(8,128)(2,1)} %copy-done.14, ...), custom_call_target="tpu_custom_call" | custom-call | flops 805306368 | bytes 3145728 | tf_op jit(solution)/shard_map/project/pallas_call | solution.py:402
  118.8 13.8 %all_to_all.15 = f32[16,8,128]{2,1,0:T(8,128)S(1)} all-to-all(f32[16,8,128]{2,1,0:T(8,128)} %project.3), channel_id=1, replica_groups=mesh['pw'=16,'band'=8] {'pw'}, dimensions={0} | all-to-all | bytes 131072 | tf_op jit(solution)/shard_map/all_to_all | solution.py:462
  (50 shorter events, 3.5 us)
Async XLA Ops:
  6.5 67.5 %all-gather.2.cloned.1.call-start = ((), (), s32[]{:S(2)}) async-start(), calls=%async_computation.3 | async-start | bytes 1769472 | tf_op jit(solution)/shard_map/all_gather | solution.py:444
  19.1 18.7 %all-to-all-start = ((bf16[16,72,256]{2,1,0:T(8,128)(2,1)}), bf16[16,72,256]{2,1,0:T(8,128)(2,1)S(1)}, u32[]{:S(2)}, u32[]{:S(2)}) async-start(bf16[16,72,256]{2,1,0:T(8,128)(2,1)} %get-tuple-element.17), calls=%async_computation | async-start | bytes 1179648 | tf_op jit(solution)/shard_map/all_to_all | solution.py:443
  37.9 0.9 copy-start.6
  38.7 35.3 %copy-start = (f32[4,2,12288]{2,1,0:T(2,128)S(1)}, f32[4,2,12288]{2,1,0:T(2,128)}, u32[]{:S(2)}) copy-start(f32[4,2,12288]{2,1,0:T(2,128)} %panel_ref.5) | copy-start | bytes 1179652
  38.7 35.3 %copy-start.1 = (s32[12288]{0:T(1024)S(1)}, s32[12288]{0:T(1024)}, u32[]{:S(2)}) copy-start(s32[12288]{0:T(1024)} %param.14) | copy-start | bytes 147460
  38.7 35.3 %copy-start.2 = (s32[256]{0:T(256)S(1)}, s32[256]{0:T(256)}, u32[]{:S(2)}) copy-start(s32[256]{0:T(256)} %param.15) | copy-start | bytes 3076
  38.7 35.3 %copy-start.3 = (bf16[352,256]{1,0:T(8,128)(2,1)S(1)}, bf16[352,256]{1,0:T(8,128)(2,1)}, u32[]{:S(2)}) copy-start(bf16[352,256]{1,0:T(8,128)(2,1)} %constant.76.clone.table_ref) | copy-start | bytes 540676
  59.1 14.9 %all-to-all-start.1 = ((bf16[16,64,256]{2,1,0:T(8,128)(2,1)}), bf16[16,64,256]{2,1,0:T(8,128)(2,1)S(1)}, u32[]{:S(2)}, u32[]{:S(2)}) async-start(bf16[16,64,256]{2,1,0:T(8,128)(2,1)} %on_grid.1), calls=%async_computation.1 | async-start | bytes 1048576 | tf_op jit(solution)/shard_map/all_to_all | solution.py:448
  79.6 8.7 %collective-permute-start.3 = (bf16[8,6144]{1,0:T(8,128)(2,1)S(1)}, bf16[8,6144]{1,0:T(8,128)(2,1)S(1)}, u32[]{:S(2)}, u32[]{:S(2)}) collective-permute-start(bf16[8,6144]{1,0:T(8,128)(2,1)S(1)} %collect.3), channel_id=1, source_target_pairs={{0,1},{1,0},{2,3},{3,2},{4,5},{5,4},{6,7},{7,6},{8,9},{9,8},{10,11... | collective-permute-start | bytes 294920 | tf_op jit(solution)/shard_map/ppermute | solution.py:424
  87.7 5.1 %collective-permute-start = (bf16[8,6144]{1,0:T(8,128)(2,1)S(1)}, bf16[8,6144]{1,0:T(8,128)(2,1)S(1)}, u32[]{:S(2)}, u32[]{:S(2)}) collective-permute-start(bf16[8,6144]{1,0:T(8,128)(2,1)S(1)} %collect.2), channel_id=1, source_target_pairs={{0,1},{1,0},{2,3},{3,2},{4,5},{5,4},{6,7},{7,6},{8,9},{9,8},{10,11... | collective-permute-start | bytes 294920 | tf_op jit(solution)/shard_map/ppermute | solution.py:424
  88.3 15.1 %copy-start.5 = (bf16[2,8,6144]{2,1,0:T(8,128)(2,1)}, bf16[2,8,6144]{2,1,0:T(8,128)(2,1)S(1)}, u32[]{:S(2)}) copy-start(bf16[2,8,6144]{2,1,0:T(8,128)(2,1)S(1)} %pad_maximum_fusion.1.refs_0_) | copy-start | bytes 589828
  88.4 7.6 %collective-permute-start.5 = (bf16[2,8,6144]{2,1,0:T(8,128)(2,1)S(1)}, bf16[2,8,6144]{2,1,0:T(8,128)(2,1)S(1)}, u32[]{:S(2)}, u32[]{:S(2)}) collective-permute-start(bf16[2,8,6144]{2,1,0:T(8,128)(2,1)S(1)} %pad_maximum_fusion.1.refs_0_), channel_id=1, source_target_pairs={{0,6},{1,7},{2,0},{3,1},{4,2},{5,3},{6,4},{7,5},{8,14},{9,15},{10,... | collective-permute-start | bytes 589832 | tf_op jit(solution)/shard_map/ppermute | solution.py:424
  91.4 5.7 %collective-permute-start.4 = (bf16[2,8,6144]{2,1,0:T(8,128)(2,1)S(1)}, bf16[2,8,6144]{2,1,0:T(8,128)(2,1)S(1)}, u32[]{:S(2)}, u32[]{:S(2)}) collective-permute-start(bf16[2,8,6144]{2,1,0:T(8,128)(2,1)S(1)} %pad_maximum_fusion.1.refs_0_), channel_id=1, source_target_pairs={{0,2},{1,3},{2,4},{3,5},{4,6},{5,7},{6,0},{7,1},{8,10},{9,11},{10,... | collective-permute-start | bytes 589832 | tf_op jit(solution)/shard_map/ppermute | solution.py:424
  92.8 20.2 %copy-start.4 = (bf16[2,8,6144]{2,1,0:T(8,128)(2,1)}, bf16[2,8,6144]{2,1,0:T(8,128)(2,1)S(1)}, u32[]{:S(2)}) copy-start(bf16[2,8,6144]{2,1,0:T(8,128)(2,1)S(1)} %pad_maximum_fusion.refs_0_) | copy-start | bytes 589828
  92.8 7.1 %collective-permute-start.2 = (bf16[2,8,6144]{2,1,0:T(8,128)(2,1)S(1)}, bf16[2,8,6144]{2,1,0:T(8,128)(2,1)S(1)}, u32[]{:S(2)}, u32[]{:S(2)}) collective-permute-start(bf16[2,8,6144]{2,1,0:T(8,128)(2,1)S(1)} %pad_maximum_fusion.refs_0_), channel_id=1, source_target_pairs={{0,6},{1,7},{2,0},{3,1},{4,2},{5,3},{6,4},{7,5},{8,14},{9,15},{10,... | collective-permute-start | bytes 589832 | tf_op jit(solution)/shard_map/ppermute | solution.py:424
  95.9 5.8 %collective-permute-start.1 = (bf16[2,8,6144]{2,1,0:T(8,128)(2,1)S(1)}, bf16[2,8,6144]{2,1,0:T(8,128)(2,1)S(1)}, u32[]{:S(2)}, u32[]{:S(2)}) collective-permute-start(bf16[2,8,6144]{2,1,0:T(8,128)(2,1)S(1)} %pad_maximum_fusion.refs_0_), channel_id=1, source_target_pairs={{0,2},{1,3},{2,4},{3,5},{4,6},{5,7},{6,0},{7,1},{8,10},{9,11},{10,... | collective-permute-start | bytes 589832 | tf_op jit(solution)/shard_map/ppermute | solution.py:424
  95.9 7.5 %copy-start.9 = (bf16[2,8,6144]{2,1,0:T(8,128)(2,1)}, bf16[2,8,6144]{2,1,0:T(8,128)(2,1)S(1)}, u32[]{:S(2)}) copy-start(bf16[2,8,6144]{2,1,0:T(8,128)(2,1)S(1)} %collective-permute-done.5.refs_2_) | copy-start | bytes 589828
  97.1 6.3 %copy-start.10 = (bf16[2,8,6144]{2,1,0:T(8,128)(2,1)}, bf16[2,8,6144]{2,1,0:T(8,128)(2,1)S(1)}, u32[]{:S(2)}) copy-start(bf16[2,8,6144]{2,1,0:T(8,128)(2,1)S(1)} %collective-permute-done.4.refs_1_) | copy-start | bytes 589828
  97.2 5.6 %collective-permute-start.6 = (bf16[8,6144]{1,0:T(8,128)(2,1)S(1)}, bf16[8,6144]{1,0:T(8,128)(2,1)S(1)}, u32[]{:S(2)}, u32[]{:S(2)}) collective-permute-start(bf16[8,6144]{1,0:T(8,128)(2,1)S(1)} %slice_bitcast_fusion.1), channel_id=1, source_target_pairs={{0,2},{1,3},{2,4},{3,5},{4,6},{5,7},{6,0},{7,1},{8,10},{9,11},{10,... | collective-permute-start | bytes 294920 | tf_op jit(solution)/shard_map/ppermute | solution.py:424
  97.2 5.5 %collective-permute-start.7 = (bf16[8,6144]{1,0:T(8,128)(2,1)S(1)}, bf16[8,6144]{1,0:T(8,128)(2,1)S(1)}, u32[]{:S(2)}, u32[]{:S(2)}) collective-permute-start(bf16[8,6144]{1,0:T(8,128)(2,1)S(1)} %slice_bitcast_fusion), channel_id=1, source_target_pairs={{0,6},{1,7},{2,0},{3,1},{4,2},{5,3},{6,4},{7,5},{8,14},{9,15},{10,... | collective-permute-start | bytes 294920 | tf_op jit(solution)/shard_map/ppermute | solution.py:424
  99.9 13.2 %copy-start.7 = (bf16[2,8,6144]{2,1,0:T(8,128)(2,1)}, bf16[2,8,6144]{2,1,0:T(8,128)(2,1)S(1)}, u32[]{:S(2)}) copy-start(bf16[2,8,6144]{2,1,0:T(8,128)(2,1)S(1)} %collective-permute-done.2.refs_2_) | copy-start | bytes 589828
  101.7 11.4 %copy-start.8 = (bf16[2,8,6144]{2,1,0:T(8,128)(2,1)}, bf16[2,8,6144]{2,1,0:T(8,128)(2,1)S(1)}, u32[]{:S(2)}) copy-start(bf16[2,8,6144]{2,1,0:T(8,128)(2,1)S(1)} %collective-permute-done.1.refs_1_) | copy-start | bytes 589828
  107.9 5.1 %collective-permute-start.8 = (bf16[8,6144]{1,0:T(8,128)(2,1)S(1)}, bf16[8,6144]{1,0:T(8,128)(2,1)S(1)}, u32[]{:S(2)}, u32[]{:S(2)}) collective-permute-start(bf16[8,6144]{1,0:T(8,128)(2,1)S(1)} %slice_bitcast_fusion.3), channel_id=1, source_target_pairs={{0,2},{1,3},{2,4},{3,5},{4,6},{5,7},{6,0},{7,1},{8,10},{9,11},{10,... | collective-permute-start | bytes 294920 | tf_op jit(solution)/shard_map/ppermute | solution.py:424
  108.0 5.0 %collective-permute-start.9 = (bf16[8,6144]{1,0:T(8,128)(2,1)S(1)}, bf16[8,6144]{1,0:T(8,128)(2,1)S(1)}, u32[]{:S(2)}, u32[]{:S(2)}) collective-permute-start(bf16[8,6144]{1,0:T(8,128)(2,1)S(1)} %slice_bitcast_fusion.2), channel_id=1, source_target_pairs={{0,6},{1,7},{2,0},{3,1},{4,2},{5,3},{6,4},{7,5},{8,14},{9,15},{10,... | collective-permute-start | bytes 294920 | tf_op jit(solution)/shard_map/ppermute | solution.py:424
  (4 other events, 2.7 us)
Sparse Core Ops, SparseCore 0:
  19.3 53.0 all-gather.1

commit v4 on v2

--- a/solution.py
+++ b/solution.py
@@ -351,7 +351,7 @@
             pltpu.VMEM((cols // LEN, 2 * count * THIRDS, LEN), F32),
             pltpu.VMEM((2 * count * THIRDS + 16, 2 * cols), BF16),
         ],
-        compiler_params=pltpu.CompilerParams(vmem_limit_bytes=56 << 20),
+        compiler_params=pltpu.CompilerParams(vmem_limit_bytes=40 << 20),
         cost_estimate=pl.CostEstimate(
             flops=2 * 4 * count * THIRDS * cols * length, bytes_accessed=4 << 20, transcendentals=0
         ),
@@ -409,7 +409,7 @@
             scratch_shapes=[pltpu.VMEM((sum(sizes), both.shape[0]), F32)],
         ),
         out_shape=jax.ShapeDtypeStruct(prev.shape, F32),
-        compiler_params=pltpu.CompilerParams(vmem_limit_bytes=56 << 20),
+        compiler_params=pltpu.CompilerParams(vmem_limit_bytes=32 << 20),
         cost_estimate=pl.CostEstimate(
             flops=2 * 256 * both.shape[0] * length,
             bytes_accessed=2 * both.shape[0] * length,
@@ -424,12 +424,13 @@
     return lax.ppermute(x, axis, [(i, target(i) % size) for i in range(size)])
 
 
-def share(x):
+def share(x, meanwhile):
     pair = jnp.stack([x, moved(x, "band", lambda i: i ^ 1)])
+    pair, meanwhile = lax.optimization_barrier((pair, meanwhile))
     below = moved(pair, "band", lambda i: i + 2)
     above = moved(pair, "band", lambda i: i - 2)
     far = [moved(below[0], "band", lambda i: i + 2), moved(above[1], "band", lambda i: i - 2)]
-    return [pair, below, above] + far
+    return [pair, below, above] + far, meanwhile
 
 
 def per_device(slab, panel, potential, pw_slot, columns):
@@ -450,18 +451,14 @@
     row, odd = me // 2, me % 2
     terms = jnp.zeros((parts, bands // parts, bands), F32)
     pick = lambda *seats: jnp.stack([jnp.asarray(seat, jnp.int32) for seat in seats])
+    applied = collect(panel, slot, columns, waves, 0, length, 3072)
     seats = pick(8, 9, 10, 11, 0, 0, 0, 0, 0)
     terms = project([coeffs], both, terms, seats, 0, 3072)
+    shared, terms = share(applied, terms)
     seats = pick(row, (row + 3) % 4, (row + 1) % 4, (row + 2) % 4, 0, 0, 0, 0, odd)
-    step = length // PIECES
-    for piece in range(PIECES):
-        applied = collect(panel, slot, columns, waves, piece * step, step, min(3072, step))
-        terms = project(share(applied), both, terms, seats, piece * step, min(3072, step))
+    terms = project(shared, both, terms, seats, 0, 3072)
     terms = lax.all_to_all(terms, "pw", split_axis=0, concat_axis=0, tiled=True)
     return jnp.sum(terms, axis=0).T
-
-
-PIECES = 2
 
 
 def solution(mesh):

time: 147 us -> 137 us (0.932)
  blocking collectives: 13.9 us -> 26.9 us
  Pallas kernels: 62.3 us -> 50.7 us
  starting transfers between devices: 27.7 us -> 16.3 us
    all_to_all x0 -> x1, blocking collectives: none -> 14.8 us  [per_device(): waves = lax.all_to_all(waves, 'pw', split_axis=0, concat_axis=0, tiled=True)]
    all_to_all x2 -> x1, waiting for transfers between devices: 10.8 us -> 1.53 us  [per_device(): waves = lax.all_to_all(waves, 'pw', split_axis=0, concat_axis=0, tiled=True)]
    ppermute x10 -> x5, waiting for transfers between devices: 1.6 us -> 10.8 us  [moved(): return lax.ppermute(x, axis, [(i, target(i) % size) for i in range(size)])]
    pallas_call x3 -> x2, Pallas kernels: 14.7 us -> 7.1 us  [project(): pl.pallas_call(functools.partial(project_kernel, sizes), grid_spec=pltpu....]
    ppermute x10 -> x5, starting transfers between devices: 15 us -> 8.53 us  [moved(): return lax.ppermute(x, axis, [(i, target(i) % size) for i in range(size)])]
    all_to_all x2 -> x1, starting transfers between devices: 12.8 us -> 7.78 us  [per_device(): waves = lax.all_to_all(waves, 'pw', split_axis=0, concat_axis=0, tiled=True)]
    pallas_call x2 -> x1, Pallas kernels: 14.7 us -> 10.7 us  [collect(): pl.pallas_call(collect_kernel, grid=(length // chunk,), in_specs=[pl.Bloc...]
    unnamed x26 -> x18, local copies, waits for them, and re-layouts: 4.24 us -> 6.46 us
  transfers between devices with their start and end apart: 13 -> 7, of which waited for: 3 -> 3; matrix products, arithmetic and copies ran while one was open for 8% -> 7% of each run, Pallas kernels for 26% -> 18%
where the time goes in v4:
time: 137 us; the launch traced here: 136 us
  Pallas kernels  50.7 us (37%)
  blocking collectives  26.9 us (20%)
  starting transfers between devices  16.3 us (12%)
  local copies, waits for them, and re-layouts  16 us (12%)
  between operations  13.5 us (10%)
  waiting for transfers between devices  12.3 us (9%)
    pallas_call x1, Pallas kernels, on_grid(): pl.pallas_call(grid_kernel, in_specs=[whole(*waves.shape), whole(*potenti...  20.4 us
    all_to_all x1, blocking collectives, per_device(): waves = lax.all_to_all(waves, 'pw', split_axis=0, concat_axis=0, tiled=True)  14.8 us
    pallas_call x1, Pallas kernels, spread(): pl.pallas_call(spread_kernel, grid=(waves // chunk,), in_specs=[pl.BlockS...  12.5 us
    all_to_all x1, blocking collectives, per_device(): terms = lax.all_to_all(terms, 'pw', split_axis=0, concat_axis=0, tiled=True)  12.1 us
    ppermute x5, waiting for transfers between devices, moved(): return lax.ppermute(x, axis, [(i, target(i) % size) for i in range(size)])  10.8 us
    pallas_call x1, Pallas kernels, collect(): pl.pallas_call(collect_kernel, grid=(length // chunk,), in_specs=[pl.Bloc...  10.7 us
    transpose x1, local copies, waits for them, and re-layouts, per_device(): both = jnp.transpose(slab, (1, 0, 2)).reshape(2 * bands, length)  9.4 us
    ppermute x5, starting transfers between devices, moved(): return lax.ppermute(x, axis, [(i, target(i) % size) for i in range(size)])  8.53 us
  transfers between devices with their start and end apart: 7, of which 3 were waited for; matrix products, arithmetic and copies ran while one was open for 7% of the time, Pallas kernels for 18%

profile of v4, /device:TPU:1, one launch (start us, length us, event | category | flops | bytes accessed | tf_op | source)
XLA Modules:
  0.0 136.4 jit_solution(11073759853411770803)
XLA Ops:
  6.5 12.5 %spread.1 = (bf16[16,72,256]{2,1,0:T(8,128)(2,1)}, bf16[8,12288]{1,0:T(8,128)(2,1)}) custom-call(s32[1,12288]{1,0:T(1,128)} %bitcast.19, s32[1,256]{1,0:T(1,128)} %bitcast.21, f32[4,2,12288]{2,1,0:T(2,128)} %panel_ref.3, bf16[512,176]{1,0:T(8,128)(2,1)} %constant.66.clone.table_ref), custom_call_target="tpu_custom_call" | custom-call | flops 8858370048 | bytes 4194304 | tf_op jit(solution)/shard_map/spread/pallas_call | solution.py:142
  19.1 0.0 all-gather.2.cloned.1.call-update
  19.1 7.8 %all-to-all-start = ((bf16[16,72,256]{2,1,0:T(8,128)(2,1)}), bf16[16,72,256]{2,1,0:T(8,128)(2,1)S(1)}, u32[]{:S(2)}, u32[]{:S(2)}) async-start(bf16[16,72,256]{2,1,0:T(8,128)(2,1)} %get-tuple-element.13), calls=%async_computation | async-start | bytes 1179648 | tf_op jit(solution)/shard_map/all_to_all | solution.py:443
  26.9 9.4 %copy.12 = bf16[2,128,12288]{2,1,0:T(8,128)(2,1)} copy(bf16[2,128,12288]{2,0,1:T(2,128)(2,1)} %bitcast.23) | data formatting | bytes 12582912 | tf_op jit(solution)/shard_map/transpose | solution.py:445
  36.3 1.5 %all-to-all-done.in_ref = bf16[16,72,256]{2,1,0:T(8,128)(2,1)S(1)} async-done(((bf16[16,72,256]{2,1,0:T(8,128)(2,1)}), bf16[16,72,256]{2,1,0:T(8,128)(2,1)S(1)}, u32[]{:S(2)}, u32[]{:S(2)}) %all-to-all-start) | async-done | bytes 589856 | tf_op jit(solution)/shard_map/all_to_all | solution.py:443
  37.8 0.9 copy-done.8
  38.7 20.4 %on_grid.1 = bf16[16,64,256]{2,1,0:T(8,128)(2,1)} custom-call(bf16[16,72,256]{2,1,0:T(8,128)(2,1)} %copy-done.8, f32[8,128,128]{2,1,0:T(8,128)} %pot_ref.1, bf16[256,512]{1,0:T(8,128)(2,1)} %constant.67.clone.ti_ref, bf16[512,192]{1,0:T(8,128)(2,1)} %constant.68.clone.oi_ref, bf16[384,256]{1,0:T(8,128)(2,1)} %constant.69.clone.oo_ref, ...), custom_call_target="tpu_custom_call" | custom-call | flops 10737418240 | bytes 4194304 | tf_op jit(solution)/shard_map/on_grid/pallas_call | solution.py:262
  59.1 14.8 %all_to_all.15.in_ref = bf16[16,64,256]{2,1,0:T(8,128)(2,1)S(1)} all-to-all(bf16[16,64,256]{2,1,0:T(8,128)(2,1)} %on_grid.1), channel_id=1, replica_groups=mesh['pw'=16,'band'=8] {'pw'}, dimensions={0} | all-to-all | bytes 1048576 | tf_op jit(solution)/shard_map/all_to_all | solution.py:448
  74.0 10.7 %collect.1 = bf16[8,12288]{1,0:T(8,128)(2,1)S(1)} custom-call(s32[1,12288]{1,0:T(1,128)S(1)} %bitcast.20, s32[1,256]{1,0:T(1,128)S(1)} %bitcast.22, f32[4,2,12288]{2,1,0:T(2,128)S(1)} %copy-done.4, bf16[16,64,256]{2,1,0:T(8,128)(2,1)S(1)} %all_to_all.15.in_ref, bf16[352,256]{1,0:T(8,128)(2,1)S(1)} %copy-done.7), custom_call_target="tpu_custom_call" | custom-call | flops 8858370048 | bytes 4194304 | tf_op jit(solution)/shard_map/collect/pallas_call | solution.py:338
  84.7 2.5 %collective-permute-start = (bf16[8,12288]{1,0:T(8,128)(2,1)S(1)}, bf16[8,12288]{1,0:T(8,128)(2,1)S(1)}, u32[]{:S(2)}, u32[]{:S(2)}) collective-permute-start(bf16[8,12288]{1,0:T(8,128)(2,1)S(1)} %collect.1), channel_id=1, source_target_pairs={{0,1},{1,0},{2,3},{3,2},{4,5},{5,4},{6,7},{7,6},{8,9},{9,8},{10,11... | collective-permute-start | bytes 589832 | tf_op jit(solution)/shard_map/ppermute | solution.py:424
  87.2 2.8 %copy-done = bf16[2,128,12288]{2,1,0:T(8,128)(2,1)S(1)} copy-done((bf16[2,128,12288]{2,1,0:T(8,128)(2,1)S(1)}, bf16[2,128,12288]{2,1,0:T(8,128)(2,1)}, u32[]{:S(2)}) %copy-start) | copy-done | bytes 6291480
  90.0 3.6 %project.2.refs_6_ = f32[16,8,128]{2,1,0:T(8,128)S(1)} custom-call(s32[9]{0:T(128)S(1)} %copy-done.3, bf16[64,12288]{1,0:T(8,128)(2,1)S(1)} %copy-done.2, bf16[256,12288]{1,0:T(8,128)(2,1)S(1)} %bitcast.16, f32[16,8,128]{2,1,0:T(8,128)S(1)} %broadcast_in_dim.3.refs_2_), custom_call_target="tpu_custom_call" | custom-call | flops 1610612736 | bytes 6291456 | tf_op jit(solution)/shard_map/project/pallas_call | solution.py:398
  93.6 0.0 collective-permute-done
  93.6 1.5 %collective-permute-start.1 = (bf16[2,8,12288]{2,1,0:T(8,128)(2,1)S(1)}, bf16[2,8,12288]{2,1,0:T(8,128)(2,1)S(1)}, u32[]{:S(2)}, u32[]{:S(2)}) collective-permute-start(bf16[2,8,12288]{2,1,0:T(8,128)(2,1)S(1)} %pad_maximum_fusion.refs_0_), channel_id=1, source_target_pairs={{0,2},{1,3},{2,4},{3,5},{4,6},{5,7},{6,0},{7,1},{8,10},{9,11},{10,... | collective-permute-start | bytes 1179656 | tf_op jit(solution)/shard_map/ppermute | solution.py:424
  95.1 1.7 %collective-permute-start.2 = (bf16[2,8,12288]{2,1,0:T(8,128)(2,1)S(1)}, bf16[2,8,12288]{2,1,0:T(8,128)(2,1)S(1)}, u32[]{:S(2)}, u32[]{:S(2)}) collective-permute-start(bf16[2,8,12288]{2,1,0:T(8,128)(2,1)S(1)} %pad_maximum_fusion.refs_0_), channel_id=1, source_target_pairs={{0,6},{1,7},{2,0},{3,1},{4,2},{5,3},{6,4},{7,5},{8,14},{9,15},{10,... | collective-permute-start | bytes 1179656 | tf_op jit(solution)/shard_map/ppermute | solution.py:424
  96.8 7.9 %collective-permute-done.1.refs_1_ = bf16[2,8,12288]{2,1,0:T(8,128)(2,1)S(1)} collective-permute-done((bf16[2,8,12288]{2,1,0:T(8,128)(2,1)S(1)}, bf16[2,8,12288]{2,1,0:T(8,128)(2,1)S(1)}, u32[]{:S(2)}, u32[]{:S(2)}) %collective-permute-start.1) | collective-permute-done | bytes 393248 | tf_op jit(solution)/shard_map/ppermute | solution.py:424
  104.7 0.1 collective-permute-start.3
  104.9 2.7 %collective-permute-start.4 = (bf16[8,12288]{1,0:T(8,128)(2,1)S(1)}, bf16[8,12288]{1,0:T(8,128)(2,1)S(1)}, u32[]{:S(2)}, u32[]{:S(2)}) collective-permute-start(bf16[8,12288]{1,0:T(8,128)(2,1)S(1)} %slice_bitcast_fusion), channel_id=1, source_target_pairs={{0,6},{1,7},{2,0},{3,1},{4,2},{5,3},{6,4},{7,5},{8,14},{9,15},{10,... | collective-permute-start | bytes 589832 | tf_op jit(solution)/shard_map/ppermute | solution.py:424
  107.6 0.1 stack.32.seat_ref
  107.7 2.9 %collective-permute-done.3.refs_3_ = bf16[8,12288]{1,0:T(8,128)(2,1)S(1)} collective-permute-done((bf16[8,12288]{1,0:T(8,128)(2,1)S(1)}, bf16[8,12288]{1,0:T(8,128)(2,1)S(1)}, u32[]{:S(2)}, u32[]{:S(2)}) %collective-permute-start.3) | collective-permute-done | bytes 196640 | tf_op jit(solution)/shard_map/ppermute | solution.py:424
  110.5 2.8 %copy-done.1 = bf16[2,128,12288]{2,1,0:T(8,128)(2,1)S(1)} copy-done((bf16[2,128,12288]{2,1,0:T(8,128)(2,1)S(1)}, bf16[2,128,12288]{2,1,0:T(8,128)(2,1)}, u32[]{:S(2)}) %copy-start.1) | copy-done | bytes 6291480
  113.3 3.5 %project.3 = f32[16,8,128]{2,1,0:T(8,128)S(1)} custom-call(s32[9]{0:T(128)S(1)} %stack.32.seat_ref, bf16[2,8,12288]{2,1,0:T(8,128)(2,1)S(1)} %pad_maximum_fusion.refs_0_, bf16[2,8,12288]{2,1,0:T(8,128)(2,1)S(1)} %collective-permute-done.1.refs_1_, bf16[2,8,12288]{2,1,0:T(8,128)(2,1)S(1)} %collective-permute-done.2.refs_2_, ...), custom_call_target="tpu_custom_call" | custom-call | flops 1610612736 | bytes 6291456 | tf_op jit(solution)/shard_map/project/pallas_call | solution.py:398
  116.9 12.1 %all_to_all.16 = f32[16,8,128]{2,1,0:T(8,128)S(1)} all-to-all(f32[16,8,128]{2,1,0:T(8,128)S(1)} %project.3), channel_id=1, replica_groups=mesh['pw'=16,'band'=8] {'pw'}, dimensions={0} | all-to-all | bytes 131072 | tf_op jit(solution)/shard_map/all_to_all | solution.py:460
  128.9 0.6 reduce_sum.9
  (24 shorter events, 0.1 us)
Async XLA Ops:
  6.5 67.4 %all-gather.2.cloned.1.call-start = ((), (), s32[]{:S(2)}) async-start(), calls=%async_computation.3 | async-start | bytes 1769472 | tf_op jit(solution)/shard_map/all_gather | solution.py:444
  19.1 18.7 %all-to-all-start = ((bf16[16,72,256]{2,1,0:T(8,128)(2,1)}), bf16[16,72,256]{2,1,0:T(8,128)(2,1)S(1)}, u32[]{:S(2)}, u32[]{:S(2)}) async-start(bf16[16,72,256]{2,1,0:T(8,128)(2,1)} %get-tuple-element.13), calls=%async_computation | async-start | bytes 1179648 | tf_op jit(solution)/shard_map/all_to_all | solution.py:443
  37.8 0.9 copy-start.8
  38.7 35.3 %copy-start.4 = (f32[4,2,12288]{2,1,0:T(2,128)S(1)}, f32[4,2,12288]{2,1,0:T(2,128)}, u32[]{:S(2)}) copy-start(f32[4,2,12288]{2,1,0:T(2,128)} %panel_ref.3) | copy-start | bytes 1179652
  38.7 35.3 %copy-start.5 = (s32[12288]{0:T(1024)S(1)}, s32[12288]{0:T(1024)}, u32[]{:S(2)}) copy-start(s32[12288]{0:T(1024)} %param.14) | copy-start | bytes 147460
  38.7 35.3 %copy-start.6 = (s32[256]{0:T(256)S(1)}, s32[256]{0:T(256)}, u32[]{:S(2)}) copy-start(s32[256]{0:T(256)} %param.15) | copy-start | bytes 3076
  38.7 35.3 %copy-start.7 = (bf16[352,256]{1,0:T(8,128)(2,1)S(1)}, bf16[352,256]{1,0:T(8,128)(2,1)}, u32[]{:S(2)}) copy-start(bf16[352,256]{1,0:T(8,128)(2,1)} %constant.71.clone.table_ref) | copy-start | bytes 540676
  73.9 13.3 %copy-start.3 = (s32[9]{0:T(128)S(1)}, s32[9]{0:T(128)}, u32[]{:S(2)}) copy-start(s32[9]{0:T(128)} %constant.64.clone.1.seat_ref) | copy-start | bytes 112
  74.0 13.2 %copy-start.2 = (bf16[64,12288]{1,0:T(8,128)(2,1)S(1)}, bf16[64,12288]{1,0:T(8,128)(2,1)}, u32[]{:S(2)}) copy-start(bf16[64,12288]{1,0:T(8,128)(2,1)} %all-gather.2.cloned.1.call-done.refs_0_) | copy-start | bytes 4718596
  84.7 8.9 %collective-permute-start = (bf16[8,12288]{1,0:T(8,128)(2,1)S(1)}, bf16[8,12288]{1,0:T(8,128)(2,1)S(1)}, u32[]{:S(2)}, u32[]{:S(2)}) collective-permute-start(bf16[8,12288]{1,0:T(8,128)(2,1)S(1)} %collect.1), channel_id=1, source_target_pairs={{0,1},{1,0},{2,3},{3,2},{4,5},{5,4},{6,7},{7,6},{8,9},{9,8},{10,11... | collective-permute-start | bytes 589832 | tf_op jit(solution)/shard_map/ppermute | solution.py:424
  87.2 2.8 %copy-start = (bf16[2,128,12288]{2,1,0:T(8,128)(2,1)S(1)}, bf16[2,128,12288]{2,1,0:T(8,128)(2,1)}, u32[]{:S(2)}) copy-start(bf16[2,128,12288]{2,1,0:T(8,128)(2,1)} %copy.12) | copy-start | bytes 18874372
  93.6 11.1 %collective-permute-start.1 = (bf16[2,8,12288]{2,1,0:T(8,128)(2,1)S(1)}, bf16[2,8,12288]{2,1,0:T(8,128)(2,1)S(1)}, u32[]{:S(2)}, u32[]{:S(2)}) collective-permute-start(bf16[2,8,12288]{2,1,0:T(8,128)(2,1)S(1)} %pad_maximum_fusion.refs_0_), channel_id=1, source_target_pairs={{0,2},{1,3},{2,4},{3,5},{4,6},{5,7},{6,0},{7,1},{8,10},{9,11},{10,... | collective-permute-start | bytes 1179656 | tf_op jit(solution)/shard_map/ppermute | solution.py:424
  95.1 9.7 %collective-permute-start.2 = (bf16[2,8,12288]{2,1,0:T(8,128)(2,1)S(1)}, bf16[2,8,12288]{2,1,0:T(8,128)(2,1)S(1)}, u32[]{:S(2)}, u32[]{:S(2)}) collective-permute-start(bf16[2,8,12288]{2,1,0:T(8,128)(2,1)S(1)} %pad_maximum_fusion.refs_0_), channel_id=1, source_target_pairs={{0,6},{1,7},{2,0},{3,1},{4,2},{5,3},{6,4},{7,5},{8,14},{9,15},{10,... | collective-permute-start | bytes 1179656 | tf_op jit(solution)/shard_map/ppermute | solution.py:424
  104.7 5.8 %collective-permute-start.3 = (bf16[8,12288]{1,0:T(8,128)(2,1)S(1)}, bf16[8,12288]{1,0:T(8,128)(2,1)S(1)}, u32[]{:S(2)}, u32[]{:S(2)}) collective-permute-start(bf16[8,12288]{1,0:T(8,128)(2,1)S(1)} %slice_bitcast_fusion.1), channel_id=1, source_target_pairs={{0,2},{1,3},{2,4},{3,5},{4,6},{5,7},{6,0},{7,1},{8,10},{9,11},{10,... | collective-permute-start | bytes 589832 | tf_op jit(solution)/shard_map/ppermute | solution.py:424
  104.9 5.7 %collective-permute-start.4 = (bf16[8,12288]{1,0:T(8,128)(2,1)S(1)}, bf16[8,12288]{1,0:T(8,128)(2,1)S(1)}, u32[]{:S(2)}, u32[]{:S(2)}) collective-permute-start(bf16[8,12288]{1,0:T(8,128)(2,1)S(1)} %slice_bitcast_fusion), channel_id=1, source_target_pairs={{0,6},{1,7},{2,0},{3,1},{4,2},{5,3},{6,4},{7,5},{8,14},{9,15},{10,... | collective-permute-start | bytes 589832 | tf_op jit(solution)/shard_map/ppermute | solution.py:424
  110.5 2.8 %copy-start.1 = (bf16[2,128,12288]{2,1,0:T(8,128)(2,1)S(1)}, bf16[2,128,12288]{2,1,0:T(8,128)(2,1)}, u32[]{:S(2)}) copy-start(bf16[2,128,12288]{2,1,0:T(8,128)(2,1)} %copy.12) | copy-start | bytes 18874372
Sparse Core Ops, SparseCore 0:
  19.2 53.0 all-gather.1

commit v5 on v4

--- a/solution.py
+++ b/solution.py
@@ -367,7 +367,9 @@
     def _():
         acc_ref[...] = jnp.zeros_like(acc_ref)
 
-    rows = jnp.concatenate([ref[...].reshape(-1, ref.shape[-1]) for ref in pieces], axis=0)
+    chunk = both_ref.shape[1]
+    here = pl.ds(pl.multiple_of(step * chunk, chunk), chunk)
+    rows = jnp.concatenate([ref[:, here] for ref in pieces], axis=0)
     acc_ref[...] += dot_nt(rows, both_ref[...])
 
     @pl.when(step == pl.num_programs(0) - 1)
@@ -392,15 +394,12 @@
     length = pieces[0].shape[-1]
     sizes = [math.prod(piece.shape[:-1]) for piece in pieces]
     skip = start // chunk
-    block = lambda piece: pl.BlockSpec(
-        piece.shape[:-1] + (chunk,), lambda i, *_, n=piece.ndim: (0,) * (n - 1) + (i,)
-    )
     return pl.pallas_call(
         functools.partial(project_kernel, sizes),
         grid_spec=pltpu.PrefetchScalarGridSpec(
             num_scalar_prefetch=1,
             grid=(length // chunk,),
-            in_specs=[block(piece) for piece in pieces]
+            in_specs=[whole(*piece.shape) for piece in pieces]
             + [
                 pl.BlockSpec((both.shape[0], chunk), lambda i, *_: (0, i + skip)),
                 whole(*prev.shape),
@@ -409,7 +408,7 @@
             scratch_shapes=[pltpu.VMEM((sum(sizes), both.shape[0]), F32)],
         ),
         out_shape=jax.ShapeDtypeStruct(prev.shape, F32),
-        compiler_params=pltpu.CompilerParams(vmem_limit_bytes=32 << 20),
+        compiler_params=pltpu.CompilerParams(vmem_limit_bytes=56 << 20),
         cost_estimate=pl.CostEstimate(
             flops=2 * 256 * both.shape[0] * length,
             bytes_accessed=2 * both.shape[0] * length,
@@ -425,12 +424,14 @@
 
 
 def share(x, meanwhile):
-    pair = jnp.stack([x, moved(x, "band", lambda i: i ^ 1)])
-    pair, meanwhile = lax.optimization_barrier((pair, meanwhile))
-    below = moved(pair, "band", lambda i: i + 2)
-    above = moved(pair, "band", lambda i: i - 2)
-    far = [moved(below[0], "band", lambda i: i + 2), moved(above[1], "band", lambda i: i - 2)]
-    return [pair, below, above] + far, meanwhile
+    other = moved(x, "band", lambda i: i ^ 1)
+    below = [moved(x, "band", lambda i: i + 2)]
+    above = [moved(x, "band", lambda i: i - 2)]
+    above.append(moved(other, "band", lambda i: i - 2))
+    below.append(moved(other, "band", lambda i: i + 2))
+    first, second, meanwhile = lax.optimization_barrier((below[0], above[1], meanwhile))
+    far = [moved(first, "band", lambda i: i + 2), moved(second, "band", lambda i: i - 2)]
+    return [x, other] + below + above + far, meanwhile
 
 
 def per_device(slab, panel, potential, pw_slot, columns):

time: 137 us -> 141 us (1.029)
  Pallas kernels: 50.7 us -> 56.7 us
  waiting for transfers between devices: 12.3 us -> 9.05 us
  local copies, waits for them, and re-layouts: 16 us -> 12.9 us
  starting transfers between devices: 16.3 us -> 18.9 us
  blocking collectives: 26.9 us -> 28.6 us
    pallas_call x2, Pallas kernels: 7.1 us -> 13.1 us  [project(): pl.pallas_call(functools.partial(project_kernel, sizes), grid_spec=pltpu....]
    unnamed x18 -> x26, local copies, waits for them, and re-layouts: 6.46 us -> 2.2 us
    ppermute x5 -> x7, waiting for transfers between devices: 10.8 us -> 7.49 us  [moved(): return lax.ppermute(x, axis, [(i, target(i) % size) for i in range(size)])]
    ppermute x5 -> x7, starting transfers between devices: 8.53 us -> 11.2 us  [moved(): return lax.ppermute(x, axis, [(i, target(i) % size) for i in range(size)])]
    all_to_all x1, blocking collectives: 12.1 us -> 13.7 us  [per_device(): terms = lax.all_to_all(terms, 'pw', split_axis=0, concat_axis=0, tiled=True)]
  transfers between devices with their start and end apart: 7 -> 9, of which waited for: 3 -> 4; matrix products, arithmetic and copies ran while one was open for 7% -> 8% of each run, Pallas kernels for 18% -> 19%
where the time goes in v5:
time: 141 us; the launch traced here: 140 us
  Pallas kernels  56.7 us (40%)
  blocking collectives  28.6 us (20%)
  starting transfers between devices  18.9 us (13%)
  between operations  13.5 us (10%)
  local copies, waits for them, and re-layouts  12.9 us (9%)
  waiting for transfers between devices  9.05 us (6%)
    pallas_call x1, Pallas kernels, on_grid(): pl.pallas_call(grid_kernel, in_specs=[whole(*waves.shape), whole(*potenti...  20.4 us
    all_to_all x1, blocking collectives, per_device(): waves = lax.all_to_all(waves, 'pw', split_axis=0, concat_axis=0, tiled=True)  14.8 us
    all_to_all x1, blocking collectives, per_device(): terms = lax.all_to_all(terms, 'pw', split_axis=0, concat_axis=0, tiled=True)  13.7 us
    pallas_call x2, Pallas kernels, project(): pl.pallas_call(functools.partial(project_kernel, sizes), grid_spec=pltpu....  13.1 us
    pallas_call x1, Pallas kernels, spread(): pl.pallas_call(spread_kernel, grid=(waves // chunk,), in_specs=[pl.BlockS...  12.6 us
    ppermute x7, starting transfers between devices, moved(): return lax.ppermute(x, axis, [(i, target(i) % size) for i in range(size)])  11.2 us
    pallas_call x1, Pallas kernels, collect(): pl.pallas_call(collect_kernel, grid=(length // chunk,), in_specs=[pl.Bloc...  10.7 us
    transpose x1, local copies, waits for them, and re-layouts, per_device(): both = jnp.transpose(slab, (1, 0, 2)).reshape(2 * bands, length)  9.39 us
  transfers between devices with their start and end apart: 9, of which 4 were waited for; matrix products, arithmetic and copies ran while one was open for 8% of the time, Pallas kernels for 19%

profile of v5, /device:TPU:1, one launch (start us, length us, event | category | flops | bytes accessed | tf_op | source)
XLA Modules:
  0.0 140.2 jit_solution(17486409120547710452)
XLA Ops:
  6.5 12.6 %spread.1 = (bf16[16,72,256]{2,1,0:T(8,128)(2,1)}, bf16[8,12288]{1,0:T(8,128)(2,1)}) custom-call(s32[1,12288]{1,0:T(1,128)} %bitcast.10, s32[1,256]{1,0:T(1,128)} %bitcast.12, f32[4,2,12288]{2,1,0:T(2,128)} %panel_ref.3, bf16[512,176]{1,0:T(8,128)(2,1)} %constant.66.clone.table_ref), custom_call_target="tpu_custom_call" | custom-call | flops 8858370048 | bytes 4194304 | tf_op jit(solution)/shard_map/spread/pallas_call | solution.py:142
  19.1 7.8 %all-to-all-start = ((bf16[16,72,256]{2,1,0:T(8,128)(2,1)}), bf16[16,72,256]{2,1,0:T(8,128)(2,1)S(1)}, u32[]{:S(2)}, u32[]{:S(2)}) async-start(bf16[16,72,256]{2,1,0:T(8,128)(2,1)} %get-tuple-element.14), calls=%async_computation | async-start | bytes 1179648 | tf_op jit(solution)/shard_map/all_to_all | solution.py:444
  26.9 9.4 %copy.12 = bf16[2,128,12288]{2,1,0:T(8,128)(2,1)} copy(bf16[2,128,12288]{2,0,1:T(2,128)(2,1)} %bitcast.16) | data formatting | bytes 12582912 | tf_op jit(solution)/shard_map/transpose | solution.py:446
  36.3 1.5 %all-to-all-done.in_ref = bf16[16,72,256]{2,1,0:T(8,128)(2,1)S(1)} async-done(((bf16[16,72,256]{2,1,0:T(8,128)(2,1)}), bf16[16,72,256]{2,1,0:T(8,128)(2,1)S(1)}, u32[]{:S(2)}, u32[]{:S(2)}) %all-to-all-start) | async-done | bytes 589856 | tf_op jit(solution)/shard_map/all_to_all | solution.py:444
  37.8 0.9 copy-done.5
  38.7 20.4 %on_grid.1 = bf16[16,64,256]{2,1,0:T(8,128)(2,1)} custom-call(bf16[16,72,256]{2,1,0:T(8,128)(2,1)} %copy-done.5, f32[8,128,128]{2,1,0:T(8,128)} %pot_ref.1, bf16[256,512]{1,0:T(8,128)(2,1)} %constant.67.clone.ti_ref, bf16[512,192]{1,0:T(8,128)(2,1)} %constant.68.clone.oi_ref, bf16[384,256]{1,0:T(8,128)(2,1)} %constant.69.clone.oo_ref, ...), custom_call_target="tpu_custom_call" | custom-call | flops 10737418240 | bytes 4194304 | tf_op jit(solution)/shard_map/on_grid/pallas_call | solution.py:262
  59.1 14.8 %all_to_all.15.in_ref = bf16[16,64,256]{2,1,0:T(8,128)(2,1)S(1)} all-to-all(bf16[16,64,256]{2,1,0:T(8,128)(2,1)} %on_grid.1), channel_id=1, replica_groups=mesh['pw'=16,'band'=8] {'pw'}, dimensions={0} | all-to-all | bytes 1048576 | tf_op jit(solution)/shard_map/all_to_all | solution.py:449
  74.0 10.7 %collect.1.refs_0_ = bf16[8,12288]{1,0:T(8,128)(2,1)S(1)} custom-call(s32[1,12288]{1,0:T(1,128)S(1)} %bitcast.11, s32[1,256]{1,0:T(1,128)S(1)} %bitcast.13, f32[4,2,12288]{2,1,0:T(2,128)S(1)} %copy-done.1, bf16[16,64,256]{2,1,0:T(8,128)(2,1)S(1)} %all_to_all.15.in_ref, bf16[352,256]{1,0:T(8,128)(2,1)S(1)} %copy-done.4), custom_call_target="tpu_custom_call" | custom-call | flops 8858370048 | bytes 4194304 | tf_op jit(solution)/shard_map/collect/pallas_call | solution.py:338
  84.7 2.5 %collective-permute-start = (bf16[8,12288]{1,0:T(8,128)(2,1)S(1)}, bf16[8,12288]{1,0:T(8,128)(2,1)S(1)}, u32[]{:S(2)}, u32[]{:S(2)}) collective-permute-start(bf16[8,12288]{1,0:T(8,128)(2,1)S(1)} %collect.1.refs_0_), channel_id=1, source_target_pairs={{0,1},{1,0},{2,3},{3,2},{4,5},{5,4},{6,7},{7,6},{8,9},{9,8},{10,11... | collective-permute-start | bytes 589832 | tf_op jit(solution)/shard_map/ppermute | solution.py:423
  87.2 1.4 %collective-permute-start.1 = (bf16[8,12288]{1,0:T(8,128)(2,1)S(1)}, bf16[8,12288]{1,0:T(8,128)(2,1)S(1)}, u32[]{:S(2)}, u32[]{:S(2)}) collective-permute-start(bf16[8,12288]{1,0:T(8,128)(2,1)S(1)} %collect.1.refs_0_), channel_id=1, source_target_pairs={{0,2},{1,3},{2,4},{3,5},{4,6},{5,7},{6,0},{7,1},{8,10},{9,11},{10,... | collective-permute-start | bytes 589832 | tf_op jit(solution)/shard_map/ppermute | solution.py:423
  88.6 2.9 %collective-permute-done.refs_1_ = bf16[8,12288]{1,0:T(8,128)(2,1)S(1)} collective-permute-done((bf16[8,12288]{1,0:T(8,128)(2,1)S(1)}, bf16[8,12288]{1,0:T(8,128)(2,1)S(1)}, u32[]{:S(2)}, u32[]{:S(2)}) %collective-permute-start) | collective-permute-done | bytes 196640 | tf_op jit(solution)/shard_map/ppermute | solution.py:423
  91.5 3.0 %collective-permute-start.4 = (bf16[8,12288]{1,0:T(8,128)(2,1)S(1)}, bf16[8,12288]{1,0:T(8,128)(2,1)S(1)}, u32[]{:S(2)}, u32[]{:S(2)}) collective-permute-start(bf16[8,12288]{1,0:T(8,128)(2,1)S(1)} %collective-permute-done.refs_1_), channel_id=1, source_target_pairs={{0,6},{1,7},{2,0},{3,1},{4,2},{5,3},{6,4},{7,5},{8,14},{9,15},{10,... | collective-permute-start | bytes 589832 | tf_op jit(solution)/shard_map/ppermute | solution.py:423
  94.9 0.6 broadcast_in_dim.3.refs_2_
  95.5 6.6 %project.2.refs_9_ = f32[16,8,128]{2,1,0:T(8,128)} custom-call(s32[9]{0:T(128)} %constant.64.clone.1.seat_ref, bf16[64,12288]{1,0:T(8,128)(2,1)} %all-gather.2.cloned.1.call-done.refs_0_, bf16[256,12288]{1,0:T(8,128)(2,1)} %bitcast.14, f32[16,8,128]{2,1,0:T(8,128)} %broadcast_in_dim.3.refs_2_), custom_call_target="tpu_custom_call" | custom-call | flops 1610612736 | bytes 6291456 | tf_op jit(solution)/shard_map/project/pallas_call | solution.py:397
  102.0 1.1 collective-permute-start.2
  103.2 2.7 %collective-permute-start.6 = (bf16[8,12288]{1,0:T(8,128)(2,1)S(1)}, bf16[8,12288]{1,0:T(8,128)(2,1)S(1)}, u32[]{:S(2)}, u32[]{:S(2)}) collective-permute-start(bf16[8,12288]{1,0:T(8,128)(2,1)S(1)} %collective-permute-done.4.refs_5_), channel_id=1, source_target_pairs={{0,6},{1,7},{2,0},{3,1},{4,2},{5,3},{6,4},{7,5},{8,14},{9,15},{10,... | collective-permute-start | bytes 589832 | tf_op jit(solution)/shard_map/ppermute | solution.py:423
  105.9 0.7 stack.23.seat_ref
  106.6 1.2 collective-permute-done.2.refs_3_
  107.8 3.4 %collective-permute-done.5.refs_6_ = bf16[8,12288]{1,0:T(8,128)(2,1)S(1)} collective-permute-done((bf16[8,12288]{1,0:T(8,128)(2,1)S(1)}, bf16[8,12288]{1,0:T(8,128)(2,1)S(1)}, u32[]{:S(2)}, u32[]{:S(2)}) %collective-permute-start.5) | collective-permute-done | bytes 196640 | tf_op jit(solution)/shard_map/ppermute | solution.py:423
  111.3 0.6 copy-done.11
  111.9 0.7 copy-done.12
  112.6 6.5 %project.3 = f32[16,8,128]{2,1,0:T(8,128)} custom-call(s32[9]{0:T(128)} %stack.23.seat_ref, bf16[8,12288]{1,0:T(8,128)(2,1)} %copy-done, bf16[8,12288]{1,0:T(8,128)(2,1)} %copy-done.6, bf16[8,12288]{1,0:T(8,128)(2,1)} %copy-done.7, bf16[8,12288]{1,0:T(8,128)(2,1)} %copy-done.10, bf16[8,12288]{1,0:T(8,128)(2,1)} %copy-done.9, bf16[8,12288]{1,0:T(8,128)(2,1)} %copy-done.8, ...), custom_call_target="tpu_custom_call" | custom-call | flops 1610612736 | bytes 6291456 | tf_op jit(solution)/shard_map/project/pallas_call | solution.py:397
  119.1 13.7 %all_to_all.16 = f32[16,8,128]{2,1,0:T(8,128)S(1)} all-to-all(f32[16,8,128]{2,1,0:T(8,128)} %project.3), channel_id=1, replica_groups=mesh['pw'=16,'band'=8] {'pw'}, dimensions={0} | all-to-all | bytes 131072 | tf_op jit(solution)/shard_map/all_to_all | solution.py:461
  132.8 0.6 reduce_sum.9
  (33 shorter events, 0.5 us)
Async XLA Ops:
  6.5 67.5 %all-gather.2.cloned.1.call-start = ((), (), s32[]{:S(2)}) async-start(), calls=%async_computation.3 | async-start | bytes 1769472 | tf_op jit(solution)/shard_map/all_gather | solution.py:445
  19.1 18.7 %all-to-all-start = ((bf16[16,72,256]{2,1,0:T(8,128)(2,1)}), bf16[16,72,256]{2,1,0:T(8,128)(2,1)S(1)}, u32[]{:S(2)}, u32[]{:S(2)}) async-start(bf16[16,72,256]{2,1,0:T(8,128)(2,1)} %get-tuple-element.14), calls=%async_computation | async-start | bytes 1179648 | tf_op jit(solution)/shard_map/all_to_all | solution.py:444
  37.8 0.9 copy-start.5
  38.7 35.3 %copy-start.1 = (f32[4,2,12288]{2,1,0:T(2,128)S(1)}, f32[4,2,12288]{2,1,0:T(2,128)}, u32[]{:S(2)}) copy-start(f32[4,2,12288]{2,1,0:T(2,128)} %panel_ref.3) | copy-start | bytes 1179652
  38.7 35.3 %copy-start.2 = (s32[12288]{0:T(1024)S(1)}, s32[12288]{0:T(1024)}, u32[]{:S(2)}) copy-start(s32[12288]{0:T(1024)} %param.14) | copy-start | bytes 147460
  38.7 35.3 %copy-start.3 = (s32[256]{0:T(256)S(1)}, s32[256]{0:T(256)}, u32[]{:S(2)}) copy-start(s32[256]{0:T(256)} %param.15) | copy-start | bytes 3076
  38.7 35.3 %copy-start.4 = (bf16[352,256]{1,0:T(8,128)(2,1)S(1)}, bf16[352,256]{1,0:T(8,128)(2,1)}, u32[]{:S(2)}) copy-start(bf16[352,256]{1,0:T(8,128)(2,1)} %constant.71.clone.table_ref) | copy-start | bytes 540676
  84.7 26.5 %copy-start = (bf16[8,12288]{1,0:T(8,128)(2,1)}, bf16[8,12288]{1,0:T(8,128)(2,1)S(1)}, u32[]{:S(2)}) copy-start(bf16[8,12288]{1,0:T(8,128)(2,1)S(1)} %collect.1.refs_0_) | copy-start | bytes 589828
  84.7 6.8 %collective-permute-start = (bf16[8,12288]{1,0:T(8,128)(2,1)S(1)}, bf16[8,12288]{1,0:T(8,128)(2,1)S(1)}, u32[]{:S(2)}, u32[]{:S(2)}) collective-permute-start(bf16[8,12288]{1,0:T(8,128)(2,1)S(1)} %collect.1.refs_0_), channel_id=1, source_target_pairs={{0,1},{1,0},{2,3},{3,2},{4,5},{5,4},{6,7},{7,6},{8,9},{9,8},{10,11... | collective-permute-start | bytes 589832 | tf_op jit(solution)/shard_map/ppermute | solution.py:423
  87.2 15.9 %collective-permute-start.1 = (bf16[8,12288]{1,0:T(8,128)(2,1)S(1)}, bf16[8,12288]{1,0:T(8,128)(2,1)S(1)}, u32[]{:S(2)}, u32[]{:S(2)}) collective-permute-start(bf16[8,12288]{1,0:T(8,128)(2,1)S(1)} %collect.1.refs_0_), channel_id=1, source_target_pairs={{0,2},{1,3},{2,4},{3,5},{4,6},{5,7},{6,0},{7,1},{8,10},{9,11},{10,... | collective-permute-start | bytes 589832 | tf_op jit(solution)/shard_map/ppermute | solution.py:423
  91.5 19.7 %copy-start.6 = (bf16[8,12288]{1,0:T(8,128)(2,1)}, bf16[8,12288]{1,0:T(8,128)(2,1)S(1)}, u32[]{:S(2)}) copy-start(bf16[8,12288]{1,0:T(8,128)(2,1)S(1)} %collective-permute-done.refs_1_) | copy-start | bytes 589828
  91.5 11.6 %collective-permute-start.4 = (bf16[8,12288]{1,0:T(8,128)(2,1)S(1)}, bf16[8,12288]{1,0:T(8,128)(2,1)S(1)}, u32[]{:S(2)}, u32[]{:S(2)}) collective-permute-start(bf16[8,12288]{1,0:T(8,128)(2,1)S(1)} %collective-permute-done.refs_1_), channel_id=1, source_target_pairs={{0,6},{1,7},{2,0},{3,1},{4,2},{5,3},{6,4},{7,5},{8,14},{9,15},{10,... | collective-permute-start | bytes 589832 | tf_op jit(solution)/shard_map/ppermute | solution.py:423
  94.5 12.1 %collective-permute-start.3 = (bf16[8,12288]{1,0:T(8,128)(2,1)S(1)}, bf16[8,12288]{1,0:T(8,128)(2,1)S(1)}, u32[]{:S(2)}, u32[]{:S(2)}) collective-permute-start(bf16[8,12288]{1,0:T(8,128)(2,1)S(1)} %collect.1.refs_0_), channel_id=1, source_target_pairs={{0,6},{1,7},{2,0},{3,1},{4,2},{5,3},{6,4},{7,5},{8,14},{9,15},{10,... | collective-permute-start | bytes 589832 | tf_op jit(solution)/shard_map/ppermute | solution.py:423
  102.0 5.7 %collective-permute-start.2 = (bf16[8,12288]{1,0:T(8,128)(2,1)S(1)}, bf16[8,12288]{1,0:T(8,128)(2,1)S(1)}, u32[]{:S(2)}, u32[]{:S(2)}) collective-permute-start(bf16[8,12288]{1,0:T(8,128)(2,1)S(1)} %collective-permute-done.refs_1_), channel_id=1, source_target_pairs={{0,2},{1,3},{2,4},{3,5},{4,6},{5,7},{6,0},{7,1},{8,10},{9,11},{10,... | collective-permute-start | bytes 589832 | tf_op jit(solution)/shard_map/ppermute | solution.py:423
  103.1 8.1 %copy-start.7 = (bf16[8,12288]{1,0:T(8,128)(2,1)}, bf16[8,12288]{1,0:T(8,128)(2,1)S(1)}, u32[]{:S(2)}) copy-start(bf16[8,12288]{1,0:T(8,128)(2,1)S(1)} %collective-permute-done.1.refs_2_) | copy-start | bytes 589828
  103.1 8.1 %copy-start.8 = (bf16[8,12288]{1,0:T(8,128)(2,1)}, bf16[8,12288]{1,0:T(8,128)(2,1)S(1)}, u32[]{:S(2)}) copy-start(bf16[8,12288]{1,0:T(8,128)(2,1)S(1)} %collective-permute-done.4.refs_5_) | copy-start | bytes 589828
  103.2 8.1 %collective-permute-start.5 = (bf16[8,12288]{1,0:T(8,128)(2,1)S(1)}, bf16[8,12288]{1,0:T(8,128)(2,1)S(1)}, u32[]{:S(2)}, u32[]{:S(2)}) collective-permute-start(bf16[8,12288]{1,0:T(8,128)(2,1)S(1)} %collective-permute-done.1.refs_2_), channel_id=1, source_target_pairs={{0,2},{1,3},{2,4},{3,5},{4,6},{5,7},{6,0},{7,1},{8,10},{9,11},{10,... | collective-permute-start | bytes 589832 | tf_op jit(solution)/shard_map/ppermute | solution.py:423
  103.2 8.0 %collective-permute-start.6 = (bf16[8,12288]{1,0:T(8,128)(2,1)S(1)}, bf16[8,12288]{1,0:T(8,128)(2,1)S(1)}, u32[]{:S(2)}, u32[]{:S(2)}) collective-permute-start(bf16[8,12288]{1,0:T(8,128)(2,1)S(1)} %collective-permute-done.4.refs_5_), channel_id=1, source_target_pairs={{0,6},{1,7},{2,0},{3,1},{4,2},{5,3},{6,4},{7,5},{8,14},{9,15},{10,... | collective-permute-start | bytes 589832 | tf_op jit(solution)/shard_map/ppermute | solution.py:423
  106.6 4.7 %copy-start.9 = (bf16[8,12288]{1,0:T(8,128)(2,1)}, bf16[8,12288]{1,0:T(8,128)(2,1)S(1)}, u32[]{:S(2)}) copy-start(bf16[8,12288]{1,0:T(8,128)(2,1)S(1)} %collective-permute-done.3.refs_4_) | copy-start | bytes 589828
  107.8 3.5 %copy-start.10 = (bf16[8,12288]{1,0:T(8,128)(2,1)}, bf16[8,12288]{1,0:T(8,128)(2,1)S(1)}, u32[]{:S(2)}) copy-start(bf16[8,12288]{1,0:T(8,128)(2,1)S(1)} %collective-permute-done.2.refs_3_) | copy-start | bytes 589828
  111.2 0.7 copy-start.11
  111.9 0.7 copy-start.12
Sparse Core Ops, SparseCore 0:
  19.2 52.9 all-gather.1

commit v6 on v4

--- a/solution.py
+++ b/solution.py
@@ -19,6 +19,7 @@
 PARTS = 4
 STEP = 24
 USED = 20
+GROUP = 4
 FIRSTS = PARTS * STEP
 NT = (((1,), (1,)), ((), ()))
 
@@ -171,6 +172,7 @@
     tall = 2 * planes
     count = rows // tall
 
+    field = None
     for owner in range(owners):
         here = slice(owner * cols, (owner + 1) * cols)
         values = in_ref[owner].astype(F32)
@@ -182,7 +184,11 @@
         lhs_ref[:, here] = jnp.concatenate(
             [values[row : row + 1] * mask for row in range(rows)], axis=0
         ).astype(BF16)
-    field = dot_nt(lhs_ref[...], pick_ref[...]).astype(BF16)
+        if (owner + 1) % GROUP == 0:
+            group = slice((owner + 1 - GROUP) * cols, (owner + 1) * cols)
+            found = dot_nt(lhs_ref[:, group], pick_ref[:, group])
+            field = found if field is None else field + found
+    field = field.astype(BF16)
     block = planes * STEP
     lanes = lambda bit: slice(bit * LEN, (bit + 1) * LEN)
     spun = []

time: 137 us -> 137 us (level)
  no operation moved by 1% of the time
where the time goes in v6:
time: 137 us; the launch traced here: 136 us
  Pallas kernels  50.7 us (37%)
  blocking collectives  26.9 us (20%)
  starting transfers between devices  16.3 us (12%)
  local copies, waits for them, and re-layouts  16 us (12%)
  between operations  13.5 us (10%)
  waiting for transfers between devices  12.3 us (9%)
    pallas_call x1, Pallas kernels, on_grid(): pl.pallas_call(grid_kernel, in_specs=[whole(*waves.shape), whole(*potenti...  20.4 us
    all_to_all x1, blocking collectives, per_device(): waves = lax.all_to_all(waves, 'pw', split_axis=0, concat_axis=0, tiled=True)  14.8 us
    pallas_call x1, Pallas kernels, spread(): pl.pallas_call(spread_kernel, grid=(waves // chunk,), in_specs=[pl.BlockS...  12.5 us
    all_to_all x1, blocking collectives, per_device(): terms = lax.all_to_all(terms, 'pw', split_axis=0, concat_axis=0, tiled=True)  12.1 us
    ppermute x5, waiting for transfers between devices, moved(): return lax.ppermute(x, axis, [(i, target(i) % size) for i in range(size)])  10.8 us
    pallas_call x1, Pallas kernels, collect(): pl.pallas_call(collect_kernel, grid=(length // chunk,), in_specs=[pl.Bloc...  10.7 us
    transpose x1, local copies, waits for them, and re-layouts, per_device(): both = jnp.transpose(slab, (1, 0, 2)).reshape(2 * bands, length)  9.4 us
    ppermute x5, starting transfers between devices, moved(): return lax.ppermute(x, axis, [(i, target(i) % size) for i in range(size)])  8.53 us
  transfers between devices with their start and end apart: 7, of which 3 were waited for; matrix products, arithmetic and copies ran while one was open for 7% of the time, Pallas kernels for 18%

profile of v6, /device:TPU:1, one launch (start us, length us, event | category | flops | bytes accessed | tf_op | source)
XLA Modules:
  0.0 136.4 jit_solution(2426503876008871999)
XLA Ops:
  6.5 12.5 %spread.1 = (bf16[16,72,256]{2,1,0:T(8,128)(2,1)}, bf16[8,12288]{1,0:T(8,128)(2,1)}) custom-call(s32[1,12288]{1,0:T(1,128)} %bitcast.19, s32[1,256]{1,0:T(1,128)} %bitcast.21, f32[4,2,12288]{2,1,0:T(2,128)} %panel_ref.3, bf16[512,176]{1,0:T(8,128)(2,1)} %constant.66.clone.table_ref), custom_call_target="tpu_custom_call" | custom-call | flops 8858370048 | bytes 4194304 | tf_op jit(solution)/shard_map/spread/pallas_call | solution.py:143
  19.1 0.0 all-gather.2.cloned.1.call-update
  19.1 7.8 %all-to-all-start = ((bf16[16,72,256]{2,1,0:T(8,128)(2,1)}), bf16[16,72,256]{2,1,0:T(8,128)(2,1)S(1)}, u32[]{:S(2)}, u32[]{:S(2)}) async-start(bf16[16,72,256]{2,1,0:T(8,128)(2,1)} %get-tuple-element.13), calls=%async_computation | async-start | bytes 1179648 | tf_op jit(solution)/shard_map/all_to_all | solution.py:449
  26.9 9.4 %copy.12 = bf16[2,128,12288]{2,1,0:T(8,128)(2,1)} copy(bf16[2,128,12288]{2,0,1:T(2,128)(2,1)} %bitcast.23) | data formatting | bytes 12582912 | tf_op jit(solution)/shard_map/transpose | solution.py:451
  36.3 1.5 %all-to-all-done.in_ref = bf16[16,72,256]{2,1,0:T(8,128)(2,1)S(1)} async-done(((bf16[16,72,256]{2,1,0:T(8,128)(2,1)}), bf16[16,72,256]{2,1,0:T(8,128)(2,1)S(1)}, u32[]{:S(2)}, u32[]{:S(2)}) %all-to-all-start) | async-done | bytes 589856 | tf_op jit(solution)/shard_map/all_to_all | solution.py:449
  37.8 0.9 copy-done.8
  38.7 20.4 %on_grid.1 = bf16[16,64,256]{2,1,0:T(8,128)(2,1)} custom-call(bf16[16,72,256]{2,1,0:T(8,128)(2,1)} %copy-done.8, f32[8,128,128]{2,1,0:T(8,128)} %pot_ref.1, bf16[256,512]{1,0:T(8,128)(2,1)} %constant.67.clone.ti_ref, bf16[512,192]{1,0:T(8,128)(2,1)} %constant.68.clone.oi_ref, bf16[384,256]{1,0:T(8,128)(2,1)} %constant.69.clone.oo_ref, ...), custom_call_target="tpu_custom_call" | custom-call | flops 10737418240 | bytes 4194304 | tf_op jit(solution)/shard_map/on_grid/pallas_call | solution.py:268
  59.1 14.8 %all_to_all.15.in_ref = bf16[16,64,256]{2,1,0:T(8,128)(2,1)S(1)} all-to-all(bf16[16,64,256]{2,1,0:T(8,128)(2,1)} %on_grid.1), channel_id=1, replica_groups=mesh['pw'=16,'band'=8] {'pw'}, dimensions={0} | all-to-all | bytes 1048576 | tf_op jit(solution)/shard_map/all_to_all | solution.py:454
  74.0 10.7 %collect.1 = bf16[8,12288]{1,0:T(8,128)(2,1)S(1)} custom-call(s32[1,12288]{1,0:T(1,128)S(1)} %bitcast.20, s32[1,256]{1,0:T(1,128)S(1)} %bitcast.22, f32[4,2,12288]{2,1,0:T(2,128)S(1)} %copy-done.4, bf16[16,64,256]{2,1,0:T(8,128)(2,1)S(1)} %all_to_all.15.in_ref, bf16[352,256]{1,0:T(8,128)(2,1)S(1)} %copy-done.7), custom_call_target="tpu_custom_call" | custom-call | flops 8858370048 | bytes 4194304 | tf_op jit(solution)/shard_map/collect/pallas_call | solution.py:344
  84.7 2.6 %collective-permute-start = (bf16[8,12288]{1,0:T(8,128)(2,1)S(1)}, bf16[8,12288]{1,0:T(8,128)(2,1)S(1)}, u32[]{:S(2)}, u32[]{:S(2)}) collective-permute-start(bf16[8,12288]{1,0:T(8,128)(2,1)S(1)} %collect.1), channel_id=1, source_target_pairs={{0,1},{1,0},{2,3},{3,2},{4,5},{5,4},{6,7},{7,6},{8,9},{9,8},{10,11... | collective-permute-start | bytes 589832 | tf_op jit(solution)/shard_map/ppermute | solution.py:430
  87.3 2.8 %copy-done = bf16[2,128,12288]{2,1,0:T(8,128)(2,1)S(1)} copy-done((bf16[2,128,12288]{2,1,0:T(8,128)(2,1)S(1)}, bf16[2,128,12288]{2,1,0:T(8,128)(2,1)}, u32[]{:S(2)}) %copy-start) | copy-done | bytes 6291480
  90.0 3.6 %project.2.refs_6_ = f32[16,8,128]{2,1,0:T(8,128)S(1)} custom-call(s32[9]{0:T(128)S(1)} %copy-done.3, bf16[64,12288]{1,0:T(8,128)(2,1)S(1)} %copy-done.2, bf16[256,12288]{1,0:T(8,128)(2,1)S(1)} %bitcast.16, f32[16,8,128]{2,1,0:T(8,128)S(1)} %broadcast_in_dim.3.refs_2_), custom_call_target="tpu_custom_call" | custom-call | flops 1610612736 | bytes 6291456 | tf_op jit(solution)/shard_map/project/pallas_call | solution.py:404
  93.7 1.5 %collective-permute-start.1 = (bf16[2,8,12288]{2,1,0:T(8,128)(2,1)S(1)}, bf16[2,8,12288]{2,1,0:T(8,128)(2,1)S(1)}, u32[]{:S(2)}, u32[]{:S(2)}) collective-permute-start(bf16[2,8,12288]{2,1,0:T(8,128)(2,1)S(1)} %pad_maximum_fusion.refs_0_), channel_id=1, source_target_pairs={{0,2},{1,3},{2,4},{3,5},{4,6},{5,7},{6,0},{7,1},{8,10},{9,11},{10,... | collective-permute-start | bytes 1179656 | tf_op jit(solution)/shard_map/ppermute | solution.py:430
  95.1 1.7 %collective-permute-start.2 = (bf16[2,8,12288]{2,1,0:T(8,128)(2,1)S(1)}, bf16[2,8,12288]{2,1,0:T(8,128)(2,1)S(1)}, u32[]{:S(2)}, u32[]{:S(2)}) collective-permute-start(bf16[2,8,12288]{2,1,0:T(8,128)(2,1)S(1)} %pad_maximum_fusion.refs_0_), channel_id=1, source_target_pairs={{0,6},{1,7},{2,0},{3,1},{4,2},{5,3},{6,4},{7,5},{8,14},{9,15},{10,... | collective-permute-start | bytes 1179656 | tf_op jit(solution)/shard_map/ppermute | solution.py:430
  96.8 7.9 %collective-permute-done.1.refs_1_ = bf16[2,8,12288]{2,1,0:T(8,128)(2,1)S(1)} collective-permute-done((bf16[2,8,12288]{2,1,0:T(8,128)(2,1)S(1)}, bf16[2,8,12288]{2,1,0:T(8,128)(2,1)S(1)}, u32[]{:S(2)}, u32[]{:S(2)}) %collective-permute-start.1) | collective-permute-done | bytes 393248 | tf_op jit(solution)/shard_map/ppermute | solution.py:430
  104.7 0.1 collective-permute-start.3
  104.9 2.7 %collective-permute-start.4 = (bf16[8,12288]{1,0:T(8,128)(2,1)S(1)}, bf16[8,12288]{1,0:T(8,128)(2,1)S(1)}, u32[]{:S(2)}, u32[]{:S(2)}) collective-permute-start(bf16[8,12288]{1,0:T(8,128)(2,1)S(1)} %slice_bitcast_fusion), channel_id=1, source_target_pairs={{0,6},{1,7},{2,0},{3,1},{4,2},{5,3},{6,4},{7,5},{8,14},{9,15},{10,... | collective-permute-start | bytes 589832 | tf_op jit(solution)/shard_map/ppermute | solution.py:430
  107.6 0.1 stack.32.seat_ref
  107.7 2.9 %collective-permute-done.3.refs_3_ = bf16[8,12288]{1,0:T(8,128)(2,1)S(1)} collective-permute-done((bf16[8,12288]{1,0:T(8,128)(2,1)S(1)}, bf16[8,12288]{1,0:T(8,128)(2,1)S(1)}, u32[]{:S(2)}, u32[]{:S(2)}) %collective-permute-start.3) | collective-permute-done | bytes 196640 | tf_op jit(solution)/shard_map/ppermute | solution.py:430
  110.5 0.0 collective-permute-done.4.refs_4_
  110.5 2.8 %copy-done.1 = bf16[2,128,12288]{2,1,0:T(8,128)(2,1)S(1)} copy-done((bf16[2,128,12288]{2,1,0:T(8,128)(2,1)S(1)}, bf16[2,128,12288]{2,1,0:T(8,128)(2,1)}, u32[]{:S(2)}) %copy-start.1) | copy-done | bytes 6291480
  113.3 3.5 %project.3 = f32[16,8,128]{2,1,0:T(8,128)S(1)} custom-call(s32[9]{0:T(128)S(1)} %stack.32.seat_ref, bf16[2,8,12288]{2,1,0:T(8,128)(2,1)S(1)} %pad_maximum_fusion.refs_0_, bf16[2,8,12288]{2,1,0:T(8,128)(2,1)S(1)} %collective-permute-done.1.refs_1_, bf16[2,8,12288]{2,1,0:T(8,128)(2,1)S(1)} %collective-permute-done.2.refs_2_, ...), custom_call_target="tpu_custom_call" | custom-call | flops 1610612736 | bytes 6291456 | tf_op jit(solution)/shard_map/project/pallas_call | solution.py:404
  116.9 12.1 %all_to_all.16 = f32[16,8,128]{2,1,0:T(8,128)S(1)} all-to-all(f32[16,8,128]{2,1,0:T(8,128)S(1)} %project.3), channel_id=1, replica_groups=mesh['pw'=16,'band'=8] {'pw'}, dimensions={0} | all-to-all | bytes 131072 | tf_op jit(solution)/shard_map/all_to_all | solution.py:466
  128.9 0.6 reduce_sum.9
  (24 shorter events, 0.1 us)
Async XLA Ops:
  6.5 67.4 %all-gather.2.cloned.1.call-start = ((), (), s32[]{:S(2)}) async-start(), calls=%async_computation.3 | async-start | bytes 1769472 | tf_op jit(solution)/shard_map/all_gather | solution.py:450
  19.1 18.7 %all-to-all-start = ((bf16[16,72,256]{2,1,0:T(8,128)(2,1)}), bf16[16,72,256]{2,1,0:T(8,128)(2,1)S(1)}, u32[]{:S(2)}, u32[]{:S(2)}) async-start(bf16[16,72,256]{2,1,0:T(8,128)(2,1)} %get-tuple-element.13), calls=%async_computation | async-start | bytes 1179648 | tf_op jit(solution)/shard_map/all_to_all | solution.py:449
  37.8 0.9 copy-start.8
  38.7 35.3 %copy-start.4 = (f32[4,2,12288]{2,1,0:T(2,128)S(1)}, f32[4,2,12288]{2,1,0:T(2,128)}, u32[]{:S(2)}) copy-start(f32[4,2,12288]{2,1,0:T(2,128)} %panel_ref.3) | copy-start | bytes 1179652
  38.7 35.3 %copy-start.5 = (s32[12288]{0:T(1024)S(1)}, s32[12288]{0:T(1024)}, u32[]{:S(2)}) copy-start(s32[12288]{0:T(1024)} %param.14) | copy-start | bytes 147460
  38.7 35.3 %copy-start.6 = (s32[256]{0:T(256)S(1)}, s32[256]{0:T(256)}, u32[]{:S(2)}) copy-start(s32[256]{0:T(256)} %param.15) | copy-start | bytes 3076
  38.7 35.3 %copy-start.7 = (bf16[352,256]{1,0:T(8,128)(2,1)S(1)}, bf16[352,256]{1,0:T(8,128)(2,1)}, u32[]{:S(2)}) copy-start(bf16[352,256]{1,0:T(8,128)(2,1)} %constant.71.clone.table_ref) | copy-start | bytes 540676
  74.0 13.3 %copy-start.3 = (s32[9]{0:T(128)S(1)}, s32[9]{0:T(128)}, u32[]{:S(2)}) copy-start(s32[9]{0:T(128)} %constant.64.clone.1.seat_ref) | copy-start | bytes 112
  74.0 13.2 %copy-start.2 = (bf16[64,12288]{1,0:T(8,128)(2,1)S(1)}, bf16[64,12288]{1,0:T(8,128)(2,1)}, u32[]{:S(2)}) copy-start(bf16[64,12288]{1,0:T(8,128)(2,1)} %all-gather.2.cloned.1.call-done.refs_0_) | copy-start | bytes 4718596
  84.7 8.9 %collective-permute-start = (bf16[8,12288]{1,0:T(8,128)(2,1)S(1)}, bf16[8,12288]{1,0:T(8,128)(2,1)S(1)}, u32[]{:S(2)}, u32[]{:S(2)}) collective-permute-start(bf16[8,12288]{1,0:T(8,128)(2,1)S(1)} %collect.1), channel_id=1, source_target_pairs={{0,1},{1,0},{2,3},{3,2},{4,5},{5,4},{6,7},{7,6},{8,9},{9,8},{10,11... | collective-permute-start | bytes 589832 | tf_op jit(solution)/shard_map/ppermute | solution.py:430
  87.2 2.8 %copy-start = (bf16[2,128,12288]{2,1,0:T(8,128)(2,1)S(1)}, bf16[2,128,12288]{2,1,0:T(8,128)(2,1)}, u32[]{:S(2)}) copy-start(bf16[2,128,12288]{2,1,0:T(8,128)(2,1)} %copy.12) | copy-start | bytes 18874372
  93.7 11.1 %collective-permute-start.1 = (bf16[2,8,12288]{2,1,0:T(8,128)(2,1)S(1)}, bf16[2,8,12288]{2,1,0:T(8,128)(2,1)S(1)}, u32[]{:S(2)}, u32[]{:S(2)}) collective-permute-start(bf16[2,8,12288]{2,1,0:T(8,128)(2,1)S(1)} %pad_maximum_fusion.refs_0_), channel_id=1, source_target_pairs={{0,2},{1,3},{2,4},{3,5},{4,6},{5,7},{6,0},{7,1},{8,10},{9,11},{10,... | collective-permute-start | bytes 1179656 | tf_op jit(solution)/shard_map/ppermute | solution.py:430
  95.1 9.7 %collective-permute-start.2 = (bf16[2,8,12288]{2,1,0:T(8,128)(2,1)S(1)}, bf16[2,8,12288]{2,1,0:T(8,128)(2,1)S(1)}, u32[]{:S(2)}, u32[]{:S(2)}) collective-permute-start(bf16[2,8,12288]{2,1,0:T(8,128)(2,1)S(1)} %pad_maximum_fusion.refs_0_), channel_id=1, source_target_pairs={{0,6},{1,7},{2,0},{3,1},{4,2},{5,3},{6,4},{7,5},{8,14},{9,15},{10,... | collective-permute-start | bytes 1179656 | tf_op jit(solution)/shard_map/ppermute | solution.py:430
  104.7 5.8 %collective-permute-start.3 = (bf16[8,12288]{1,0:T(8,128)(2,1)S(1)}, bf16[8,12288]{1,0:T(8,128)(2,1)S(1)}, u32[]{:S(2)}, u32[]{:S(2)}) collective-permute-start(bf16[8,12288]{1,0:T(8,128)(2,1)S(1)} %slice_bitcast_fusion.1), channel_id=1, source_target_pairs={{0,2},{1,3},{2,4},{3,5},{4,6},{5,7},{6,0},{7,1},{8,10},{9,11},{10,... | collective-permute-start | bytes 589832 | tf_op jit(solution)/shard_map/ppermute | solution.py:430
  104.9 5.7 %collective-permute-start.4 = (bf16[8,12288]{1,0:T(8,128)(2,1)S(1)}, bf16[8,12288]{1,0:T(8,128)(2,1)S(1)}, u32[]{:S(2)}, u32[]{:S(2)}) collective-permute-start(bf16[8,12288]{1,0:T(8,128)(2,1)S(1)} %slice_bitcast_fusion), channel_id=1, source_target_pairs={{0,6},{1,7},{2,0},{3,1},{4,2},{5,3},{6,4},{7,5},{8,14},{9,15},{10,... | collective-permute-start | bytes 589832 | tf_op jit(solution)/shard_map/ppermute | solution.py:430
  110.5 2.8 %copy-start.1 = (bf16[2,128,12288]{2,1,0:T(8,128)(2,1)S(1)}, bf16[2,128,12288]{2,1,0:T(8,128)(2,1)}, u32[]{:S(2)}) copy-start(bf16[2,128,12288]{2,1,0:T(8,128)(2,1)} %copy.12) | copy-start | bytes 18874372
Sparse Core Ops, SparseCore 0:
  19.2 53.0 all-gather.1
